TPU v7x, 32 devices: a whole 2x2x4 slice. The times are simulated.
32 devices in a mesh: row: 4 (over y, x), col: 8 (over z, core).
Axes of the slice: x: 2, y: 2, z: 4, core: 2. Of those that a mesh axis runs over, the one named last changes fastest.
Arguments:
- trailing_slab: float32 [32768, 1024], P('row', 'col'), may hold values from -6 to 6, as said below
- panel_columns: float32 [32, 32768], P(None, 'row'), may hold values from -965.0967 to 965.0967
- far_image: float32 [32, 32768], P(None, 'row'), may hold values from -1024 to 1024
Outputs:
- updated_slab: float32 [32768, 1024], P('row', 'col')
- update_factor: float32 [32, 32768], P(None, 'row')
Inputs may be any that keep to these rules, and one draw needn't show every extreme that they name: Rows 0 to 1023 of trailing_slab form a symmetric block.
All inputs are finite; a program needn't handle non-finite values.
Results may differ from a plain program's by a relative error of at most 0.0003.
Values sent between devices are 32-bit elements; how exact they have to be, the bound alone decides.
No kernel may reach another device: no remote copies, remote signals or barrier semaphores. Data moves between devices by JAX's collectives and lax.ppermute only.
A program may use at most 64 MiB of HBM per device.

v0:
```python
import jax
import jax.numpy as jnp
from jax import lax
from jax.experimental import pallas as pl
from jax.experimental.pallas import tpu as pltpu
from jax.sharding import PartitionSpec as P

F32, BF16 = jnp.float32, jnp.bfloat16
VMEM_LIMIT = 32 * 1024 * 1024
NT = (((1,), (1,)), ((), ()))
TN = (((0,), (0,)), ((), ()))
NN = (((1,), (0,)), ((), ()))


def params(limit=VMEM_LIMIT):
    return pltpu.CompilerParams(vmem_limit_bytes=limit)


def cost(microseconds):
    return pl.CostEstimate(flops=0, bytes_accessed=int(microseconds * 3.6e6), transcendentals=0)


def full(left, right, dims=NN):
    return lax.dot_general(left, right, dims, precision=lax.Precision.HIGHEST, preferred_element_type=F32)


def fast(left, right, dims=NN):
    return lax.dot_general(left, right, dims, preferred_element_type=F32)


def split(value, terms):
    found = []
    for _ in range(terms - 1):
        found.append(value.astype(BF16))
        value = value - found[-1].astype(F32)
    return found + [value.astype(BF16)]


def tree(parts):
    while len(parts) > 1:
        parts = [parts[i] + parts[i + 1] for i in range(0, len(parts), 2)]
    return parts[0]


def sweep_kernel(nc, panel_hbm, far_hbm, slab_hbm, out_ref, panel_ref, far_ref, slab_ref, panel_sem, far_sem, slab_sem):
    nb, rows = panel_ref.shape
    width = slab_ref.shape[1]
    head = nc * width
    chunk = max(head, 1024)
    parts = slab_sem.shape[0]
    length = rows // parts
    on_top = lax.axis_index("row") == 0
    col_pos = lax.axis_index("col")

    panel_copy = pltpu.make_async_copy(panel_hbm, panel_ref, panel_sem)
    panel_copy.start()
    far_copy = pltpu.make_async_copy(far_hbm, far_ref, far_sem)
    far_copy.start()
    slab_copies = []
    for k in range(parts):
        here = pl.ds(k * length, length)
        slab_copies.append(pltpu.make_async_copy(slab_hbm.at[here, :], slab_ref.at[here, :], slab_sem.at[k]))
        slab_copies[-1].start()

    panel_copy.wait()
    far_copy.wait()
    panels = []
    small = jnp.zeros((5 * nb, 3 * nb), F32)
    for k in range(rows // chunk):
        here = slice(k * chunk, (k + 1) * chunk)
        panels.append(jnp.concatenate(split(panel_ref[:, here], 3), axis=0))
        far = split(far_ref[:, here], 2)
        small += fast(jnp.concatenate([panels[k]] + far, axis=0), panels[k], NT)

    wide = [jnp.zeros((2 * nb, width), F32)] * 2
    for k in range(rows // chunk):
        if k * chunk % length == 0:
            slab_copies[k * chunk // length].wait()
        slab = split(slab_ref[k * chunk : (k + 1) * chunk, :], 2)
        terms = [fast(panels[k][: 2 * nb], part) for part in slab]
        if k == 0:
            head_terms = terms
        wide = [a + b for a, b in zip(wide, terms)]

    def at(i, j):
        return small[i * nb : (i + 1) * nb, j * nb : (j + 1) * nb]

    def whole(parts):
        high, low = parts
        return (high[:nb] + high[nb:]) + (low[:nb] + low[nb:])

    own = pl.ds(pl.multiple_of(col_pos * width, 128), width)
    minor = (at(0, 2) + at(2, 0)) + at(1, 1)
    out_ref[:, 0:nb] = at(0, 0) + ((at(0, 1) + at(1, 0)) + minor)
    out_ref[:, nb : 2 * nb] = jnp.where(on_top, panel_ref[:, 0:nb], 0.0)
    out_ref[:, 2 * nb : 3 * nb] = (at(3, 0) + at(3, 1)) + (at(4, 0) + at(4, 1))
    out_ref[:, 3 * nb : width] = jnp.zeros((nb, width - 3 * nb), F32)
    out_ref[:, width : 2 * width] = whole(wide)
    out_ref[:, 2 * width : 3 * width] = jnp.where(on_top, whole(head_terms) + far_ref[:, own], 0.0)
    out_ref[:, 3 * width : 4 * width] = jnp.where(on_top, slab_ref[0:nb, :], 0.0)
    out_ref[:, 4 * width : 5 * width] = jnp.where(on_top, panel_ref[:, own], 0.0)


def sweep(nc, panel, far, slab):
    nb = panel.shape[0]
    width = slab.shape[1]
    parts = 2
    hbm = pl.BlockSpec(memory_space=pltpu.HBM)
    return pl.pallas_call(
        lambda *refs: sweep_kernel(nc, *refs),
        in_specs=[hbm] * 3,
        out_specs=[pl.BlockSpec(memory_space=pltpu.VMEM)] * 4,
        out_shape=[pltpu.VMEM((nb, 5 * width), F32)] + [pltpu.VMEM(a.shape, F32) for a in (panel, far, slab)],
        scratch_shapes=[pltpu.SemaphoreType.DMA, pltpu.SemaphoreType.DMA, pltpu.SemaphoreType.DMA((parts,))],
        compiler_params=params(57 * 1024 * 1024),
        cost_estimate=cost(4),
        name="sweep",
    )(panel, far, slab)


def factor_kernel(count, *refs):
    parts, (total_ref, shifted_ref, inner_ref, state_ref) = refs[:count], refs[count:]
    nb = total_ref.shape[0]
    width = total_ref.shape[1] // 5
    total_ref[...] = tree([part[...] for part in parts])
    row = lax.broadcasted_iota(jnp.int32, (nb, 128), 0)
    lane = lax.broadcasted_iota(jnp.int32, (nb, 128), 1)
    eye2 = (row + 2 * nb == lane).astype(F32)
    state = jnp.where(lane < 2 * nb, total_ref[:, 0:128], eye2)
    for j in range(nb):
        pivot_row = state[j : j + 1, :]
        factor = jnp.where(row[:, 0:1] > j, state[:, j : j + 1] / pivot_row[:, j : j + 1], 0.0)
        state = state - factor * pivot_row
    diagonal = jnp.sum(jnp.where(row == lane, state, 0.0), axis=1, keepdims=True)
    state = state / jnp.sqrt(diagonal)
    top_diagonal = jnp.sum(jnp.where(row + nb == lane, state, 0.0), axis=1, keepdims=True)
    state = state * jnp.where(top_diagonal >= 0.0, -1.0, 1.0)
    state_ref[...] = state
    own = total_ref[:, 4 * width : 5 * width]
    cross = total_ref[:, width : 2 * width]
    eye = (row == lane).astype(F32)[:, 0:nb]
    first = lax.axis_index("col") == 0
    shifted_ref[...] = own
    far = jnp.where(first, total_ref[:, 2 * nb : 3 * nb], 0.0)
    root_t = state[:, 2 * nb : 3 * nb]
    inner_ref[...] = full(full(root_t, full(own, cross, NT) + far), root_t, NT)

    @pl.when(first)
    def _():
        shifted_ref[:, 0:nb] = own[:, 0:nb] - full(state[:, 0:nb], eye, TN)
        mixed = full(cross[:, 0:nb], root_t, (((0,), (1,)), ((), ())))
        head = full(root_t, total_ref[:, 2 * width : 2 * width + nb])
        inner_ref[...] += total_ref[:, 3 * width : 3 * width + nb] - (mixed + head)


def factor(parts):
    nb, size = parts[0].shape
    width = size // 5
    return pl.pallas_call(
        lambda *refs: factor_kernel(len(parts), *refs),
        out_shape=[
            jax.ShapeDtypeStruct(shape, F32) for shape in ((nb, size), (nb, width), (nb, nb), (nb, 4 * nb))
        ],
        compiler_params=params(),
        cost_estimate=cost(3),
        name="factor",
    )(*parts)


def decompose_kernel(state_ref, after_ref, out_ref):
    nb = state_ref.shape[0]
    row = lax.broadcasted_iota(jnp.int32, (nb, 128), 0)
    lane = lax.broadcasted_iota(jnp.int32, (nb, 128), 1)
    given = state_ref[...]
    out_ref[:, 0:nb] = given[:, 2 * nb : 3 * nb]
    eye = (row == lane).astype(F32)
    units = ((row + nb == lane) | (row + 2 * nb == lane)).astype(F32)
    state = jnp.where(lane < nb, eye - pltpu.roll(given, 128 - nb, 1), units)
    for j in range(nb):
        pivot_row = state[j : j + 1, :]
        scaled = jnp.where(lane[0:1, :] < 2 * nb, pivot_row / pivot_row[:, j : j + 1], pivot_row)
        below = (row > j) & (lane < 2 * nb)
        above = (row < j) & ((lane < nb) | (lane >= 2 * nb))
        factor = jnp.where(below | above, state[:, j : j + 1], 0.0)
        state = jnp.where(row == j, scaled, state - factor * scaled)
    out_ref[:, nb : 3 * nb] = state[:, nb : 3 * nb]


def decompose(state, after):
    nb = state.shape[0]
    return pl.pallas_call(
        decompose_kernel,
        in_specs=[pl.BlockSpec(memory_space=pltpu.VMEM), pl.BlockSpec(memory_space=pl.ANY)],
        out_shape=jax.ShapeDtypeStruct((nb, 3 * nb), F32),
        compiler_params=params(),
        cost_estimate=cost(3),
        name="decompose",
    )(state, after)


def images_kernel(flip, panel_ref, slab_ref, inner_ref, out_ref):
    nb, width = panel_ref.shape
    rows = slab_ref.shape[0] // 2
    chunk = 1024
    start = (lax.axis_index("col") % 2 ^ flip) * rows
    high, low = split(panel_ref[...], 2)
    pair = jnp.concatenate([jnp.concatenate([high, high], 1), jnp.concatenate([low, low], 1)], 0)
    for k in range(rows // chunk):
        here = pl.ds(pl.multiple_of(start + k * chunk, chunk), chunk)
        slab = jnp.concatenate(split(slab_ref[here, :], 2), axis=1)
        both = fast(pair, slab, NT)
        both = both[:nb] + both[nb:]
        for b in range(chunk // 128):
            at = (k * (chunk // 128) + b) * nb
            out_ref[at : at + nb, :] = both[:, b * 128 : (b + 1) * 128]
    at = rows // 128 * nb
    for b in range(nb // 8):
        out_ref[at : at + 8, b * nb : (b + 1) * nb] = inner_ref[8 * b : 8 * b + 8, :]


def images(flip, panel, slab, inner):
    nb = panel.shape[0]
    return pl.pallas_call(
        lambda *refs: images_kernel(flip, *refs),
        out_shape=jax.ShapeDtypeStruct((slab.shape[0] // 2 // 128 * nb + 8, 128), F32),
        compiler_params=params(),
        cost_estimate=cost(0.8),
        name="images",
    )(panel, slab, inner)


def scatter_kernel(nz, mine_ref, other_ref, *out_refs):
    z = lax.axis_index("col") // 2
    size = out_refs[0].shape[0] - 8
    inner = mine_ref[nz * size :, :] + other_ref[nz * size :, :]
    for m in range(nz):
        here = pl.ds(pl.multiple_of((z ^ m) * size, 8), size)
        out_refs[m][0:size, :] = mine_ref[here, :] + other_ref[here, :]
        out_refs[m][size:, :] = inner


def scatter(nz, mine, other):
    piece = jax.ShapeDtypeStruct(((mine.shape[0] - 8) // nz + 8, 128), F32)
    return pl.pallas_call(
        lambda *refs: scatter_kernel(nz, *refs),
        out_shape=[piece] * nz,
        compiler_params=params(),
        cost_estimate=cost(0.3),
        name="scatter",
    )(mine, other)


def join(left, right):
    def body(left_ref, right_ref, out_ref):
        out_ref[...] = left_ref[...] + right_ref[...]

    return pl.pallas_call(
        body,
        out_shape=jax.ShapeDtypeStruct(left.shape, F32),
        compiler_params=params(),
        cost_estimate=cost(0.2),
        name="join",
    )(left, right)


def weights_kernel(nz, *refs):
    pieces = refs[:-6]
    far_ref, panel_ref, total_ref, factor_ref, weights_ref, small_ref = refs[-6:]
    nb, size = weights_ref.shape
    width = total_ref.shape[1] // 5
    col = lax.axis_index("col")
    cut = pl.ds(pl.multiple_of((col % 2 * nz + col // 2) * size, 128), size)
    whole = pieces[0][...]
    for part in pieces[1:]:
        whole = whole + part[...]
    inner = whole[size // 128 * nb :, :]
    kernel_t = jnp.concatenate([inner[:, b * nb : (b + 1) * nb] for b in range(nb // 8)], axis=0)
    root_t = factor_ref[:, 0:nb]
    upper_t = factor_ref[:, nb : 2 * nb]
    lower_t = factor_ref[:, 2 * nb : 3 * nb]
    core_t = full(full(lower_t, kernel_t, TN), lower_t)
    spread = full(lower_t, root_t, TN)
    reflect = full(upper_t, root_t)
    half_core = 0.5 * core_t
    sums = jnp.concatenate([whole[b * nb : (b + 1) * nb, :] for b in range(size // 128)], axis=1) + far_ref[:, cut]
    both = jnp.concatenate([sums, panel_ref[:, cut]], axis=0)
    coefficients = jnp.concatenate([-spread, full(half_core, reflect)], axis=1)
    weights_ref[...] = full(coefficients, both)

    @pl.when((lax.axis_index("row") == 0) & (col == 0))
    def _():
        weights_ref[:, 0:nb] -= full(half_core, upper_t)

    lane = lax.broadcasted_iota(jnp.int32, (nb, width), 1)
    row = lax.broadcasted_iota(jnp.int32, (nb, width), 0)
    unit = jnp.where(col == 0, (row == lane).astype(F32), 0.0)
    own = total_ref[:, 4 * width : 5 * width]
    own_v = full(upper_t, unit) - full(reflect, own)
    own_w = (
        full(lower_t, total_ref[:, 3 * width : 4 * width], TN)
        - full(spread, total_ref[:, 2 * width : 3 * width])
        - full(half_core, own_v)
    )
    small_ref[0:nb, :] = -full(reflect, own_w, TN)
    small_ref[nb : 2 * nb, :] = own_v
    small_ref[2 * nb : 3 * nb, :] = full(upper_t, own_w, TN)


def weights_slice(nz, pieces, far, panel, total, factors):
    nb = panel.shape[0]
    size = panel.shape[1] // (2 * nz)
    width = total.shape[1] // 5
    return pl.pallas_call(
        lambda *refs: weights_kernel(nz, *refs),
        out_shape=[jax.ShapeDtypeStruct((nb, size), F32), jax.ShapeDtypeStruct((3 * nb, width), F32)],
        compiler_params=params(),
        cost_estimate=cost(1.8),
        name="weights",
    )(*pieces, far, panel, total, factors)


def update_kernel(nz, m, tokens, pieces, panel_ref, slab_ref, small_ref, out_hbm, weights_hbm, buffer, out_sem, weights_sem):
    nb, size = pieces[0].shape
    width = slab_ref.shape[1]
    for token_ref in tokens:
        token_ref[...] = jnp.zeros_like(token_ref)
    col = lax.axis_index("col")
    core, z = col % 2, col // 2
    high, low = split(small_ref[0 : 2 * nb, :], 2)
    right = jnp.concatenate([high, low], axis=1)
    right = jnp.concatenate([right, right], axis=0)
    copies = []
    for i in range(2):
        block = (core ^ i) * nz + (z ^ m)
        here = pl.ds(pl.multiple_of(block * size, 128), size)
        copies.append(pltpu.make_async_copy(pieces[i], weights_hbm.at[:, here], weights_sem.at[i]))
        copies[-1].start()
    length = size // 2
    for i in range(2):
        block = (core ^ i) * nz + (z ^ m)
        for k in range(2):
            here = pl.ds(pl.multiple_of(block * size + k * length, 128), length)
            there = slice(k * length, (k + 1) * length)
            left = jnp.concatenate([panel_ref[:, here], pieces[i][:, there]], axis=0)
            both = fast(jnp.concatenate(split(left, 2), axis=0), right, TN)
            buffer[i, there, :] = slab_ref[here, :] - (both[:, :width] + both[:, width:])

            if k == 0:
                @pl.when((lax.axis_index("row") == 0) & (block == 0))
                def _():
                    buffer[i, 0:nb, :] -= small_ref[2 * nb : 3 * nb, :]

            copies.append(pltpu.make_async_copy(buffer.at[i, there, :], out_hbm.at[here, :], out_sem.at[2 * i + k]))
            copies[-1].start()
    for copy in copies:
        copy.wait()


def update(nz, m, pieces, panel, slab, small, so_far, marks):
    nb, size = pieces[0].shape
    rows, width = slab.shape
    vmem, hbm = pl.BlockSpec(memory_space=pltpu.VMEM), pl.BlockSpec(memory_space=pltpu.HBM)
    given = len(so_far)

    def body(*refs):
        outs = refs[5 + given :]
        update_kernel(nz, m, outs[2 : 2 + marks], refs[:2], *refs[2:5], *outs[:2], *outs[2 + marks :])

    results = [jax.ShapeDtypeStruct((rows, width), F32), jax.ShapeDtypeStruct((nb, rows), F32)]
    results = pl.pallas_call(
        body,
        in_specs=[vmem] * 5 + [hbm] * given,
        out_specs=[hbm] * 2 + [vmem] * marks,
        out_shape=results + [pltpu.VMEM((8, 128), F32)] * marks,
        scratch_shapes=[
            pltpu.VMEM((2, size, width), F32),
            pltpu.SemaphoreType.DMA((4,)),
            pltpu.SemaphoreType.DMA((2,)),
        ],
        input_output_aliases={5 + i: i for i in range(given)},
        compiler_params=params(),
        cost_estimate=cost(1.5),
        name="update",
    )(*pieces, panel, slab, small, *so_far)
    return results[:2], results[-1]


def gate(array, token):
    vmem = pl.BlockSpec(memory_space=pltpu.VMEM)
    return pl.pallas_call(
        lambda *refs: None,
        in_specs=[vmem] * 2,
        out_specs=vmem,
        out_shape=pltpu.VMEM(array.shape, F32),
        input_output_aliases={0: 0},
        compiler_params=params(),
        name="gate",
    )(array, token)


def partner(array, axis, size, mask):
    return lax.ppermute(array, axis, [(i, i ^ mask) for i in range(size)])


def local(nr, nc, slab, panel, far):
    nz = nc // 2
    message, panel, far, slab = sweep(nc, panel, far, slab)
    parts = [message]
    done = 1
    while done < nr:
        value = parts[0] if len(parts) == 1 else tree(parts)
        parts = [value] + [partner(value, "row", nr, m * done) for m in range(1, 4)]
        done *= 4
    total, shifted, inner, state = factor(parts)

    theirs = partner(images(1, shifted, slab, inner), "col", nc, 1)
    mine = images(0, shifted, slab, inner)
    pieces = scatter(nz, mine, theirs)
    factors = decompose(state, pieces[0])
    pieces, received, step = dict(enumerate(pieces)), [], 1
    while step < nz:
        sent = [m for m in sorted(pieces, reverse=True) if m & step]
        moved = {m ^ step: partner(pieces.pop(m), "col", nc, 2 * step) for m in sent}
        received.append(moved.pop(0))
        for m in moved:
            pieces[m] = join(pieces[m], moved[m])
        step *= 2
    pieces = [pieces[0]] + received

    own, small = weights_slice(nz, pieces, far, panel, total, factors)
    step = nz // 2
    held = {0: own, step: partner(own, "col", nc, 2 * step)}
    other = {}
    while step > 1:
        step //= 2
        held.update({m | step: partner(held[m], "col", nc, 2 * step) for m in sorted(held, reverse=True)})
    held[1] = gate(held[1], held[nz // 2])
    so_far, tokens = (), {}
    for m in range(nz):
        if m == nz - 1:
            held[m] = gate(held[m], tokens[m - 2])
        other[m] = partner(held[m], "col", nc, 1)
        if m == 0:
            other[0] = gate(other[0], held[nz // 2])
        marks = int(m == nz - 3)
        so_far, tokens[m] = update(nz, m, [held[m], other[m]], panel, slab, small, so_far, marks)
    return tuple(so_far)


def solution(mesh):
    nr, nc = mesh.shape["row"], mesh.shape["col"]
    in_specs = (P("row", "col"), P(None, "row"), P(None, "row"))
    out_specs = (P("row", "col"), P(None, "row"))
    return jax.shard_map(
        lambda *args: local(nr, nc, *args), mesh=mesh, in_specs=in_specs, out_specs=out_specs, check_vma=False
    )
```

profile of v0, /device:TPU:1, one launch (start us, length us, event | category | flops | bytes accessed | tf_op | source)
XLA Modules:
  0.0 54.7 jit_solution(17722933915695761412)
XLA Ops:
  0.6 4.9 %sweep.1 = (f32[32,640]{1,0:T(8,128)S(1)}, f32[32,8192]{1,0:T(8,128)S(1)}, f32[32,8192]{1,0:T(8,128)S(1)}, f32[8192,128]{1,0:T(8,128)S(1)}) custom-call(f32[32,8192]{1,0:T(8,128)} %refs_0_.1, f32[32,8192]{1,0:T(8,128)} %refs_1_.1, f32[8192,128]{1,0:T(8,128)} %refs_2_.1), custom_call_target="tpu_custom_call" | custom-call | bytes 14400000 | tf_op jit(solution)/shard_map/sweep/pallas_call | solution.py:109
  5.6 2.1 %collective-permute-start = (f32[32,640]{1,0:T(8,128)S(1)}, f32[32,640]{1,0:T(8,128)S(1)}, u32[]{:S(2)}, u32[]{:S(2)}) collective-permute-start(f32[32,640]{1,0:T(8,128)S(1)} %get-tuple-element.23.refs_0_), channel_id=1, source_target_pairs={{0,8},{8,0},{16,24},{24,16},{1,9},{9,1},{17,25},{25,17},{2,10},{10... | collective-permute-start | bytes 245768 | tf_op jit(solution)/shard_map/ppermute | solution.py:402
  7.7 1.2 %collective-permute-start.1 = (f32[32,640]{1,0:T(8,128)S(1)}, f32[32,640]{1,0:T(8,128)S(1)}, u32[]{:S(2)}, u32[]{:S(2)}) collective-permute-start(f32[32,640]{1,0:T(8,128)S(1)} %get-tuple-element.23.refs_0_), channel_id=1, source_target_pairs={{0,16},{8,24},{16,0},{24,8},{1,17},{9,25},{17,1},{25,9},{2,18},{10... | collective-permute-start | bytes 245768 | tf_op jit(solution)/shard_map/ppermute | solution.py:402
  8.9 0.9 %collective-permute-done.refs_1_ = f32[32,640]{1,0:T(8,128)S(1)} collective-permute-done((f32[32,640]{1,0:T(8,128)S(1)}, f32[32,640]{1,0:T(8,128)S(1)}, u32[]{:S(2)}, u32[]{:S(2)}) %collective-permute-start) | collective-permute-done | bytes 81952 | tf_op jit(solution)/shard_map/ppermute | solution.py:402
  9.9 1.1 %collective-permute-done.1.refs_2_ = f32[32,640]{1,0:T(8,128)S(1)} collective-permute-done((f32[32,640]{1,0:T(8,128)S(1)}, f32[32,640]{1,0:T(8,128)S(1)}, u32[]{:S(2)}, u32[]{:S(2)}) %collective-permute-start.1) | collective-permute-done | bytes 81952 | tf_op jit(solution)/shard_map/ppermute | solution.py:402
  11.0 2.2 %collective-permute-done.2.refs_3_ = f32[32,640]{1,0:T(8,128)S(1)} collective-permute-done((f32[32,640]{1,0:T(8,128)S(1)}, f32[32,640]{1,0:T(8,128)S(1)}, u32[]{:S(2)}, u32[]{:S(2)}) %collective-permute-start.2) | collective-permute-done | bytes 81952 | tf_op jit(solution)/shard_map/ppermute | solution.py:402
  13.2 3.0 %factor.1 = (f32[32,640]{1,0:T(8,128)S(1)}, f32[32,128]{1,0:T(8,128)S(1)}, f32[32,32]{1,0:T(8,128)S(1)}, f32[32,128]{1,0:T(8,128)S(1)}) custom-call(f32[32,640]{1,0:T(8,128)S(1)} %get-tuple-element.23.refs_0_, f32[32,640]{1,0:T(8,128)S(1)} %collective-permute-done.refs_1_, f32[32,640]{1,0:T(8,128)S(1)} %collective-permute-done.1.refs_2_, ...), custom_call_target="tpu_custom_call" | custom-call | bytes 10800000 | tf_op jit(solution)/shard_map/factor/pallas_call | solution.py:159
  16.2 0.8 %images.3 = f32[1032,128]{1,0:T(8,128)S(1)} custom-call(f32[32,128]{1,0:T(8,128)S(1)} %get-tuple-element.24.refs_0_, f32[8192,128]{1,0:T(8,128)S(1)} %get-tuple-element.25.refs_1_.refs_3_, f32[32,32]{1,0:T(8,128)S(1)} %get-tuple-element.26.refs_2_), custom_call_target="tpu_custom_call" | custom-call | bytes 2880000 | tf_op jit(solution)/shard_map/images/pallas_call | solution.py:223
  17.0 2.6 %collective-permute-start.3 = (f32[1032,128]{1,0:T(8,128)S(1)}, f32[1032,128]{1,0:T(8,128)S(1)}, u32[]{:S(2)}, u32[]{:S(2)}) collective-permute-start(f32[1032,128]{1,0:T(8,128)S(1)} %images.3), channel_id=1, source_target_pairs={{0,1},{1,0},{2,3},{3,2},{4,5},{5,4},{6,7},{7,6},{8,9},{9,8},{10,11... | collective-permute-start | bytes 1585160 | tf_op jit(solution)/shard_map/ppermute | solution.py:402
  20.3 0.8 %collective-permute-done.3.refs_1_ = f32[1032,128]{1,0:T(8,128)S(1)} collective-permute-done((f32[1032,128]{1,0:T(8,128)S(1)}, f32[1032,128]{1,0:T(8,128)S(1)}, u32[]{:S(2)}, u32[]{:S(2)}) %collective-permute-start.3) | collective-permute-done | bytes 528416 | tf_op jit(solution)/shard_map/ppermute | solution.py:402
  21.2 1.1 %collective-permute-start.5 = (f32[264,128]{1,0:T(8,128)S(1)}, f32[264,128]{1,0:T(8,128)S(1)}, u32[]{:S(2)}, u32[]{:S(2)}) collective-permute-start(f32[264,128]{1,0:T(8,128)S(1)} %get-tuple-element.30), channel_id=1, source_target_pairs={{0,2},{1,3},{2,0},{3,1},{4,6},{5,7},{6,4},{7,5},{8,10},{9,11},{10,... | collective-permute-start | bytes 405512 | tf_op jit(solution)/shard_map/ppermute | solution.py:402
  22.7 3.3 %collective-permute-done.5.right_ref = f32[264,128]{1,0:T(8,128)S(1)} collective-permute-done((f32[264,128]{1,0:T(8,128)S(1)}, f32[264,128]{1,0:T(8,128)S(1)}, u32[]{:S(2)}, u32[]{:S(2)}) %collective-permute-start.5) | collective-permute-done | bytes 135200 | tf_op jit(solution)/shard_map/ppermute | solution.py:402
  26.1 2.1 %collective-permute-start.6 = (f32[264,128]{1,0:T(8,128)S(1)}, f32[264,128]{1,0:T(8,128)S(1)}, u32[]{:S(2)}, u32[]{:S(2)}) collective-permute-start(f32[264,128]{1,0:T(8,128)S(1)} %join.1), channel_id=1, source_target_pairs={{0,4},{1,5},{2,6},{3,7},{4,0},{5,1},{6,2},{7,3},{8,12},{9,13},{10,... | collective-permute-start | bytes 405512 | tf_op jit(solution)/shard_map/ppermute | solution.py:402
  28.2 2.7 %decompose.1.refs_6_ = f32[32,96]{1,0:T(8,128)S(1)} custom-call(f32[32,128]{1,0:T(8,128)S(1)} %get-tuple-element.34.state_ref, f32[264,128]{1,0:T(8,128)S(1)} %get-tuple-element.27.after_ref.refs_0_), custom_call_target="tpu_custom_call" | custom-call | bytes 10800000 | tf_op jit(solution)/shard_map/decompose/pallas_call | solution.py:191
  31.4 1.5 %weights.1 = (f32[32,1024]{1,0:T(8,128)S(1)}, f32[96,128]{1,0:T(8,128)S(1)}) custom-call(f32[264,128]{1,0:T(8,128)S(1)} %get-tuple-element.27.after_ref.refs_0_, f32[264,128]{1,0:T(8,128)S(1)} %collective-permute-done.4.refs_1_, f32[264,128]{1,0:T(8,128)S(1)} %collective-permute-done.6.refs_2_, f32[32,8192]{1,0:T(8,128)S(1)} %get-tuple-element.31.refs_3_, ...), custom_call_target="tpu_custom_call" | custom-call | bytes 6480000 | tf_op jit(solution)/shard_map/weights/pallas_call | solution.py:313
  32.8 1.7 %collective-permute-start.7 = (f32[32,1024]{1,0:T(8,128)S(1)}, f32[32,1024]{1,0:T(8,128)S(1)}, u32[]{:S(2)}, u32[]{:S(2)}) collective-permute-start(f32[32,1024]{1,0:T(8,128)S(1)} %get-tuple-element.35.refs_0_), channel_id=1, source_target_pairs={{0,4},{1,5},{2,6},{3,7},{4,0},{5,1},{6,2},{7,3},{8,12},{9,13},{10,... | collective-permute-start | bytes 393224 | tf_op jit(solution)/shard_map/ppermute | solution.py:402
  34.5 4.5 %collective-permute-start.9 = (f32[32,1024]{1,0:T(8,128)S(1)}, f32[32,1024]{1,0:T(8,128)S(1)}, u32[]{:S(2)}, u32[]{:S(2)}) collective-permute-start(f32[32,1024]{1,0:T(8,128)S(1)} %get-tuple-element.35.refs_0_), channel_id=1, source_target_pairs={{0,2},{1,3},{2,0},{3,1},{4,6},{5,7},{6,4},{7,5},{8,10},{9,11},{10,... | collective-permute-start | bytes 393224 | tf_op jit(solution)/shard_map/ppermute | solution.py:402
  39.1 2.1 %collective-permute-start.11 = (f32[32,1024]{1,0:T(8,128)S(1)}, f32[32,1024]{1,0:T(8,128)S(1)}, u32[]{:S(2)}, u32[]{:S(2)}) collective-permute-start(f32[32,1024]{1,0:T(8,128)S(1)} %get-tuple-element.35.refs_0_), channel_id=1, source_target_pairs={{0,1},{1,0},{2,3},{3,2},{4,5},{5,4},{6,7},{7,6},{8,9},{9,8},{10,11... | collective-permute-start | bytes 393224 | tf_op jit(solution)/shard_map/ppermute | solution.py:402
  41.5 3.8 %collective-permute-start.10 = (f32[32,1024]{1,0:T(8,128)S(1)}, f32[32,1024]{1,0:T(8,128)S(1)}, u32[]{:S(2)}, u32[]{:S(2)}) collective-permute-start(f32[32,1024]{1,0:T(8,128)S(1)} %gate.3.refs_0_), channel_id=1, source_target_pairs={{0,1},{1,0},{2,3},{3,2},{4,5},{5,4},{6,7},{7,6},{8,9},{9,8},{10,11... | collective-permute-start | bytes 393224 | tf_op jit(solution)/shard_map/ppermute | solution.py:402
  45.9 1.7 %update.4 = (f32[8192,128]{1,0:T(8,128)}, f32[32,8192]{1,0:T(8,128)}) custom-call(f32[32,1024]{1,0:T(8,128)S(1)} %get-tuple-element.35.refs_0_, f32[32,1024]{1,0:T(8,128)S(1)} %gate.4.refs_1_, f32[32,8192]{1,0:T(8,128)S(1)} %get-tuple-element.32.refs_4_.refs_2_, f32[8192,128]{1,0:T(8,128)S(1)} %get-tuple-element.25.refs_1_.refs_3_, ...), custom_call_target="tpu_custom_call" | custom-call | bytes 5400000 | tf_op jit(solution)/shard_map/update/pallas_call | solution.py:370
  48.0 1.7 %update.5 = (f32[8192,128]{1,0:T(8,128)}, f32[32,8192]{1,0:T(8,128)}, f32[8,128]{1,0:T(8,128)S(1)}) custom-call(f32[32,1024]{1,0:T(8,128)S(1)} %gate.3.refs_0_, f32[32,1024]{1,0:T(8,128)S(1)} %collective-permute-done.10.refs_1_, f32[32,8192]{1,0:T(8,128)S(1)} %get-tuple-element.32.refs_4_.refs_2_, ...), custom_call_target="tpu_custom_call", output_to_operand_aliasing={{0}: (5, {}), {1}: (6, {})} | custom-call | bytes 5400000 | tf_op jit(solution)/shard_map/update/pallas_call | solution.py:370
  50.4 0.8 %collective-permute-start.12 = (f32[32,1024]{1,0:T(8,128)S(1)}, f32[32,1024]{1,0:T(8,128)S(1)}, u32[]{:S(2)}, u32[]{:S(2)}) collective-permute-start(f32[32,1024]{1,0:T(8,128)S(1)} %gate.5.refs_0_), channel_id=1, source_target_pairs={{0,1},{1,0},{2,3},{3,2},{4,5},{5,4},{6,7},{7,6},{8,9},{9,8},{10,11... | collective-permute-start | bytes 393224 | tf_op jit(solution)/shard_map/ppermute | solution.py:402
  51.2 1.7 %update.6 = (f32[8192,128]{1,0:T(8,128)}, f32[32,8192]{1,0:T(8,128)}) custom-call(f32[32,1024]{1,0:T(8,128)S(1)} %collective-permute-done.7.refs_1_.refs_0_, f32[32,1024]{1,0:T(8,128)S(1)} %collective-permute-done.13.refs_1_, f32[32,8192]{1,0:T(8,128)S(1)} %get-tuple-element.32.refs_4_.refs_2_, ...), custom_call_target="tpu_custom_call", output_to_operand_aliasing={{0}: (5, {}), {1}: (6, {})} | custom-call | bytes 5400000 | tf_op jit(solution)/shard_map/update/pallas_call | solution.py:370
  53.0 1.7 %update.7 = (f32[8192,128]{1,0:T(8,128)}, f32[32,8192]{1,0:T(8,128)}) custom-call(f32[32,1024]{1,0:T(8,128)S(1)} %gate.5.refs_0_, f32[32,1024]{1,0:T(8,128)S(1)} %collective-permute-done.12.refs_1_, f32[32,8192]{1,0:T(8,128)S(1)} %get-tuple-element.32.refs_4_.refs_2_, ...), custom_call_target="tpu_custom_call", output_to_operand_aliasing={{0}: (5, {}), {1}: (6, {})} | custom-call | bytes 5400000 | tf_op jit(solution)/shard_map/update/pallas_call | solution.py:370
  (19 shorter events, 3.6 us)
Async XLA Ops:
  5.6 4.3 %collective-permute-start = (f32[32,640]{1,0:T(8,128)S(1)}, f32[32,640]{1,0:T(8,128)S(1)}, u32[]{:S(2)}, u32[]{:S(2)}) collective-permute-start(f32[32,640]{1,0:T(8,128)S(1)} %get-tuple-element.23.refs_0_), channel_id=1, source_target_pairs={{0,8},{8,0},{16,24},{24,16},{1,9},{9,1},{17,25},{25,17},{2,10},{10... | collective-permute-start | bytes 245768 | tf_op jit(solution)/shard_map/ppermute | solution.py:402
  7.7 3.3 %collective-permute-start.1 = (f32[32,640]{1,0:T(8,128)S(1)}, f32[32,640]{1,0:T(8,128)S(1)}, u32[]{:S(2)}, u32[]{:S(2)}) collective-permute-start(f32[32,640]{1,0:T(8,128)S(1)} %get-tuple-element.23.refs_0_), channel_id=1, source_target_pairs={{0,16},{8,24},{16,0},{24,8},{1,17},{9,25},{17,1},{25,9},{2,18},{10... | collective-permute-start | bytes 245768 | tf_op jit(solution)/shard_map/ppermute | solution.py:402
  8.9 4.3 %collective-permute-start.2 = (f32[32,640]{1,0:T(8,128)S(1)}, f32[32,640]{1,0:T(8,128)S(1)}, u32[]{:S(2)}, u32[]{:S(2)}) collective-permute-start(f32[32,640]{1,0:T(8,128)S(1)} %get-tuple-element.23.refs_0_), channel_id=1, source_target_pairs={{0,24},{8,16},{16,8},{24,0},{1,25},{9,17},{17,9},{25,1},{2,26},{10... | collective-permute-start | bytes 245768 | tf_op jit(solution)/shard_map/ppermute | solution.py:402
  17.0 4.1 %collective-permute-start.3 = (f32[1032,128]{1,0:T(8,128)S(1)}, f32[1032,128]{1,0:T(8,128)S(1)}, u32[]{:S(2)}, u32[]{:S(2)}) collective-permute-start(f32[1032,128]{1,0:T(8,128)S(1)} %images.3), channel_id=1, source_target_pairs={{0,1},{1,0},{2,3},{3,2},{4,5},{5,4},{6,7},{7,6},{8,9},{9,8},{10,11... | collective-permute-start | bytes 1585160 | tf_op jit(solution)/shard_map/ppermute | solution.py:402
  21.2 4.9 %collective-permute-start.5 = (f32[264,128]{1,0:T(8,128)S(1)}, f32[264,128]{1,0:T(8,128)S(1)}, u32[]{:S(2)}, u32[]{:S(2)}) collective-permute-start(f32[264,128]{1,0:T(8,128)S(1)} %get-tuple-element.30), channel_id=1, source_target_pairs={{0,2},{1,3},{2,0},{3,1},{4,6},{5,7},{6,4},{7,5},{8,10},{9,11},{10,... | collective-permute-start | bytes 405512 | tf_op jit(solution)/shard_map/ppermute | solution.py:402
  22.3 8.6 %collective-permute-start.4 = (f32[264,128]{1,0:T(8,128)S(1)}, f32[264,128]{1,0:T(8,128)S(1)}, u32[]{:S(2)}, u32[]{:S(2)}) collective-permute-start(f32[264,128]{1,0:T(8,128)S(1)} %get-tuple-element.28), channel_id=1, source_target_pairs={{0,2},{1,3},{2,0},{3,1},{4,6},{5,7},{6,4},{7,5},{8,10},{9,11},{10,... | collective-permute-start | bytes 405512 | tf_op jit(solution)/shard_map/ppermute | solution.py:402
  26.1 5.3 %collective-permute-start.6 = (f32[264,128]{1,0:T(8,128)S(1)}, f32[264,128]{1,0:T(8,128)S(1)}, u32[]{:S(2)}, u32[]{:S(2)}) collective-permute-start(f32[264,128]{1,0:T(8,128)S(1)} %join.1), channel_id=1, source_target_pairs={{0,4},{1,5},{2,6},{3,7},{4,0},{5,1},{6,2},{7,3},{8,12},{9,13},{10,... | collective-permute-start | bytes 405512 | tf_op jit(solution)/shard_map/ppermute | solution.py:402
  32.8 8.4 %collective-permute-start.7 = (f32[32,1024]{1,0:T(8,128)S(1)}, f32[32,1024]{1,0:T(8,128)S(1)}, u32[]{:S(2)}, u32[]{:S(2)}) collective-permute-start(f32[32,1024]{1,0:T(8,128)S(1)} %get-tuple-element.35.refs_0_), channel_id=1, source_target_pairs={{0,4},{1,5},{2,6},{3,7},{4,0},{5,1},{6,2},{7,3},{8,12},{9,13},{10,... | collective-permute-start | bytes 393224 | tf_op jit(solution)/shard_map/ppermute | solution.py:402
  34.5 6.9 %collective-permute-start.9 = (f32[32,1024]{1,0:T(8,128)S(1)}, f32[32,1024]{1,0:T(8,128)S(1)}, u32[]{:S(2)}, u32[]{:S(2)}) collective-permute-start(f32[32,1024]{1,0:T(8,128)S(1)} %get-tuple-element.35.refs_0_), channel_id=1, source_target_pairs={{0,2},{1,3},{2,0},{3,1},{4,6},{5,7},{6,4},{7,5},{8,10},{9,11},{10,... | collective-permute-start | bytes 393224 | tf_op jit(solution)/shard_map/ppermute | solution.py:402
  39.1 6.8 %collective-permute-start.11 = (f32[32,1024]{1,0:T(8,128)S(1)}, f32[32,1024]{1,0:T(8,128)S(1)}, u32[]{:S(2)}, u32[]{:S(2)}) collective-permute-start(f32[32,1024]{1,0:T(8,128)S(1)} %get-tuple-element.35.refs_0_), channel_id=1, source_target_pairs={{0,1},{1,0},{2,3},{3,2},{4,5},{5,4},{6,7},{7,6},{8,9},{9,8},{10,11... | collective-permute-start | bytes 393224 | tf_op jit(solution)/shard_map/ppermute | solution.py:402
  41.5 6.5 %collective-permute-start.10 = (f32[32,1024]{1,0:T(8,128)S(1)}, f32[32,1024]{1,0:T(8,128)S(1)}, u32[]{:S(2)}, u32[]{:S(2)}) collective-permute-start(f32[32,1024]{1,0:T(8,128)S(1)} %gate.3.refs_0_), channel_id=1, source_target_pairs={{0,1},{1,0},{2,3},{3,2},{4,5},{5,4},{6,7},{7,6},{8,9},{9,8},{10,11... | collective-permute-start | bytes 393224 | tf_op jit(solution)/shard_map/ppermute | solution.py:402
  45.3 5.1 %collective-permute-start.8 = (f32[32,1024]{1,0:T(8,128)S(1)}, f32[32,1024]{1,0:T(8,128)S(1)}, u32[]{:S(2)}, u32[]{:S(2)}) collective-permute-start(f32[32,1024]{1,0:T(8,128)S(1)} %collective-permute-done.7.refs_1_.refs_0_), channel_id=1, source_target_pairs={{0,2},{1,3},{2,0},{3,1},{4,6},{5,7},{6,4},{7,5},{8,10},{9,11},{10,... | collective-permute-start | bytes 393224 | tf_op jit(solution)/shard_map/ppermute | solution.py:402
  47.7 3.5 %collective-permute-start.13 = (f32[32,1024]{1,0:T(8,128)S(1)}, f32[32,1024]{1,0:T(8,128)S(1)}, u32[]{:S(2)}, u32[]{:S(2)}) collective-permute-start(f32[32,1024]{1,0:T(8,128)S(1)} %collective-permute-done.7.refs_1_.refs_0_), channel_id=1, source_target_pairs={{0,1},{1,0},{2,3},{3,2},{4,5},{5,4},{6,7},{7,6},{8,9},{9,8},{10,11... | collective-permute-start | bytes 393224 | tf_op jit(solution)/shard_map/ppermute | solution.py:402
  50.4 2.5 %collective-permute-start.12 = (f32[32,1024]{1,0:T(8,128)S(1)}, f32[32,1024]{1,0:T(8,128)S(1)}, u32[]{:S(2)}, u32[]{:S(2)}) collective-permute-start(f32[32,1024]{1,0:T(8,128)S(1)} %gate.5.refs_0_), channel_id=1, source_target_pairs={{0,1},{1,0},{2,3},{3,2},{4,5},{5,4},{6,7},{7,6},{8,9},{9,8},{10,11... | collective-permute-start | bytes 393224 | tf_op jit(solution)/shard_map/ppermute | solution.py:402
where the time goes:
time: 54.9 us; the launch traced here: 54.7 us
  starting transfers between devices  23.6 us (43%)
  Pallas kernels  20.7 us (38%)
  waiting for transfers between devices  9.77 us (18%)
  between operations  0.7 us (1%)
    ppermute x14, starting transfers between devices, partner(): return lax.ppermute(array, axis, [(i, i ^ mask) for i in range(size)])  23.6 us
    ppermute x14, waiting for transfers between devices, partner(): return lax.ppermute(array, axis, [(i, i ^ mask) for i in range(size)])  9.77 us
    pallas_call x4, Pallas kernels, update(): pl.pallas_call(body, in_specs=[vmem] * 5 + [hbm] * given, out_specs=[hbm]...  6.96 us
    pallas_call x1, Pallas kernels, sweep(): pl.pallas_call(lambda *refs: sweep_kernel(nc, *refs), in_specs=[hbm] * 3,...  4.94 us
    pallas_call x1, Pallas kernels, factor(): pl.pallas_call(lambda *refs: factor_kernel(len(parts), *refs), out_shape=...  3.01 us
    pallas_call x1, Pallas kernels, decompose(): pl.pallas_call(decompose_kernel, in_specs=[pl.BlockSpec(memory_space=pltp...  2.7 us
    pallas_call x2, Pallas kernels, images(): pl.pallas_call(lambda *refs: images_kernel(flip, *refs), out_shape=jax.Sh...  1.51 us
    pallas_call x1, Pallas kernels, weights_slice(): pl.pallas_call(lambda *refs: weights_kernel(nz, *refs), out_shape=[jax.Sh...  1.47 us
  transfers between devices with their start and end apart: 14, of which 8 were waited for; matrix products, arithmetic and copies ran while one was open for 0% of the time, Pallas kernels for 16%

commit v1 on v0

--- a/solution.py
+++ b/solution.py
@@ -42,7 +42,9 @@
     return parts[0]
 
 
-def sweep_kernel(nc, panel_hbm, far_hbm, slab_hbm, out_ref, panel_ref, far_ref, slab_ref, panel_sem, far_sem, slab_sem):
+def sweep_kernel(
+    nc, panel_hbm, far_hbm, slab_hbm, out_ref, panel_ref, far_ref, slab_ref, panel_sem, far_sem, slab_sem
+):
     nb, rows = panel_ref.shape
     width = slab_ref.shape[1]
     head = nc * width
@@ -93,12 +95,15 @@
     minor = (at(0, 2) + at(2, 0)) + at(1, 1)
     out_ref[:, 0:nb] = at(0, 0) + ((at(0, 1) + at(1, 0)) + minor)
     out_ref[:, nb : 2 * nb] = jnp.where(on_top, panel_ref[:, 0:nb], 0.0)
-    out_ref[:, 2 * nb : 3 * nb] = (at(3, 0) + at(3, 1)) + (at(4, 0) + at(4, 1))
-    out_ref[:, 3 * nb : width] = jnp.zeros((nb, width - 3 * nb), F32)
     out_ref[:, width : 2 * width] = whole(wide)
-    out_ref[:, 2 * width : 3 * width] = jnp.where(on_top, whole(head_terms) + far_ref[:, own], 0.0)
-    out_ref[:, 3 * width : 4 * width] = jnp.where(on_top, slab_ref[0:nb, :], 0.0)
-    out_ref[:, 4 * width : 5 * width] = jnp.where(on_top, panel_ref[:, own], 0.0)
+    out_ref[:, 2 * width : 3 * width] = jnp.where(on_top, panel_ref[:, own], 0.0)
+    head_images = jnp.where(on_top, whole(head_terms) + far_ref[:, own], 0.0)
+    corner = jnp.where(on_top, slab_ref[0:nb, :], 0.0)
+    out_ref[:, 3 * width : 4 * width] = head_images
+    out_ref[:, 4 * width : 5 * width] = corner
+    cross = (at(3, 0) + at(3, 1)) + (at(4, 0) + at(4, 1))
+    out_ref[:, 2 * nb : 3 * nb] = jnp.where(col_pos == 1, cross, head_images[:, 0:nb])
+    out_ref[:, 3 * nb : 4 * nb] = corner[:, 0:nb]
 
 
 def sweep(nc, panel, far, slab):
@@ -136,12 +141,12 @@
     top_diagonal = jnp.sum(jnp.where(row + nb == lane, state, 0.0), axis=1, keepdims=True)
     state = state * jnp.where(top_diagonal >= 0.0, -1.0, 1.0)
     state_ref[...] = state
-    own = total_ref[:, 4 * width : 5 * width]
+    own = total_ref[:, 2 * width : 3 * width]
     cross = total_ref[:, width : 2 * width]
     eye = (row == lane).astype(F32)[:, 0:nb]
     first = lax.axis_index("col") == 0
     shifted_ref[...] = own
-    far = jnp.where(first, total_ref[:, 2 * nb : 3 * nb], 0.0)
+    far = jnp.where(lax.axis_index("col") == 1, total_ref[:, 2 * nb : 3 * nb], 0.0)
     root_t = state[:, 2 * nb : 3 * nb]
     inner_ref[...] = full(full(root_t, full(own, cross, NT) + far), root_t, NT)
 
@@ -149,8 +154,8 @@
     def _():
         shifted_ref[:, 0:nb] = own[:, 0:nb] - full(state[:, 0:nb], eye, TN)
         mixed = full(cross[:, 0:nb], root_t, (((0,), (1,)), ((), ())))
-        head = full(root_t, total_ref[:, 2 * width : 2 * width + nb])
-        inner_ref[...] += total_ref[:, 3 * width : 3 * width + nb] - (mixed + head)
+        head = full(root_t, total_ref[:, 2 * nb : 3 * nb])
+        inner_ref[...] += total_ref[:, 3 * nb : 4 * nb] - (mixed + head)
 
 
 def factor(parts):
@@ -167,12 +172,12 @@
     )(*parts)
 
 
-def decompose_kernel(state_ref, after_ref, out_ref):
+def decompose_kernel(state_ref, total_ref, after_ref, out_ref, own_ref):
     nb = state_ref.shape[0]
+    width = own_ref.shape[1]
     row = lax.broadcasted_iota(jnp.int32, (nb, 128), 0)
     lane = lax.broadcasted_iota(jnp.int32, (nb, 128), 1)
     given = state_ref[...]
-    out_ref[:, 0:nb] = given[:, 2 * nb : 3 * nb]
     eye = (row == lane).astype(F32)
     units = ((row + nb == lane) | (row + 2 * nb == lane)).astype(F32)
     state = jnp.where(lane < nb, eye - pltpu.roll(given, 128 - nb, 1), units)
@@ -183,19 +188,33 @@
         above = (row < j) & ((lane < nb) | (lane >= 2 * nb))
         factor = jnp.where(below | above, state[:, j : j + 1], 0.0)
         state = jnp.where(row == j, scaled, state - factor * scaled)
-    out_ref[:, nb : 3 * nb] = state[:, nb : 3 * nb]
-
-
-def decompose(state, after):
+    root_t = given[:, 2 * nb : 3 * nb]
+    upper_t = state[:, nb : 2 * nb]
+    lower_t = state[:, 2 * nb : 3 * nb]
+    reflect = full(upper_t, root_t)
+    out_ref[:, 0:nb] = lower_t
+    out_ref[:, nb : 2 * nb] = full(lower_t, root_t, TN)
+    out_ref[:, 2 * nb : 3 * nb] = reflect
+    out_ref[:, 3 * nb : 4 * nb] = upper_t
+    own_ref[...] = -full(reflect, total_ref[:, 2 * width : 3 * width])
+
+    @pl.when(lax.axis_index("col") == 0)
+    def _():
+        own_ref[:, 0:nb] += upper_t
+
+
+def decompose(state, total, after):
     nb = state.shape[0]
+    width = total.shape[1] // 5
+    vmem = pl.BlockSpec(memory_space=pltpu.VMEM)
     return pl.pallas_call(
         decompose_kernel,
-        in_specs=[pl.BlockSpec(memory_space=pltpu.VMEM), pl.BlockSpec(memory_space=pl.ANY)],
-        out_shape=jax.ShapeDtypeStruct((nb, 3 * nb), F32),
+        in_specs=[vmem, vmem, pl.BlockSpec(memory_space=pl.ANY)],
+        out_shape=[jax.ShapeDtypeStruct((nb, 4 * nb), F32), jax.ShapeDtypeStruct((nb, width), F32)],
         compiler_params=params(),
         cost_estimate=cost(3),
         name="decompose",
-    )(state, after)
+    )(state, total, after)
 
 
 def images_kernel(flip, panel_ref, slab_ref, inner_ref, out_ref):
@@ -264,10 +283,9 @@
 
 
 def weights_kernel(nz, *refs):
-    pieces = refs[:-6]
-    far_ref, panel_ref, total_ref, factor_ref, weights_ref, small_ref = refs[-6:]
+    pieces = refs[:-5]
+    far_ref, panel_ref, factor_ref, weights_ref, half_ref = refs[-5:]
     nb, size = weights_ref.shape
-    width = total_ref.shape[1] // 5
     col = lax.axis_index("col")
     cut = pl.ds(pl.multiple_of((col % 2 * nz + col // 2) * size, 128), size)
     whole = pieces[0][...]
@@ -275,111 +293,118 @@
         whole = whole + part[...]
     inner = whole[size // 128 * nb :, :]
     kernel_t = jnp.concatenate([inner[:, b * nb : (b + 1) * nb] for b in range(nb // 8)], axis=0)
-    root_t = factor_ref[:, 0:nb]
-    upper_t = factor_ref[:, nb : 2 * nb]
-    lower_t = factor_ref[:, 2 * nb : 3 * nb]
-    core_t = full(full(lower_t, kernel_t, TN), lower_t)
-    spread = full(lower_t, root_t, TN)
-    reflect = full(upper_t, root_t)
-    half_core = 0.5 * core_t
+    lower_t, spread, reflect, upper_t = (factor_ref[:, i * nb : (i + 1) * nb] for i in range(4))
+    half_core = 0.5 * full(full(lower_t, kernel_t, TN), lower_t)
+    half_ref[...] = half_core
     sums = jnp.concatenate([whole[b * nb : (b + 1) * nb, :] for b in range(size // 128)], axis=1) + far_ref[:, cut]
-    both = jnp.concatenate([sums, panel_ref[:, cut]], axis=0)
-    coefficients = jnp.concatenate([-spread, full(half_core, reflect)], axis=1)
-    weights_ref[...] = full(coefficients, both)
+    both = split(jnp.concatenate([sums, panel_ref[:, cut]], axis=0), 2)
+    high, low = split(jnp.concatenate([-spread, full(half_core, reflect)], axis=1), 2)
+    left = jnp.concatenate([jnp.concatenate([high, high], 1), jnp.concatenate([low, low], 1)], 0)
+    out = fast(left, jnp.concatenate(both, axis=0))
+    weights_ref[...] = out[:nb] + out[nb:]
 
     @pl.when((lax.axis_index("row") == 0) & (col == 0))
     def _():
         weights_ref[:, 0:nb] -= full(half_core, upper_t)
 
-    lane = lax.broadcasted_iota(jnp.int32, (nb, width), 1)
-    row = lax.broadcasted_iota(jnp.int32, (nb, width), 0)
-    unit = jnp.where(col == 0, (row == lane).astype(F32), 0.0)
-    own = total_ref[:, 4 * width : 5 * width]
-    own_v = full(upper_t, unit) - full(reflect, own)
+
+def weights_slice(nz, pieces, far, panel, factors):
+    nb = panel.shape[0]
+    size = panel.shape[1] // (2 * nz)
+    return pl.pallas_call(
+        lambda *refs: weights_kernel(nz, *refs),
+        out_shape=[jax.ShapeDtypeStruct((nb, size), F32), jax.ShapeDtypeStruct((nb, nb), F32)],
+        compiler_params=params(),
+        cost_estimate=cost(1.2),
+        name="weights",
+    )(*pieces, far, panel, factors)
+
+
+def edges_kernel(factor_ref, own_ref, half_ref, total_ref, small_ref):
+    nb, width = own_ref.shape
+    lower_t, spread, reflect, upper_t = (factor_ref[:, i * nb : (i + 1) * nb] for i in range(4))
+    own_v = own_ref[...]
     own_w = (
-        full(lower_t, total_ref[:, 3 * width : 4 * width], TN)
-        - full(spread, total_ref[:, 2 * width : 3 * width])
-        - full(half_core, own_v)
+        full(lower_t, total_ref[:, 4 * width : 5 * width], TN)
+        - full(spread, total_ref[:, 3 * width : 4 * width])
+        - full(half_ref[...], own_v)
     )
     small_ref[0:nb, :] = -full(reflect, own_w, TN)
     small_ref[nb : 2 * nb, :] = own_v
     small_ref[2 * nb : 3 * nb, :] = full(upper_t, own_w, TN)
 
 
-def weights_slice(nz, pieces, far, panel, total, factors):
-    nb = panel.shape[0]
-    size = panel.shape[1] // (2 * nz)
-    width = total.shape[1] // 5
-    return pl.pallas_call(
-        lambda *refs: weights_kernel(nz, *refs),
-        out_shape=[jax.ShapeDtypeStruct((nb, size), F32), jax.ShapeDtypeStruct((3 * nb, width), F32)],
-        compiler_params=params(),
-        cost_estimate=cost(1.8),
-        name="weights",
-    )(*pieces, far, panel, total, factors)
-
-
-def update_kernel(nz, m, tokens, pieces, panel_ref, slab_ref, small_ref, out_hbm, weights_hbm, buffer, out_sem, weights_sem):
+def edges(factors, own_v, half, total):
+    nb, width = own_v.shape
+    return pl.pallas_call(
+        edges_kernel,
+        out_shape=jax.ShapeDtypeStruct((3 * nb, width), F32),
+        compiler_params=params(),
+        cost_estimate=cost(1),
+        name="edges",
+    )(factors, own_v, half, total)
+
+
+def update_kernel(nz, masks, tokens, pieces, panel_ref, slab_ref, small_ref, out_hbm, weights_hbm, buffer, out_sem, weights_sem):
     nb, size = pieces[0].shape
     width = slab_ref.shape[1]
     for token_ref in tokens:
         token_ref[...] = jnp.zeros_like(token_ref)
     col = lax.axis_index("col")
-    core, z = col % 2, col // 2
+    blocks = [(col % 2 ^ i) * nz + (col // 2 ^ m) for m in masks for i in range(2)]
+    copies = []
+    for i, block in enumerate(blocks):
+        here = pl.ds(pl.multiple_of(block * size, 128), size)
+        copies.append(pltpu.make_async_copy(pieces[i], weights_hbm.at[:, here], weights_sem.at[i]))
+        copies[-1].start()
     high, low = split(small_ref[0 : 2 * nb, :], 2)
     right = jnp.concatenate([high, low], axis=1)
     right = jnp.concatenate([right, right], axis=0)
-    copies = []
-    for i in range(2):
-        block = (core ^ i) * nz + (z ^ m)
-        here = pl.ds(pl.multiple_of(block * size, 128), size)
-        copies.append(pltpu.make_async_copy(pieces[i], weights_hbm.at[:, here], weights_sem.at[i]))
-        copies[-1].start()
-    length = size // 2
-    for i in range(2):
-        block = (core ^ i) * nz + (z ^ m)
-        for k in range(2):
+    cut = 2
+    length = size // cut
+    fix = lax.axis_index("row") == 0
+    for i, block in enumerate(blocks):
+        for k in range(cut):
             here = pl.ds(pl.multiple_of(block * size + k * length, 128), length)
             there = slice(k * length, (k + 1) * length)
             left = jnp.concatenate([panel_ref[:, here], pieces[i][:, there]], axis=0)
             both = fast(jnp.concatenate(split(left, 2), axis=0), right, TN)
             buffer[i, there, :] = slab_ref[here, :] - (both[:, :width] + both[:, width:])
-
             if k == 0:
-                @pl.when((lax.axis_index("row") == 0) & (block == 0))
-                def _():
-                    buffer[i, 0:nb, :] -= small_ref[2 * nb : 3 * nb, :]
-
-            copies.append(pltpu.make_async_copy(buffer.at[i, there, :], out_hbm.at[here, :], out_sem.at[2 * i + k]))
+                buffer[i, 0:nb, :] -= jnp.where(fix & (block == 0), small_ref[2 * nb : 3 * nb, :], 0.0)
+            copies.append(pltpu.make_async_copy(buffer.at[i, there, :], out_hbm.at[here, :], out_sem.at[cut * i + k]))
             copies[-1].start()
     for copy in copies:
         copy.wait()
 
 
-def update(nz, m, pieces, panel, slab, small, so_far, marks):
+def update(nz, masks, pieces, panel, slab, small, so_far, marks):
+    count = len(pieces)
     nb, size = pieces[0].shape
     rows, width = slab.shape
     vmem, hbm = pl.BlockSpec(memory_space=pltpu.VMEM), pl.BlockSpec(memory_space=pltpu.HBM)
     given = len(so_far)
 
     def body(*refs):
-        outs = refs[5 + given :]
-        update_kernel(nz, m, outs[2 : 2 + marks], refs[:2], *refs[2:5], *outs[:2], *outs[2 + marks :])
+        outs = refs[count + 3 + given :]
+        update_kernel(
+            nz, masks, outs[2 : 2 + marks], refs[:count], *refs[count : count + 3], *outs[:2], *outs[2 + marks :]
+        )
 
     results = [jax.ShapeDtypeStruct((rows, width), F32), jax.ShapeDtypeStruct((nb, rows), F32)]
     results = pl.pallas_call(
         body,
-        in_specs=[vmem] * 5 + [hbm] * given,
+        in_specs=[vmem] * (count + 3) + [hbm] * given,
         out_specs=[hbm] * 2 + [vmem] * marks,
         out_shape=results + [pltpu.VMEM((8, 128), F32)] * marks,
         scratch_shapes=[
-            pltpu.VMEM((2, size, width), F32),
-            pltpu.SemaphoreType.DMA((4,)),
-            pltpu.SemaphoreType.DMA((2,)),
+            pltpu.VMEM((count, size, width), F32),
+            pltpu.SemaphoreType.DMA((2 * count,)),
+            pltpu.SemaphoreType.DMA((count,)),
         ],
-        input_output_aliases={5 + i: i for i in range(given)},
-        compiler_params=params(),
-        cost_estimate=cost(1.5),
+        input_output_aliases={count + 3 + i: i for i in range(given)},
+        compiler_params=params(),
+        cost_estimate=cost(0.8 * count),
         name="update",
     )(*pieces, panel, slab, small, *so_far)
     return results[:2], results[-1]
@@ -389,7 +414,7 @@
     vmem = pl.BlockSpec(memory_space=pltpu.VMEM)
     return pl.pallas_call(
         lambda *refs: None,
-        in_specs=[vmem] * 2,
+        in_specs=[vmem, pl.BlockSpec(memory_space=pl.ANY)],
         out_specs=vmem,
         out_shape=pltpu.VMEM(array.shape, F32),
         input_output_aliases={0: 0},
@@ -416,7 +441,7 @@
     theirs = partner(images(1, shifted, slab, inner), "col", nc, 1)
     mine = images(0, shifted, slab, inner)
     pieces = scatter(nz, mine, theirs)
-    factors = decompose(state, pieces[0])
+    factors, own_v = decompose(state, total, pieces[0])
     pieces, received, step = dict(enumerate(pieces)), [], 1
     while step < nz:
         sent = [m for m in sorted(pieces, reverse=True) if m & step]
@@ -427,23 +452,28 @@
         step *= 2
     pieces = [pieces[0]] + received
 
-    own, small = weights_slice(nz, pieces, far, panel, total, factors)
+    own, half = weights_slice(nz, pieces, far, panel, factors)
+    small = edges(factors, own_v, half, total)
     step = nz // 2
     held = {0: own, step: partner(own, "col", nc, 2 * step)}
-    other = {}
     while step > 1:
         step //= 2
         held.update({m | step: partner(held[m], "col", nc, 2 * step) for m in sorted(held, reverse=True)})
-    held[1] = gate(held[1], held[nz // 2])
-    so_far, tokens = (), {}
-    for m in range(nz):
-        if m == nz - 1:
-            held[m] = gate(held[m], tokens[m - 2])
-        other[m] = partner(held[m], "col", nc, 1)
-        if m == 0:
-            other[0] = gate(other[0], held[nz // 2])
-        marks = int(m == nz - 3)
-        so_far, tokens[m] = update(nz, m, [held[m], other[m]], panel, slab, small, so_far, marks)
+    held[1] = gate(held[1], small)
+    groups = [[0, 1]] + [[m] for m in range(2, nz)]
+    others = {m: partner(held[m], "col", nc, 1) for m in range(nz - 1)}
+    others[0] = gate(others[0], held[nz // 2])
+    so_far = ()
+    for group in groups:
+        m = group[-1]
+        if m == nz - 2:
+            others[m] = gate(others[m], held[m + 1])
+        pairs = [piece for m in group for piece in (held[m], others[m])]
+        marks = int(group == groups[-3])
+        so_far, token = update(nz, group, pairs, panel, slab, small, so_far, marks)
+        if marks:
+            held[nz - 1] = gate(held[nz - 1], token)
+            others[nz - 1] = partner(held[nz - 1], "col", nc, 1)
     return tuple(so_far)
 
 

time: 54.9 us -> 52.9 us (0.964)
  Pallas kernels: 20.7 us -> 18.8 us
  waiting for transfers between devices: 9.77 us -> 8.44 us
  starting transfers between devices: 23.6 us -> 24.8 us
    ppermute x14, waiting for transfers between devices: 9.77 us -> 8.44 us  [partner(): return lax.ppermute(array, axis, [(i, i ^ mask) for i in range(size)])]
    pallas_call x8 -> x9, Pallas kernels: 9.66 us -> 8.35 us  [the longest x3 4.84 us: update(): pl.pallas_call(body, in_specs=[vmem] * (count + 3) + [hbm] * given, out_s...]
    ppermute x14, starting transfers between devices: 23.6 us -> 24.8 us  [partner(): return lax.ppermute(array, axis, [(i, i ^ mask) for i in range(size)])]
    pallas_call x1, Pallas kernels: 1.47 us -> 0.87 us  [weights_slice(): pl.pallas_call(lambda *refs: weights_kernel(nz, *refs), out_shape=[jax.Sh...]
  transfers between devices with their start and end apart: 14 -> 14, of which waited for: 8 -> 6; matrix products, arithmetic and copies ran while one was open for 0% -> 0% of each run, Pallas kernels for 16% -> 15%
where the time goes in v1:
time: 52.9 us; the launch traced here: 52.7 us
  starting transfers between devices  24.8 us (47%)
  Pallas kernels  18.8 us (36%)
  waiting for transfers between devices  8.44 us (16%)
  between operations  0.72 us (1%)
    ppermute x14, starting transfers between devices, partner(): return lax.ppermute(array, axis, [(i, i ^ mask) for i in range(size)])  24.8 us
    ppermute x14, waiting for transfers between devices, partner(): return lax.ppermute(array, axis, [(i, i ^ mask) for i in range(size)])  8.44 us
    pallas_call x1, Pallas kernels, sweep(): pl.pallas_call(lambda *refs: sweep_kernel(nc, *refs), in_specs=[hbm] * 3,...  4.94 us
    pallas_call x3, Pallas kernels, update(): pl.pallas_call(body, in_specs=[vmem] * (count + 3) + [hbm] * given, out_s...  4.84 us
    pallas_call x1, Pallas kernels, decompose(): pl.pallas_call(decompose_kernel, in_specs=[vmem, vmem, pl.BlockSpec(memor...  3.1 us
    pallas_call x1, Pallas kernels, factor(): pl.pallas_call(lambda *refs: factor_kernel(len(parts), *refs), out_shape=...  3.01 us
    pallas_call x2, Pallas kernels, images(): pl.pallas_call(lambda *refs: images_kernel(flip, *refs), out_shape=jax.Sh...  1.51 us
  transfers between devices with their start and end apart: 14, of which 6 were waited for; matrix products, arithmetic and copies ran while one was open for 0% of the time, Pallas kernels for 15%

profile of v1, /device:TPU:1, one launch (start us, length us, event | category | flops | bytes accessed | tf_op | source)
XLA Modules:
  0.0 52.7 jit_solution(8914518983485069515)
XLA Ops:
  0.6 4.9 %sweep.1 = (f32[32,640]{1,0:T(8,128)S(1)}, f32[32,8192]{1,0:T(8,128)S(1)}, f32[32,8192]{1,0:T(8,128)S(1)}, f32[8192,128]{1,0:T(8,128)S(1)}) custom-call(f32[32,8192]{1,0:T(8,128)} %refs_0_.1, f32[32,8192]{1,0:T(8,128)} %refs_1_.1, f32[8192,128]{1,0:T(8,128)} %refs_2_.1), custom_call_target="tpu_custom_call" | custom-call | bytes 14400000 | tf_op jit(solution)/shard_map/sweep/pallas_call | solution.py:114
  5.6 3.1 %collective-permute-start.2 = (f32[32,640]{1,0:T(8,128)S(1)}, f32[32,640]{1,0:T(8,128)S(1)}, u32[]{:S(2)}, u32[]{:S(2)}) collective-permute-start(f32[32,640]{1,0:T(8,128)S(1)} %get-tuple-element.23.refs_0_), channel_id=1, source_target_pairs={{0,24},{8,16},{16,8},{24,0},{1,25},{9,17},{17,9},{25,1},{2,26},{10... | collective-permute-start | bytes 245768 | tf_op jit(solution)/shard_map/ppermute | solution.py:427
  9.0 1.8 %collective-permute-done.2.refs_3_ = f32[32,640]{1,0:T(8,128)S(1)} collective-permute-done((f32[32,640]{1,0:T(8,128)S(1)}, f32[32,640]{1,0:T(8,128)S(1)}, u32[]{:S(2)}, u32[]{:S(2)}) %collective-permute-start.2) | collective-permute-done | bytes 81952 | tf_op jit(solution)/shard_map/ppermute | solution.py:427
  10.8 1.4 %collective-permute-done.1.refs_2_ = f32[32,640]{1,0:T(8,128)S(1)} collective-permute-done((f32[32,640]{1,0:T(8,128)S(1)}, f32[32,640]{1,0:T(8,128)S(1)}, u32[]{:S(2)}, u32[]{:S(2)}) %collective-permute-start.1) | collective-permute-done | bytes 81952 | tf_op jit(solution)/shard_map/ppermute | solution.py:427
  12.2 0.8 %collective-permute-done.refs_1_ = f32[32,640]{1,0:T(8,128)S(1)} collective-permute-done((f32[32,640]{1,0:T(8,128)S(1)}, f32[32,640]{1,0:T(8,128)S(1)}, u32[]{:S(2)}, u32[]{:S(2)}) %collective-permute-start) | collective-permute-done | bytes 81952 | tf_op jit(solution)/shard_map/ppermute | solution.py:427
  13.0 3.0 %factor.1 = (f32[32,640]{1,0:T(8,128)S(1)}, f32[32,128]{1,0:T(8,128)S(1)}, f32[32,32]{1,0:T(8,128)S(1)}, f32[32,128]{1,0:T(8,128)S(1)}) custom-call(f32[32,640]{1,0:T(8,128)S(1)} %get-tuple-element.23.refs_0_, f32[32,640]{1,0:T(8,128)S(1)} %collective-permute-done.refs_1_, f32[32,640]{1,0:T(8,128)S(1)} %collective-permute-done.1.refs_2_, ...), custom_call_target="tpu_custom_call" | custom-call | bytes 10800000 | tf_op jit(solution)/shard_map/factor/pallas_call | solution.py:164
  16.0 0.8 %images.3 = f32[1032,128]{1,0:T(8,128)S(1)} custom-call(f32[32,128]{1,0:T(8,128)S(1)} %get-tuple-element.24.refs_0_, f32[8192,128]{1,0:T(8,128)S(1)} %get-tuple-element.25.refs_1_.refs_5_.refs_3_, f32[32,32]{1,0:T(8,128)S(1)} %get-tuple-element.26.refs_2_), custom_call_target="tpu_custom_call" | custom-call | bytes 2880000 | tf_op jit(solution)/shard_map/images/pallas_call | solution.py:242
  16.8 1.9 %collective-permute-start.3 = (f32[1032,128]{1,0:T(8,128)S(1)}, f32[1032,128]{1,0:T(8,128)S(1)}, u32[]{:S(2)}, u32[]{:S(2)}) collective-permute-start(f32[1032,128]{1,0:T(8,128)S(1)} %images.3), channel_id=1, source_target_pairs={{0,1},{1,0},{2,3},{3,2},{4,5},{5,4},{6,7},{7,6},{8,9},{9,8},{10,11... | collective-permute-start | bytes 1585160 | tf_op jit(solution)/shard_map/ppermute | solution.py:427
  18.7 0.7 %images.2.refs_0_ = f32[1032,128]{1,0:T(8,128)S(1)} custom-call(f32[32,128]{1,0:T(8,128)S(1)} %get-tuple-element.24.refs_0_, f32[8192,128]{1,0:T(8,128)S(1)} %get-tuple-element.25.refs_1_.refs_5_.refs_3_, f32[32,32]{1,0:T(8,128)S(1)} %get-tuple-element.26.refs_2_), custom_call_target="tpu_custom_call" | custom-call | bytes 2880000 | tf_op jit(solution)/shard_map/images/pallas_call | solution.py:242
  19.5 0.8 %collective-permute-done.3.refs_1_ = f32[1032,128]{1,0:T(8,128)S(1)} collective-permute-done((f32[1032,128]{1,0:T(8,128)S(1)}, f32[1032,128]{1,0:T(8,128)S(1)}, u32[]{:S(2)}, u32[]{:S(2)}) %collective-permute-start.3) | collective-permute-done | bytes 528416 | tf_op jit(solution)/shard_map/ppermute | solution.py:427
  20.3 1.0 %collective-permute-start.5 = (f32[264,128]{1,0:T(8,128)S(1)}, f32[264,128]{1,0:T(8,128)S(1)}, u32[]{:S(2)}, u32[]{:S(2)}) collective-permute-start(f32[264,128]{1,0:T(8,128)S(1)} %get-tuple-element.30), channel_id=1, source_target_pairs={{0,2},{1,3},{2,0},{3,1},{4,6},{5,7},{6,4},{7,5},{8,10},{9,11},{10,... | collective-permute-start | bytes 405512 | tf_op jit(solution)/shard_map/ppermute | solution.py:427
  21.9 3.3 %collective-permute-done.5.right_ref = f32[264,128]{1,0:T(8,128)S(1)} collective-permute-done((f32[264,128]{1,0:T(8,128)S(1)}, f32[264,128]{1,0:T(8,128)S(1)}, u32[]{:S(2)}, u32[]{:S(2)}) %collective-permute-start.5) | collective-permute-done | bytes 135200 | tf_op jit(solution)/shard_map/ppermute | solution.py:427
  25.2 2.0 %collective-permute-start.6 = (f32[264,128]{1,0:T(8,128)S(1)}, f32[264,128]{1,0:T(8,128)S(1)}, u32[]{:S(2)}, u32[]{:S(2)}) collective-permute-start(f32[264,128]{1,0:T(8,128)S(1)} %join.1), channel_id=1, source_target_pairs={{0,4},{1,5},{2,6},{3,7},{4,0},{5,1},{6,2},{7,3},{8,12},{9,13},{10,... | collective-permute-start | bytes 405512 | tf_op jit(solution)/shard_map/ppermute | solution.py:427
  27.2 3.1 %decompose.1 = (f32[32,128]{1,0:T(8,128)S(1)}, f32[32,128]{1,0:T(8,128)S(1)}) custom-call(f32[32,128]{1,0:T(8,128)S(1)} %get-tuple-element.33.state_ref, f32[32,640]{1,0:T(8,128)S(1)} %get-tuple-element.34.total_ref, f32[264,128]{1,0:T(8,128)S(1)} %get-tuple-element.27.after_ref.refs_0_), custom_call_target="tpu_custom_call" | custom-call | bytes 10800000 | tf_op jit(solution)/shard_map/decompose/pallas_call | solution.py:210
  30.6 0.9 %weights.1 = (f32[32,1024]{1,0:T(8,128)S(1)}, f32[32,32]{1,0:T(8,128)S(1)}) custom-call(f32[264,128]{1,0:T(8,128)S(1)} %get-tuple-element.27.after_ref.refs_0_, f32[264,128]{1,0:T(8,128)S(1)} %collective-permute-done.4.refs_1_, f32[264,128]{1,0:T(8,128)S(1)} %collective-permute-done.6.refs_2_, f32[32,8192]{1,0:T(8,128)S(1)} %get-tuple-element.31.refs_3_, ...), custom_call_target="tpu_custom_call" | custom-call | bytes 4320000 | tf_op jit(solution)/shard_map/weights/pallas_call | solution.py:314
  31.5 2.9 %collective-permute-start.10 = (f32[32,1024]{1,0:T(8,128)S(1)}, f32[32,1024]{1,0:T(8,128)S(1)}, u32[]{:S(2)}, u32[]{:S(2)}) collective-permute-start(f32[32,1024]{1,0:T(8,128)S(1)} %get-tuple-element.36.refs_0_), channel_id=1, source_target_pairs={{0,2},{1,3},{2,0},{3,1},{4,6},{5,7},{6,4},{7,5},{8,10},{9,11},{10,... | collective-permute-start | bytes 393224 | tf_op jit(solution)/shard_map/ppermute | solution.py:427
  34.3 3.2 %collective-permute-start.7 = (f32[32,1024]{1,0:T(8,128)S(1)}, f32[32,1024]{1,0:T(8,128)S(1)}, u32[]{:S(2)}, u32[]{:S(2)}) collective-permute-start(f32[32,1024]{1,0:T(8,128)S(1)} %get-tuple-element.36.refs_0_), channel_id=1, source_target_pairs={{0,4},{1,5},{2,6},{3,7},{4,0},{5,1},{6,2},{7,3},{8,12},{9,13},{10,... | collective-permute-start | bytes 393224 | tf_op jit(solution)/shard_map/ppermute | solution.py:427
  37.6 2.1 %collective-permute-start.9 = (f32[32,1024]{1,0:T(8,128)S(1)}, f32[32,1024]{1,0:T(8,128)S(1)}, u32[]{:S(2)}, u32[]{:S(2)}) collective-permute-start(f32[32,1024]{1,0:T(8,128)S(1)} %get-tuple-element.36.refs_0_), channel_id=1, source_target_pairs={{0,1},{1,0},{2,3},{3,2},{4,5},{5,4},{6,7},{7,6},{8,9},{9,8},{10,11... | collective-permute-start | bytes 393224 | tf_op jit(solution)/shard_map/ppermute | solution.py:427
  40.1 2.6 %collective-permute-start.11 = (f32[32,1024]{1,0:T(8,128)S(1)}, f32[32,1024]{1,0:T(8,128)S(1)}, u32[]{:S(2)}, u32[]{:S(2)}) collective-permute-start(f32[32,1024]{1,0:T(8,128)S(1)} %gate.5.refs_2_), channel_id=1, source_target_pairs={{0,1},{1,0},{2,3},{3,2},{4,5},{5,4},{6,7},{7,6},{8,9},{9,8},{10,11... | collective-permute-start | bytes 393224 | tf_op jit(solution)/shard_map/ppermute | solution.py:427
  42.7 2.4 %collective-permute-start.13 = (f32[32,1024]{1,0:T(8,128)S(1)}, f32[32,1024]{1,0:T(8,128)S(1)}, u32[]{:S(2)}, u32[]{:S(2)}) collective-permute-start(f32[32,1024]{1,0:T(8,128)S(1)} %collective-permute-done.7.refs_1_.refs_0_), channel_id=1, source_target_pairs={{0,1},{1,0},{2,3},{3,2},{4,5},{5,4},{6,7},{7,6},{8,9},{9,8},{10,11... | collective-permute-start | bytes 393224 | tf_op jit(solution)/shard_map/ppermute | solution.py:427
  45.1 1.9 %update.3 = (f32[8192,128]{1,0:T(8,128)}, f32[32,8192]{1,0:T(8,128)}, f32[8,128]{1,0:T(8,128)S(1)}) custom-call(f32[32,1024]{1,0:T(8,128)S(1)} %get-tuple-element.36.refs_0_, f32[32,1024]{1,0:T(8,128)S(1)} %gate.4.refs_1_, f32[32,1024]{1,0:T(8,128)S(1)} %gate.5.refs_2_, f32[32,1024]{1,0:T(8,128)S(1)} %collective-permute-done.11.refs_3_, ...), custom_call_target="tpu_custom_call" | custom-call | bytes 11520000 | tf_op jit(solution)/shard_map/update/pallas_call | solution.py:395
  47.1 2.7 %collective-permute-start.12 = (f32[32,1024]{1,0:T(8,128)S(1)}, f32[32,1024]{1,0:T(8,128)S(1)}, u32[]{:S(2)}, u32[]{:S(2)}) collective-permute-start(f32[32,1024]{1,0:T(8,128)S(1)} %gate.6.refs_1_.refs_0_), channel_id=1, source_target_pairs={{0,1},{1,0},{2,3},{3,2},{4,5},{5,4},{6,7},{7,6},{8,9},{9,8},{10,11... | collective-permute-start | bytes 393224 | tf_op jit(solution)/shard_map/ppermute | solution.py:427
  49.8 1.5 %update.4 = (f32[8192,128]{1,0:T(8,128)}, f32[32,8192]{1,0:T(8,128)}) custom-call(f32[32,1024]{1,0:T(8,128)S(1)} %collective-permute-done.7.refs_1_.refs_0_, f32[32,1024]{1,0:T(8,128)S(1)} %gate.7.refs_1_, f32[32,8192]{1,0:T(8,128)S(1)} %get-tuple-element.32.refs_4_.refs_2_, ...), custom_call_target="tpu_custom_call", output_to_operand_aliasing={{0}: (5, {}), {1}: (6, {})} | custom-call | bytes 5760000 | tf_op jit(solution)/shard_map/update/pallas_call | solution.py:395
  51.3 1.5 %update.5 = (f32[8192,128]{1,0:T(8,128)}, f32[32,8192]{1,0:T(8,128)}) custom-call(f32[32,1024]{1,0:T(8,128)S(1)} %gate.6.refs_1_.refs_0_, f32[32,1024]{1,0:T(8,128)S(1)} %collective-permute-done.12.refs_1_, f32[32,8192]{1,0:T(8,128)S(1)} %get-tuple-element.32.refs_4_.refs_2_, ...), custom_call_target="tpu_custom_call", output_to_operand_aliasing={{0}: (5, {}), {1}: (6, {})} | custom-call | bytes 5760000 | tf_op jit(solution)/shard_map/update/pallas_call | solution.py:395
  (20 shorter events, 1.7 us)
Async XLA Ops:
  5.6 5.2 %collective-permute-start.2 = (f32[32,640]{1,0:T(8,128)S(1)}, f32[32,640]{1,0:T(8,128)S(1)}, u32[]{:S(2)}, u32[]{:S(2)}) collective-permute-start(f32[32,640]{1,0:T(8,128)S(1)} %get-tuple-element.23.refs_0_), channel_id=1, source_target_pairs={{0,24},{8,16},{16,8},{24,0},{1,25},{9,17},{17,9},{25,1},{2,26},{10... | collective-permute-start | bytes 245768 | tf_op jit(solution)/shard_map/ppermute | solution.py:427
  8.6 3.6 %collective-permute-start.1 = (f32[32,640]{1,0:T(8,128)S(1)}, f32[32,640]{1,0:T(8,128)S(1)}, u32[]{:S(2)}, u32[]{:S(2)}) collective-permute-start(f32[32,640]{1,0:T(8,128)S(1)} %get-tuple-element.23.refs_0_), channel_id=1, source_target_pairs={{0,16},{8,24},{16,0},{24,8},{1,17},{9,25},{17,1},{25,9},{2,18},{10... | collective-permute-start | bytes 245768 | tf_op jit(solution)/shard_map/ppermute | solution.py:427
  8.9 4.2 %collective-permute-start = (f32[32,640]{1,0:T(8,128)S(1)}, f32[32,640]{1,0:T(8,128)S(1)}, u32[]{:S(2)}, u32[]{:S(2)}) collective-permute-start(f32[32,640]{1,0:T(8,128)S(1)} %get-tuple-element.23.refs_0_), channel_id=1, source_target_pairs={{0,8},{8,0},{16,24},{24,16},{1,9},{9,1},{17,25},{25,17},{2,10},{10... | collective-permute-start | bytes 245768 | tf_op jit(solution)/shard_map/ppermute | solution.py:427
  16.8 3.4 %collective-permute-start.3 = (f32[1032,128]{1,0:T(8,128)S(1)}, f32[1032,128]{1,0:T(8,128)S(1)}, u32[]{:S(2)}, u32[]{:S(2)}) collective-permute-start(f32[1032,128]{1,0:T(8,128)S(1)} %images.3), channel_id=1, source_target_pairs={{0,1},{1,0},{2,3},{3,2},{4,5},{5,4},{6,7},{7,6},{8,9},{9,8},{10,11... | collective-permute-start | bytes 1585160 | tf_op jit(solution)/shard_map/ppermute | solution.py:427
  20.3 4.9 %collective-permute-start.5 = (f32[264,128]{1,0:T(8,128)S(1)}, f32[264,128]{1,0:T(8,128)S(1)}, u32[]{:S(2)}, u32[]{:S(2)}) collective-permute-start(f32[264,128]{1,0:T(8,128)S(1)} %get-tuple-element.30), channel_id=1, source_target_pairs={{0,2},{1,3},{2,0},{3,1},{4,6},{5,7},{6,4},{7,5},{8,10},{9,11},{10,... | collective-permute-start | bytes 405512 | tf_op jit(solution)/shard_map/ppermute | solution.py:427
  21.3 9.0 %collective-permute-start.4 = (f32[264,128]{1,0:T(8,128)S(1)}, f32[264,128]{1,0:T(8,128)S(1)}, u32[]{:S(2)}, u32[]{:S(2)}) collective-permute-start(f32[264,128]{1,0:T(8,128)S(1)} %get-tuple-element.28), channel_id=1, source_target_pairs={{0,2},{1,3},{2,0},{3,1},{4,6},{5,7},{6,4},{7,5},{8,10},{9,11},{10,... | collective-permute-start | bytes 405512 | tf_op jit(solution)/shard_map/ppermute | solution.py:427
  25.2 5.4 %collective-permute-start.6 = (f32[264,128]{1,0:T(8,128)S(1)}, f32[264,128]{1,0:T(8,128)S(1)}, u32[]{:S(2)}, u32[]{:S(2)}) collective-permute-start(f32[264,128]{1,0:T(8,128)S(1)} %join.1), channel_id=1, source_target_pairs={{0,4},{1,5},{2,6},{3,7},{4,0},{5,1},{6,2},{7,3},{8,12},{9,13},{10,... | collective-permute-start | bytes 405512 | tf_op jit(solution)/shard_map/ppermute | solution.py:427
  31.5 8.6 %collective-permute-start.10 = (f32[32,1024]{1,0:T(8,128)S(1)}, f32[32,1024]{1,0:T(8,128)S(1)}, u32[]{:S(2)}, u32[]{:S(2)}) collective-permute-start(f32[32,1024]{1,0:T(8,128)S(1)} %get-tuple-element.36.refs_0_), channel_id=1, source_target_pairs={{0,2},{1,3},{2,0},{3,1},{4,6},{5,7},{6,4},{7,5},{8,10},{9,11},{10,... | collective-permute-start | bytes 393224 | tf_op jit(solution)/shard_map/ppermute | solution.py:427
  34.3 8.4 %collective-permute-start.7 = (f32[32,1024]{1,0:T(8,128)S(1)}, f32[32,1024]{1,0:T(8,128)S(1)}, u32[]{:S(2)}, u32[]{:S(2)}) collective-permute-start(f32[32,1024]{1,0:T(8,128)S(1)} %get-tuple-element.36.refs_0_), channel_id=1, source_target_pairs={{0,4},{1,5},{2,6},{3,7},{4,0},{5,1},{6,2},{7,3},{8,12},{9,13},{10,... | collective-permute-start | bytes 393224 | tf_op jit(solution)/shard_map/ppermute | solution.py:427
  37.6 7.5 %collective-permute-start.9 = (f32[32,1024]{1,0:T(8,128)S(1)}, f32[32,1024]{1,0:T(8,128)S(1)}, u32[]{:S(2)}, u32[]{:S(2)}) collective-permute-start(f32[32,1024]{1,0:T(8,128)S(1)} %get-tuple-element.36.refs_0_), channel_id=1, source_target_pairs={{0,1},{1,0},{2,3},{3,2},{4,5},{5,4},{6,7},{7,6},{8,9},{9,8},{10,11... | collective-permute-start | bytes 393224 | tf_op jit(solution)/shard_map/ppermute | solution.py:427
  40.1 5.0 %collective-permute-start.11 = (f32[32,1024]{1,0:T(8,128)S(1)}, f32[32,1024]{1,0:T(8,128)S(1)}, u32[]{:S(2)}, u32[]{:S(2)}) collective-permute-start(f32[32,1024]{1,0:T(8,128)S(1)} %gate.5.refs_2_), channel_id=1, source_target_pairs={{0,1},{1,0},{2,3},{3,2},{4,5},{5,4},{6,7},{7,6},{8,9},{9,8},{10,11... | collective-permute-start | bytes 393224 | tf_op jit(solution)/shard_map/ppermute | solution.py:427
  42.7 4.3 %collective-permute-start.8 = (f32[32,1024]{1,0:T(8,128)S(1)}, f32[32,1024]{1,0:T(8,128)S(1)}, u32[]{:S(2)}, u32[]{:S(2)}) collective-permute-start(f32[32,1024]{1,0:T(8,128)S(1)} %collective-permute-done.7.refs_1_.refs_0_), channel_id=1, source_target_pairs={{0,2},{1,3},{2,0},{3,1},{4,6},{5,7},{6,4},{7,5},{8,10},{9,11},{10,... | collective-permute-start | bytes 393224 | tf_op jit(solution)/shard_map/ppermute | solution.py:427
  42.7 7.1 %collective-permute-start.13 = (f32[32,1024]{1,0:T(8,128)S(1)}, f32[32,1024]{1,0:T(8,128)S(1)}, u32[]{:S(2)}, u32[]{:S(2)}) collective-permute-start(f32[32,1024]{1,0:T(8,128)S(1)} %collective-permute-done.7.refs_1_.refs_0_), channel_id=1, source_target_pairs={{0,1},{1,0},{2,3},{3,2},{4,5},{5,4},{6,7},{7,6},{8,9},{9,8},{10,11... | collective-permute-start | bytes 393224 | tf_op jit(solution)/shard_map/ppermute | solution.py:427
  47.1 4.2 %collective-permute-start.12 = (f32[32,1024]{1,0:T(8,128)S(1)}, f32[32,1024]{1,0:T(8,128)S(1)}, u32[]{:S(2)}, u32[]{:S(2)}) collective-permute-start(f32[32,1024]{1,0:T(8,128)S(1)} %gate.6.refs_1_.refs_0_), channel_id=1, source_target_pairs={{0,1},{1,0},{2,3},{3,2},{4,5},{5,4},{6,7},{7,6},{8,9},{9,8},{10,11... | collective-permute-start | bytes 393224 | tf_op jit(solution)/shard_map/ppermute | solution.py:427

commit v2 on v1

v2 whole, which is shorter than its diff:
```python
import jax
import jax.numpy as jnp
from jax import lax
from jax.experimental import pallas as pl
from jax.experimental.pallas import tpu as pltpu
from jax.sharding import PartitionSpec as P

F32, BF16 = jnp.float32, jnp.bfloat16
VMEM_LIMIT = 32 * 1024 * 1024
BLOCK = 8
NT = (((1,), (1,)), ((), ()))
TN = (((0,), (0,)), ((), ()))
NN = (((1,), (0,)), ((), ()))


def params(limit=VMEM_LIMIT):
    return pltpu.CompilerParams(vmem_limit_bytes=limit)


def cost(microseconds):
    return pl.CostEstimate(flops=0, bytes_accessed=int(microseconds * 3.6e6), transcendentals=0)


def full(left, right, dims=NN):
    return lax.dot_general(left, right, dims, precision=lax.Precision.HIGHEST, preferred_element_type=F32)


def fast(left, right, dims=NN):
    return lax.dot_general(left, right, dims, preferred_element_type=F32)


def split(value, terms):
    found = []
    for _ in range(terms - 1):
        found.append(value.astype(BF16))
        value = value - found[-1].astype(F32)
    return found + [value.astype(BF16)]


def tree(parts):
    while len(parts) > 1:
        parts = [parts[i] + parts[i + 1] for i in range(0, len(parts), 2)]
    return parts[0]


def sweep_kernel(
    nc, panel_hbm, far_hbm, slab_hbm, out_ref, panel_ref, far_ref, slab_ref, panel_sem, far_sem, slab_sem
):
    nb, rows = panel_ref.shape
    width = slab_ref.shape[1]
    head = nc * width
    chunk = max(head, 1024)
    parts = slab_sem.shape[0]
    length = rows // parts
    on_top = lax.axis_index("row") == 0
    col_pos = lax.axis_index("col")

    panel_copy = pltpu.make_async_copy(panel_hbm, panel_ref, panel_sem)
    panel_copy.start()
    far_copy = pltpu.make_async_copy(far_hbm, far_ref, far_sem)
    far_copy.start()
    slab_copies = []
    for k in range(parts):
        here = pl.ds(k * length, length)
        slab_copies.append(pltpu.make_async_copy(slab_hbm.at[here, :], slab_ref.at[here, :], slab_sem.at[k]))
        slab_copies[-1].start()

    panel_copy.wait()
    far_copy.wait()
    small = jnp.zeros((5 * nb, 3 * nb), F32)
    wide = [jnp.zeros((2 * nb, width), F32)] * 2
    for k in range(rows // chunk):
        if k * chunk % length == 0:
            slab_copies[k * chunk // length].wait()
        here = slice(k * chunk, (k + 1) * chunk)
        terms = jnp.concatenate(split(panel_ref[:, here], 3), axis=0)
        small += fast(jnp.concatenate([terms] + split(far_ref[:, here], 2), axis=0), terms, NT)
        products = [fast(terms[: 2 * nb], part) for part in split(slab_ref[here, :], 2)]
        if k == 0:
            head_terms = products
        wide = [a + b for a, b in zip(wide, products)]

    def at(i, j):
        return small[i * nb : (i + 1) * nb, j * nb : (j + 1) * nb]

    def whole(parts):
        high, low = parts
        return (high[:nb] + high[nb:]) + (low[:nb] + low[nb:])

    own = pl.ds(pl.multiple_of(col_pos * width, 128), width)
    minor = (at(0, 2) + at(2, 0)) + at(1, 1)
    out_ref[:, 0:nb] = at(0, 0) + ((at(0, 1) + at(1, 0)) + minor)
    out_ref[:, nb : 2 * nb] = jnp.where(on_top, panel_ref[:, 0:nb], 0.0)
    out_ref[:, width : 2 * width] = whole(wide)
    out_ref[:, 2 * width : 3 * width] = jnp.where(on_top, panel_ref[:, own], 0.0)
    head_images = jnp.where(on_top, whole(head_terms) + far_ref[:, own], 0.0)
    corner = jnp.where(on_top, slab_ref[0:nb, :], 0.0)
    out_ref[:, 3 * width : 4 * width] = head_images
    out_ref[:, 4 * width : 5 * width] = corner
    cross = (at(3, 0) + at(3, 1)) + (at(4, 0) + at(4, 1))
    out_ref[:, 2 * nb : 3 * nb] = jnp.where(col_pos == 1, cross, head_images[:, 0:nb])
    out_ref[:, 3 * nb : 4 * nb] = corner[:, 0:nb]


def sweep(nc, panel, far, slab):
    nb = panel.shape[0]
    width = slab.shape[1]
    parts = 2
    hbm = pl.BlockSpec(memory_space=pltpu.HBM)
    return pl.pallas_call(
        lambda *refs: sweep_kernel(nc, *refs),
        in_specs=[hbm] * 3,
        out_specs=[pl.BlockSpec(memory_space=pltpu.VMEM)] * 4,
        out_shape=[pltpu.VMEM((nb, 5 * width), F32)] + [pltpu.VMEM(a.shape, F32) for a in (panel, far, slab)],
        scratch_shapes=[pltpu.SemaphoreType.DMA, pltpu.SemaphoreType.DMA, pltpu.SemaphoreType.DMA((parts,))],
        compiler_params=params(57 * 1024 * 1024),
        cost_estimate=cost(4),
        name="sweep",
    )(panel, far, slab)


def factor_kernel(count, *refs):
    parts, (total_ref, shifted_ref, state_ref) = refs[:count], refs[count:]
    nb, width = shifted_ref.shape
    total = tree([part[...] for part in parts])
    total_ref[...] = total
    row = lax.broadcasted_iota(jnp.int32, (nb, 128), 0)
    lane = lax.broadcasted_iota(jnp.int32, (nb, 128), 1)
    eye2 = (row + 2 * nb == lane).astype(F32)
    state = jnp.where(lane < 2 * nb, total[:, 0:128], eye2)
    for j in range(0, nb, BLOCK):
        columns = [jnp.broadcast_to(state[:, k : k + 1], state.shape) for k in range(j, j + BLOCK)]
        for t, column in enumerate(columns):
            k = j + t
            factor = jnp.where(row > k, column * (1.0 / column[k : k + 1, :]), 0.0)
            columns[t + 1 :] = [other - factor * other[k : k + 1, :] for other in columns[t + 1 :]]
            state = state - factor * state[k : k + 1, :]
    diagonal = jnp.sum(jnp.where(row == lane, state, 0.0), axis=1, keepdims=True)
    state = state / jnp.sqrt(diagonal)
    top_diagonal = jnp.sum(jnp.where(row + nb == lane, state, 0.0), axis=1, keepdims=True)
    state = state * jnp.where(top_diagonal >= 0.0, -1.0, 1.0)
    state_ref[...] = state
    own = total[:, 2 * width : 3 * width]
    shifted_ref[...] = own

    @pl.when(lax.axis_index("col") == 0)
    def _():
        shifted_ref[:, 0:nb] = own[:, 0:nb] - full(state[:, 0:nb], (row == lane).astype(F32)[:, 0:nb], TN)


def factor(parts):
    nb, size = parts[0].shape
    width = size // 5
    return pl.pallas_call(
        lambda *refs: factor_kernel(len(parts), *refs),
        out_shape=[jax.ShapeDtypeStruct(shape, F32) for shape in ((nb, size), (nb, width), (nb, 4 * nb))],
        compiler_params=params(),
        cost_estimate=cost(3),
        name="factor",
    )(*parts)


def inner_kernel(total_ref, state_ref, inner_ref):
    nb = inner_ref.shape[0]
    width = total_ref.shape[1] // 5
    root_t = state_ref[:, 2 * nb : 3 * nb]
    cross = total_ref[:, width : 2 * width]
    own = total_ref[:, 2 * width : 3 * width]
    col = lax.axis_index("col")
    far = jnp.where(col == 1, total_ref[:, 2 * nb : 3 * nb], 0.0)
    inner_ref[...] = full(full(root_t, full(own, cross, NT) + far), root_t, NT)

    @pl.when(col == 0)
    def _():
        mixed = full(cross[:, 0:nb], root_t, (((0,), (1,)), ((), ())))
        inner_ref[...] += total_ref[:, 3 * nb : 4 * nb] - (mixed + full(root_t, total_ref[:, 2 * nb : 3 * nb]))


def inner_summand(total, state):
    nb = total.shape[0]
    return pl.pallas_call(
        inner_kernel,
        out_shape=jax.ShapeDtypeStruct((nb, nb), F32),
        compiler_params=params(),
        cost_estimate=cost(0.5),
        name="inner",
    )(total, state)


def decompose_kernel(state_ref, total_ref, after_ref, out_ref, own_ref):
    nb = state_ref.shape[0]
    width = own_ref.shape[1]
    row = lax.broadcasted_iota(jnp.int32, (nb, 128), 0)
    lane = lax.broadcasted_iota(jnp.int32, (nb, 128), 1)
    given = state_ref[...]
    eye = (row == lane).astype(F32)
    units = ((row + nb == lane) | (row + 2 * nb == lane)).astype(F32)
    state = jnp.where(lane < nb, eye - pltpu.roll(given, 128 - nb, 1), units)
    for j in range(0, nb, BLOCK):
        columns = [jnp.broadcast_to(state[:, k : k + 1], state.shape) for k in range(j, j + BLOCK)]
        for t, column in enumerate(columns):
            k = j + t
            inverse = 1.0 / column[k : k + 1, :]
            for u in range(t + 1, BLOCK):
                scaled = columns[u][k : k + 1, :] * inverse
                columns[u] = jnp.where(row == k, scaled, columns[u] - column * scaled)
            scaled = jnp.where(lane[0:1, :] < 2 * nb, state[k : k + 1, :] * inverse, state[k : k + 1, :])
            below = (row > k) & (lane < 2 * nb)
            above = (row < k) & ((lane < nb) | (lane >= 2 * nb))
            state = jnp.where(row == k, scaled, state - jnp.where(below | above, column, 0.0) * scaled)
    root_t = given[:, 2 * nb : 3 * nb]
    upper_t = state[:, nb : 2 * nb]
    lower_t = state[:, 2 * nb : 3 * nb]
    reflect = full(upper_t, root_t)
    out_ref[:, 0:nb] = lower_t
    out_ref[:, nb : 2 * nb] = full(lower_t, root_t, TN)
    out_ref[:, 2 * nb : 3 * nb] = reflect
    out_ref[:, 3 * nb : 4 * nb] = upper_t
    own_ref[...] = -full(reflect, total_ref[:, 2 * width : 3 * width])

    @pl.when(lax.axis_index("col") == 0)
    def _():
        own_ref[:, 0:nb] += upper_t


def decompose(state, total, after):
    nb = state.shape[0]
    width = total.shape[1] // 5
    vmem = pl.BlockSpec(memory_space=pltpu.VMEM)
    return pl.pallas_call(
        decompose_kernel,
        in_specs=[vmem, vmem, pl.BlockSpec(memory_space=pl.ANY)],
        out_shape=[jax.ShapeDtypeStruct((nb, 4 * nb), F32), jax.ShapeDtypeStruct((nb, width), F32)],
        compiler_params=params(),
        cost_estimate=cost(3),
        name="decompose",
    )(state, total, after)


def images_kernel(flip, panel_ref, slab_ref, out_ref):
    nb, width = panel_ref.shape
    rows = slab_ref.shape[0] // 2
    chunk = 1024
    start = (lax.axis_index("col") % 2 ^ flip) * rows
    high, low = split(panel_ref[...], 2)
    pair = jnp.concatenate([jnp.concatenate([high, high], 1), jnp.concatenate([low, low], 1)], 0)
    for k in range(rows // chunk):
        here = pl.ds(pl.multiple_of(start + k * chunk, chunk), chunk)
        slab = jnp.concatenate(split(slab_ref[here, :], 2), axis=1)
        both = fast(pair, slab, NT)
        out_ref[:, k * chunk : (k + 1) * chunk] = both[:nb] + both[nb:]


def images(flip, panel, slab):
    return pl.pallas_call(
        lambda *refs: images_kernel(flip, *refs),
        out_shape=jax.ShapeDtypeStruct((panel.shape[0], slab.shape[0] // 2), F32),
        compiler_params=params(),
        cost_estimate=cost(0.8),
        name="images",
    )(panel, slab)


def scatter_kernel(nz, mine_ref, other_ref, inner_ref, *out_refs):
    nb = mine_ref.shape[0]
    z = lax.axis_index("col") // 2
    count = out_refs[0].shape[0] // nb
    for m in range(nz):
        for b in range(count):
            here = pl.ds(pl.multiple_of(((z ^ m) * count + b) * 128, 128), 128)
            out_refs[m][b * nb : (b + 1) * nb, :] = mine_ref[:, here] + other_ref[:, here]
        for b in range(nb // 8):
            out_refs[m][count * nb :, b * nb : (b + 1) * nb] = inner_ref[8 * b : 8 * b + 8, :]


def scatter(nz, mine, other, inner):
    nb, rows = mine.shape
    piece = jax.ShapeDtypeStruct((rows // nz // 128 * nb + 8, 128), F32)
    return pl.pallas_call(
        lambda *refs: scatter_kernel(nz, *refs),
        out_shape=[piece] * nz,
        compiler_params=params(),
        cost_estimate=cost(0.3),
        name="scatter",
    )(mine, other, inner)


def join(left, right):
    def body(left_ref, right_ref, out_ref):
        out_ref[...] = left_ref[...] + right_ref[...]

    return pl.pallas_call(
        body,
        out_shape=jax.ShapeDtypeStruct(left.shape, F32),
        compiler_params=params(),
        cost_estimate=cost(0.2),
        name="join",
    )(left, right)


def collect_kernel(nz, *refs):
    pieces, (far_ref, after_ref, out_ref, both_ref) = refs[:-4], refs[-4:]
    nb, size = out_ref.shape
    col = lax.axis_index("col")
    cut = pl.ds(pl.multiple_of((col % 2 * nz + col // 2) * size, 128), size)
    whole = pieces[0][...]
    for part in pieces[1:]:
        whole = whole + part[...]
    inner = whole[size // 128 * nb :, :]
    both_ref[:, size : size + nb] = jnp.concatenate([inner[:, b * nb : (b + 1) * nb] for b in range(nb // 8)], axis=0)
    whole = jnp.concatenate([whole[b * nb : (b + 1) * nb, :] for b in range(size // 128)], axis=1) + far_ref[:, cut]
    out_ref[...] = whole
    both_ref[:, 0:size] = whole


def collect(nz, pieces, far, after):
    nb, rows = far.shape
    vmem = pl.BlockSpec(memory_space=pltpu.VMEM)
    size = rows // (2 * nz)
    return pl.pallas_call(
        lambda *refs: collect_kernel(nz, *refs),
        in_specs=[vmem] * (len(pieces) + 1) + [pl.BlockSpec(memory_space=pl.ANY)],
        out_shape=[jax.ShapeDtypeStruct((nb, size), F32), jax.ShapeDtypeStruct((nb, size + 128), F32)],
        compiler_params=params(),
        cost_estimate=cost(0.4),
        name="collect",
    )(*pieces, far, after)


def edges_kernel(factor_ref, own_ref, left_ref, right_ref, total_ref, small_ref, mix_ref):
    nb, width = own_ref.shape
    lower_t, spread, reflect, upper_t = (factor_ref[:, i * nb : (i + 1) * nb] for i in range(4))
    size = left_ref.shape[1] - 128
    kernel_t = left_ref[:, size : size + nb] + right_ref[:, size : size + nb]
    half = 0.5 * full(full(lower_t, kernel_t, TN), lower_t)
    own_v = own_ref[...]
    own_w = (
        full(lower_t, total_ref[:, 4 * width : 5 * width], TN)
        - full(spread, total_ref[:, 3 * width : 4 * width])
        - full(half, own_v)
    )
    both = own_w - full(half, own_v, TN)
    small_ref[0:nb, :] = -full(reflect, both, TN)
    small_ref[nb : 2 * nb, :] = -full(spread, own_v, TN)
    small_ref[2 * nb : 3 * nb, :] = full(upper_t, both, TN)
    mix_ref[:, 0:nb] = full(half, reflect)
    mix_ref[:, nb : 2 * nb] = -spread
    mix_ref[:, 2 * nb : 3 * nb] = full(half, upper_t)


def edges(factors, own_v, left, right, total):
    nb, width = own_v.shape
    return pl.pallas_call(
        edges_kernel,
        out_shape=[jax.ShapeDtypeStruct((3 * nb, width), F32), jax.ShapeDtypeStruct((nb, 3 * nb), F32)],
        compiler_params=params(),
        cost_estimate=cost(1),
        name="edges",
    )(factors, own_v, left, right, total)


def update_kernel(
    nz, masks, tokens, pieces, panel_ref, slab_ref, small_ref, mix_ref, out_hbm, weights_hbm, buffer, factors, out_sem, weights_sem
):
    nb, size = pieces[0].shape
    width = slab_ref.shape[1]
    for token_ref in tokens:
        token_ref[...] = jnp.zeros_like(token_ref)
    col = lax.axis_index("col")
    blocks = [(col % 2 ^ i) * nz + (col // 2 ^ m) for m in masks for i in range(2)]
    high, low = split(small_ref[0 : 2 * nb, :], 2)
    right = jnp.concatenate([high, low], axis=1)
    right = jnp.concatenate([right, right], axis=0)
    high, low = split(mix_ref[:, 0 : 2 * nb], 2)
    mix = jnp.concatenate([jnp.concatenate([high, high], axis=1), jnp.concatenate([low, low], axis=1)], axis=0)
    length = size // 2
    copies = []
    for i, block in enumerate(blocks):
        first = (lax.axis_index("row") == 0) & (block == 0)
        for k in range(2):
            here = pl.ds(pl.multiple_of(block * size + k * length, 128), length)
            there = slice(k * length, (k + 1) * length)
            left = jnp.concatenate([panel_ref[:, here], pieces[i][:, there]], axis=0)
            left = jnp.concatenate(split(left, 2), axis=0)
            both = fast(left, right, TN)
            buffer[i, there, :] = slab_ref[here, :] - (both[:, :width] + both[:, width:])
            both = fast(mix, left)
            factors[i, :, there] = both[:nb] + both[nb:]
            if k == 0:
                buffer[i, 0:nb, :] -= jnp.where(first, small_ref[2 * nb : 3 * nb, :], 0.0)
                factors[i, :, 0:nb] -= jnp.where(first, mix_ref[:, 2 * nb : 3 * nb], 0.0)
            copies.append(pltpu.make_async_copy(buffer.at[i, there, :], out_hbm.at[here, :], out_sem.at[2 * i + k]))
            copies[-1].start()
        here = pl.ds(pl.multiple_of(block * size, 128), size)
        copies.append(pltpu.make_async_copy(factors.at[i], weights_hbm.at[:, here], weights_sem.at[i]))
        copies[-1].start()
    for copy in copies:
        copy.wait()


def update(nz, masks, pieces, panel, slab, small, mix, so_far, marks):
    count = len(pieces)
    nb, size = pieces[0].shape
    rows, width = slab.shape
    vmem, hbm = pl.BlockSpec(memory_space=pltpu.VMEM), pl.BlockSpec(memory_space=pltpu.HBM)
    given = len(so_far)

    def body(*refs):
        outs = refs[count + 4 + given :]
        update_kernel(
            nz, masks, outs[2 : 2 + marks], refs[:count], *refs[count : count + 4], *outs[:2], *outs[2 + marks :]
        )

    results = [jax.ShapeDtypeStruct((rows, width), F32), jax.ShapeDtypeStruct((nb, rows), F32)]
    results = pl.pallas_call(
        body,
        in_specs=[vmem] * (count + 4) + [hbm] * given,
        out_specs=[hbm] * 2 + [vmem] * marks,
        out_shape=results + [pltpu.VMEM((8, 128), F32)] * marks,
        scratch_shapes=[
            pltpu.VMEM((count, size, width), F32),
            pltpu.VMEM((count, nb, size), F32),
            pltpu.SemaphoreType.DMA((2 * count,)),
            pltpu.SemaphoreType.DMA((count,)),
        ],
        input_output_aliases={count + 4 + i: i for i in range(given)},
        compiler_params=params(),
        cost_estimate=cost(0.8 * count),
        name="update",
    )(*pieces, panel, slab, small, mix, *so_far)
    return results[:2], results[-1]


def gate(array, token):
    vmem = pl.BlockSpec(memory_space=pltpu.VMEM)
    return pl.pallas_call(
        lambda *refs: None,
        in_specs=[vmem, pl.BlockSpec(memory_space=pl.ANY)],
        out_specs=vmem,
        out_shape=pltpu.VMEM(array.shape, F32),
        input_output_aliases={0: 0},
        compiler_params=params(),
        name="gate",
    )(array, token)


def partner(array, axis, size, mask):
    return lax.ppermute(array, axis, [(i, i ^ mask) for i in range(size)])


def local(nr, nc, slab, panel, far):
    nz = nc // 2
    message, panel, far, slab = sweep(nc, panel, far, slab)
    parts = [message]
    done = 1
    while done < nr:
        value = parts[0] if len(parts) == 1 else tree(parts)
        parts = [value] + [partner(value, "row", nr, m * done) for m in range(1, 4)]
        done *= 4
    total, shifted, state = factor(parts)

    theirs = partner(images(1, shifted, slab), "col", nc, 1)
    mine = images(0, shifted, slab)
    pieces = scatter(nz, mine, theirs, inner_summand(total, state))
    factors, own_v = decompose(state, total, pieces[0])
    pieces, received, step = dict(enumerate(pieces)), [], 1
    while step < nz:
        sent = [m for m in sorted(pieces, reverse=True) if m & step]
        moved = {m ^ step: partner(pieces.pop(m), "col", nc, 2 * step) for m in sent}
        received.append(moved.pop(0))
        for m in moved:
            pieces[m] = join(pieces[m], moved[m])
        step *= 2
    own, own_both = collect(nz, [pieces[0]] + received, far, factors)

    step = nz // 2
    held = {0: own, step: partner(own, "col", nc, 2 * step)}
    while step > 1:
        step //= 2
        held.update({m | step: partner(held[m], "col", nc, 2 * step) for m in sorted(held, reverse=True)})
    others = {0: gate(partner(own_both, "col", nc, 1), held[nz // 2])}
    small, mix = edges(factors, own_v, own_both, others[0], total)
    held[1] = gate(held[1], held[nz // 2])
    groups = [[0], list(range(1, nz - 1)), [nz - 1]]
    others.update({m: partner(held[m], "col", nc, 1) for m in range(1, nz - 1)})
    so_far = ()
    for group in groups:
        m = group[-1]
        if m == nz - 2:
            others[m] = gate(others[m], held[m + 1])
        pairs = [piece for m in group for piece in (held[m], others[m])]
        marks = int(group == groups[-3])
        so_far, token = update(nz, group, pairs, panel, slab, small, mix, so_far, marks)
        if marks:
            held[nz - 1] = gate(held[nz - 1], token)
            others[nz - 1] = partner(held[nz - 1], "col", nc, 1)
    return tuple(so_far)


def solution(mesh):
    nr, nc = mesh.shape["row"], mesh.shape["col"]
    in_specs = (P("row", "col"), P(None, "row"), P(None, "row"))
    out_specs = (P("row", "col"), P(None, "row"))
    return jax.shard_map(
        lambda *args: local(nr, nc, *args), mesh=mesh, in_specs=in_specs, out_specs=out_specs, check_vma=False
    )
```

time: 52.9 us -> 48.9 us (0.924)
  waiting for transfers between devices: 8.44 us -> 13.9 us
  starting transfers between devices: 24.8 us -> 19.8 us
  Pallas kernels: 18.8 us -> 14.2 us
    ppermute x14, waiting for transfers between devices: 8.44 us -> 13.9 us  [partner(): return lax.ppermute(array, axis, [(i, i ^ mask) for i in range(size)])]
    ppermute x14, starting transfers between devices: 24.8 us -> 19.8 us  [partner(): return lax.ppermute(array, axis, [(i, i ^ mask) for i in range(size)])]
    pallas_call x1, Pallas kernels: 3.01 us -> 0.96 us  [factor(): pl.pallas_call(lambda *refs: factor_kernel(len(parts), *refs), out_shape=...]
    pallas_call x1, Pallas kernels: 3.1 us -> 1.23 us  [decompose(): pl.pallas_call(decompose_kernel, in_specs=[vmem, vmem, pl.BlockSpec(memor...]
    pallas_call x1, Pallas kernels: 4.94 us -> 4.1 us  [sweep(): pl.pallas_call(lambda *refs: sweep_kernel(nc, *refs), in_specs=[hbm] * 3,...]
    pallas_call x5 -> x6, Pallas kernels: 6.12 us -> 6.31 us  [the longest x3 4.85 us: update(): pl.pallas_call(body, in_specs=[vmem] * (count + 4) + [hbm] * given, out_s...]
  transfers between devices with their start and end apart: 14 -> 14, of which waited for: 6 -> 7; matrix products, arithmetic and copies ran while one was open for 0% -> 0% of each run, Pallas kernels for 15% -> 14%
where the time goes in v2:
time: 48.9 us; the launch traced here: 48.7 us
  starting transfers between devices  19.8 us (40%)
  Pallas kernels  14.2 us (29%)
  waiting for transfers between devices  13.9 us (28%)
  between operations  0.73 us (1%)
    ppermute x14, starting transfers between devices, partner(): return lax.ppermute(array, axis, [(i, i ^ mask) for i in range(size)])  19.8 us
    ppermute x14, waiting for transfers between devices, partner(): return lax.ppermute(array, axis, [(i, i ^ mask) for i in range(size)])  13.9 us
    pallas_call x3, Pallas kernels, update(): pl.pallas_call(body, in_specs=[vmem] * (count + 4) + [hbm] * given, out_s...  4.85 us
    pallas_call x1, Pallas kernels, sweep(): pl.pallas_call(lambda *refs: sweep_kernel(nc, *refs), in_specs=[hbm] * 3,...  4.1 us
    pallas_call x2, Pallas kernels, images(): pl.pallas_call(lambda *refs: images_kernel(flip, *refs), out_shape=jax.Sh...  1.47 us
    pallas_call x1, Pallas kernels, decompose(): pl.pallas_call(decompose_kernel, in_specs=[vmem, vmem, pl.BlockSpec(memor...  1.23 us
  transfers between devices with their start and end apart: 14, of which 7 were waited for; matrix products, arithmetic and copies ran while one was open for 0% of the time, Pallas kernels for 14%

profile of v2, /device:TPU:1, one launch (start us, length us, event | category | flops | bytes accessed | tf_op | source)
XLA Modules:
  0.0 48.7 jit_solution(5475657361270074511)
XLA Ops:
  0.6 4.1 %sweep.1 = (f32[32,640]{1,0:T(8,128)S(1)}, f32[32,8192]{1,0:T(8,128)S(1)}, f32[32,8192]{1,0:T(8,128)S(1)}, f32[8192,128]{1,0:T(8,128)S(1)}) custom-call(f32[32,8192]{1,0:T(8,128)} %refs_0_.1, f32[32,8192]{1,0:T(8,128)} %refs_1_.1, f32[8192,128]{1,0:T(8,128)} %refs_2_.1), custom_call_target="tpu_custom_call" | custom-call | bytes 14400000 | tf_op jit(solution)/shard_map/sweep/pallas_call | solution.py:110
  4.8 3.1 %collective-permute-start.2 = (f32[32,640]{1,0:T(8,128)S(1)}, f32[32,640]{1,0:T(8,128)S(1)}, u32[]{:S(2)}, u32[]{:S(2)}) collective-permute-start(f32[32,640]{1,0:T(8,128)S(1)} %get-tuple-element.24.refs_0_), channel_id=1, source_target_pairs={{0,24},{8,16},{16,8},{24,0},{1,25},{9,17},{17,9},{25,1},{2,26},{10... | collective-permute-start | bytes 245768 | tf_op jit(solution)/shard_map/ppermute | solution.py:448
  8.2 1.8 %collective-permute-done.2.refs_3_ = f32[32,640]{1,0:T(8,128)S(1)} collective-permute-done((f32[32,640]{1,0:T(8,128)S(1)}, f32[32,640]{1,0:T(8,128)S(1)}, u32[]{:S(2)}, u32[]{:S(2)}) %collective-permute-start.2) | collective-permute-done | bytes 81952 | tf_op jit(solution)/shard_map/ppermute | solution.py:448
  10.0 1.4 %collective-permute-done.1.refs_2_ = f32[32,640]{1,0:T(8,128)S(1)} collective-permute-done((f32[32,640]{1,0:T(8,128)S(1)}, f32[32,640]{1,0:T(8,128)S(1)}, u32[]{:S(2)}, u32[]{:S(2)}) %collective-permute-start.1) | collective-permute-done | bytes 81952 | tf_op jit(solution)/shard_map/ppermute | solution.py:448
  11.4 0.8 %collective-permute-done.refs_1_ = f32[32,640]{1,0:T(8,128)S(1)} collective-permute-done((f32[32,640]{1,0:T(8,128)S(1)}, f32[32,640]{1,0:T(8,128)S(1)}, u32[]{:S(2)}, u32[]{:S(2)}) %collective-permute-start) | collective-permute-done | bytes 81952 | tf_op jit(solution)/shard_map/ppermute | solution.py:448
  12.2 1.0 %factor.1 = (f32[32,640]{1,0:T(8,128)S(1)}, f32[32,128]{1,0:T(8,128)S(1)}, f32[32,128]{1,0:T(8,128)S(1)}) custom-call(f32[32,640]{1,0:T(8,128)S(1)} %get-tuple-element.24.refs_0_, f32[32,640]{1,0:T(8,128)S(1)} %collective-permute-done.refs_1_, f32[32,640]{1,0:T(8,128)S(1)} %collective-permute-done.1.refs_2_, f32[32,640]{1,0:T(8,128)S(1)} %collective-permute-done.2.refs_3_), custom_call_target="tpu_custom_call" | custom-call | bytes 10800000 | tf_op jit(solution)/shard_map/factor/pallas_call | solution.py:154
  13.2 0.7 %images.3 = f32[32,4096]{1,0:T(8,128)S(1)} custom-call(f32[32,128]{1,0:T(8,128)S(1)} %get-tuple-element.25.refs_0_, f32[8192,128]{1,0:T(8,128)S(1)} %get-tuple-element.26.refs_1_.refs_3_.refs_5_), custom_call_target="tpu_custom_call" | custom-call | bytes 2880000 | tf_op jit(solution)/shard_map/images/pallas_call | solution.py:255
  13.9 1.8 %collective-permute-start.3 = (f32[32,4096]{1,0:T(8,128)S(1)}, f32[32,4096]{1,0:T(8,128)S(1)}, u32[]{:S(2)}, u32[]{:S(2)}) collective-permute-start(f32[32,4096]{1,0:T(8,128)S(1)} %images.3), channel_id=1, source_target_pairs={{0,1},{1,0},{2,3},{3,2},{4,5},{5,4},{6,7},{7,6},{8,9},{9,8},{10,11... | collective-permute-start | bytes 1572872 | tf_op jit(solution)/shard_map/ppermute | solution.py:448
  15.7 0.7 %images.2.refs_0_ = f32[32,4096]{1,0:T(8,128)S(1)} custom-call(f32[32,128]{1,0:T(8,128)S(1)} %get-tuple-element.25.refs_0_, f32[8192,128]{1,0:T(8,128)S(1)} %get-tuple-element.26.refs_1_.refs_3_.refs_5_), custom_call_target="tpu_custom_call" | custom-call | bytes 2880000 | tf_op jit(solution)/shard_map/images/pallas_call | solution.py:255
  17.4 1.1 %collective-permute-start.5 = (f32[264,128]{1,0:T(8,128)S(1)}, f32[264,128]{1,0:T(8,128)S(1)}, u32[]{:S(2)}, u32[]{:S(2)}) collective-permute-start(f32[264,128]{1,0:T(8,128)S(1)} %get-tuple-element.32), channel_id=1, source_target_pairs={{0,2},{1,3},{2,0},{3,1},{4,6},{5,7},{6,4},{7,5},{8,10},{9,11},{10,... | collective-permute-start | bytes 405512 | tf_op jit(solution)/shard_map/ppermute | solution.py:448
  18.9 3.3 %collective-permute-done.5.right_ref = f32[264,128]{1,0:T(8,128)S(1)} collective-permute-done((f32[264,128]{1,0:T(8,128)S(1)}, f32[264,128]{1,0:T(8,128)S(1)}, u32[]{:S(2)}, u32[]{:S(2)}) %collective-permute-start.5) | collective-permute-done | bytes 135200 | tf_op jit(solution)/shard_map/ppermute | solution.py:448
  22.3 2.2 %collective-permute-start.6 = (f32[264,128]{1,0:T(8,128)S(1)}, f32[264,128]{1,0:T(8,128)S(1)}, u32[]{:S(2)}, u32[]{:S(2)}) collective-permute-start(f32[264,128]{1,0:T(8,128)S(1)} %join.1), channel_id=1, source_target_pairs={{0,4},{1,5},{2,6},{3,7},{4,0},{5,1},{6,2},{7,3},{8,12},{9,13},{10,... | collective-permute-start | bytes 405512 | tf_op jit(solution)/shard_map/ppermute | solution.py:448
  24.4 1.2 %decompose.1 = (f32[32,128]{1,0:T(8,128)S(1)}, f32[32,128]{1,0:T(8,128)S(1)}) custom-call(f32[32,128]{1,0:T(8,128)S(1)} %get-tuple-element.28.state_ref, f32[32,640]{1,0:T(8,128)S(1)} %get-tuple-element.27.total_ref, f32[264,128]{1,0:T(8,128)S(1)} %get-tuple-element.29.after_ref.refs_0_), custom_call_target="tpu_custom_call" | custom-call | bytes 10800000 | tf_op jit(solution)/shard_map/decompose/pallas_call | solution.py:230
  25.7 1.8 %collective-permute-done.6.refs_2_ = f32[264,128]{1,0:T(8,128)S(1)} collective-permute-done((f32[264,128]{1,0:T(8,128)S(1)}, f32[264,128]{1,0:T(8,128)S(1)}, u32[]{:S(2)}, u32[]{:S(2)}) %collective-permute-start.6) | collective-permute-done | bytes 135200 | tf_op jit(solution)/shard_map/ppermute | solution.py:448
  27.6 1.8 %collective-permute-start.7 = (f32[32,1024]{1,0:T(8,128)S(1)}, f32[32,1024]{1,0:T(8,128)S(1)}, u32[]{:S(2)}, u32[]{:S(2)}) collective-permute-start(f32[32,1024]{1,0:T(8,128)S(1)} %get-tuple-element.35.refs_0_), channel_id=1, source_target_pairs={{0,4},{1,5},{2,6},{3,7},{4,0},{5,1},{6,2},{7,3},{8,12},{9,13},{10,... | collective-permute-start | bytes 393224 | tf_op jit(solution)/shard_map/ppermute | solution.py:448
  29.4 3.9 %collective-permute-start.9 = (f32[32,1152]{1,0:T(8,128)S(1)}, f32[32,1152]{1,0:T(8,128)S(1)}, u32[]{:S(2)}, u32[]{:S(2)}) collective-permute-start(f32[32,1152]{1,0:T(8,128)S(1)} %get-tuple-element.36.left_ref), channel_id=1, source_target_pairs={{0,1},{1,0},{2,3},{3,2},{4,5},{5,4},{6,7},{7,6},{8,9},{9,8},{10,11... | collective-permute-start | bytes 442376 | tf_op jit(solution)/shard_map/ppermute | solution.py:448
  33.3 3.9 %collective-permute-start.11 = (f32[32,1024]{1,0:T(8,128)S(1)}, f32[32,1024]{1,0:T(8,128)S(1)}, u32[]{:S(2)}, u32[]{:S(2)}) collective-permute-start(f32[32,1024]{1,0:T(8,128)S(1)} %get-tuple-element.35.refs_0_), channel_id=1, source_target_pairs={{0,2},{1,3},{2,0},{3,1},{4,6},{5,7},{6,4},{7,5},{8,10},{9,11},{10,... | collective-permute-start | bytes 393224 | tf_op jit(solution)/shard_map/ppermute | solution.py:448
  37.3 4.4 %collective-permute-done.11.refs_0_ = f32[32,1024]{1,0:T(8,128)S(1)} collective-permute-done((f32[32,1024]{1,0:T(8,128)S(1)}, f32[32,1024]{1,0:T(8,128)S(1)}, u32[]{:S(2)}, u32[]{:S(2)}) %collective-permute-start.11) | collective-permute-done | bytes 131104 | tf_op jit(solution)/shard_map/ppermute | solution.py:448
  41.7 0.7 %collective-permute-start.12 = (f32[32,1024]{1,0:T(8,128)S(1)}, f32[32,1024]{1,0:T(8,128)S(1)}, u32[]{:S(2)}, u32[]{:S(2)}) collective-permute-start(f32[32,1024]{1,0:T(8,128)S(1)} %gate.6.refs_0_), channel_id=1, source_target_pairs={{0,1},{1,0},{2,3},{3,2},{4,5},{5,4},{6,7},{7,6},{8,9},{9,8},{10,11... | collective-permute-start | bytes 393224 | tf_op jit(solution)/shard_map/ppermute | solution.py:448
  42.4 0.9 %edges.1 = (f32[96,128]{1,0:T(8,128)S(1)}, f32[32,96]{1,0:T(8,128)S(1)}) custom-call(f32[32,128]{1,0:T(8,128)S(1)} %get-tuple-element.34.refs_4_.factor_ref, f32[32,128]{1,0:T(8,128)S(1)} %get-tuple-element.38.own_ref, f32[32,1152]{1,0:T(8,128)S(1)} %get-tuple-element.36.left_ref, f32[32,1152]{1,0:T(8,128)S(1)} %gate.4.right_ref.refs_1_, ...), custom_call_target="tpu_custom_call" | custom-call | bytes 3600000 | tf_op jit(solution)/shard_map/edges/pallas_call | solution.py:353
  43.3 1.5 %update.3 = (f32[8192,128]{1,0:T(8,128)}, f32[32,8192]{1,0:T(8,128)}, f32[8,128]{1,0:T(8,128)S(1)}) custom-call(f32[32,1024]{1,0:T(8,128)S(1)} %get-tuple-element.35.refs_0_, f32[32,1152]{1,0:T(8,128)S(1)} %gate.4.right_ref.refs_1_, f32[32,8192]{1,0:T(8,128)S(1)} %get-tuple-element.37.refs_2_.refs_4_, ...), custom_call_target="tpu_custom_call" | custom-call | bytes 5760000 | tf_op jit(solution)/shard_map/update/pallas_call | solution.py:415
  44.7 0.6 %collective-permute-start.10 = (f32[32,1024]{1,0:T(8,128)S(1)}, f32[32,1024]{1,0:T(8,128)S(1)}, u32[]{:S(2)}, u32[]{:S(2)}) collective-permute-start(f32[32,1024]{1,0:T(8,128)S(1)} %gate.5.refs_1_.refs_0_), channel_id=1, source_target_pairs={{0,1},{1,0},{2,3},{3,2},{4,5},{5,4},{6,7},{7,6},{8,9},{9,8},{10,11... | collective-permute-start | bytes 393224 | tf_op jit(solution)/shard_map/ppermute | solution.py:448
  45.3 1.9 %update.4 = (f32[8192,128]{1,0:T(8,128)}, f32[32,8192]{1,0:T(8,128)}) custom-call(f32[32,1024]{1,0:T(8,128)S(1)} %gate.6.refs_0_, f32[32,1024]{1,0:T(8,128)S(1)} %collective-permute-done.12.refs_1_, f32[32,1024]{1,0:T(8,128)S(1)} %collective-permute-done.7.refs_1_.refs_2_, ...), custom_call_target="tpu_custom_call", output_to_operand_aliasing={{0}: (8, {}), {1}: (9, {})} | custom-call | bytes 11520000 | tf_op jit(solution)/shard_map/update/pallas_call | solution.py:415
  47.3 1.4 %update.5 = (f32[8192,128]{1,0:T(8,128)}, f32[32,8192]{1,0:T(8,128)}) custom-call(f32[32,1024]{1,0:T(8,128)S(1)} %gate.5.refs_1_.refs_0_, f32[32,1024]{1,0:T(8,128)S(1)} %collective-permute-done.10.refs_1_, f32[32,8192]{1,0:T(8,128)S(1)} %get-tuple-element.37.refs_2_.refs_4_, ...), custom_call_target="tpu_custom_call", output_to_operand_aliasing={{0}: (6, {}), {1}: (7, {})} | custom-call | bytes 5760000 | tf_op jit(solution)/shard_map/update/pallas_call | solution.py:415
  (25 shorter events, 1.9 us)
Async XLA Ops:
  4.7 9.2 %copy-start = (f32[32,8192]{1,0:T(8,128)}, f32[32,8192]{1,0:T(8,128)S(1)}, u32[]{:S(2)}) copy-start(f32[32,8192]{1,0:T(8,128)S(1)} %get-tuple-element.33.refs_3_) | copy-start | bytes 3145732
  4.8 5.2 %collective-permute-start.2 = (f32[32,640]{1,0:T(8,128)S(1)}, f32[32,640]{1,0:T(8,128)S(1)}, u32[]{:S(2)}, u32[]{:S(2)}) collective-permute-start(f32[32,640]{1,0:T(8,128)S(1)} %get-tuple-element.24.refs_0_), channel_id=1, source_target_pairs={{0,24},{8,16},{16,8},{24,0},{1,25},{9,17},{17,9},{25,1},{2,26},{10... | collective-permute-start | bytes 245768 | tf_op jit(solution)/shard_map/ppermute | solution.py:448
  7.8 3.6 %collective-permute-start.1 = (f32[32,640]{1,0:T(8,128)S(1)}, f32[32,640]{1,0:T(8,128)S(1)}, u32[]{:S(2)}, u32[]{:S(2)}) collective-permute-start(f32[32,640]{1,0:T(8,128)S(1)} %get-tuple-element.24.refs_0_), channel_id=1, source_target_pairs={{0,16},{8,24},{16,0},{24,8},{1,17},{9,25},{17,1},{25,9},{2,18},{10... | collective-permute-start | bytes 245768 | tf_op jit(solution)/shard_map/ppermute | solution.py:448
  8.0 4.2 %collective-permute-start = (f32[32,640]{1,0:T(8,128)S(1)}, f32[32,640]{1,0:T(8,128)S(1)}, u32[]{:S(2)}, u32[]{:S(2)}) collective-permute-start(f32[32,640]{1,0:T(8,128)S(1)} %get-tuple-element.24.refs_0_), channel_id=1, source_target_pairs={{0,8},{8,0},{16,24},{24,16},{1,9},{9,1},{17,25},{25,17},{2,10},{10... | collective-permute-start | bytes 245768 | tf_op jit(solution)/shard_map/ppermute | solution.py:448
  13.9 3.3 %collective-permute-start.3 = (f32[32,4096]{1,0:T(8,128)S(1)}, f32[32,4096]{1,0:T(8,128)S(1)}, u32[]{:S(2)}, u32[]{:S(2)}) collective-permute-start(f32[32,4096]{1,0:T(8,128)S(1)} %images.3), channel_id=1, source_target_pairs={{0,1},{1,0},{2,3},{3,2},{4,5},{5,4},{6,7},{7,6},{8,9},{9,8},{10,11... | collective-permute-start | bytes 1572872 | tf_op jit(solution)/shard_map/ppermute | solution.py:448
  15.7 11.8 %copy-start.1 = (f32[32,8192]{1,0:T(8,128)S(1)}, f32[32,8192]{1,0:T(8,128)}, u32[]{:S(2)}) copy-start(f32[32,8192]{1,0:T(8,128)} %copy-done) | copy-start | bytes 3145732
  17.4 4.9 %collective-permute-start.5 = (f32[264,128]{1,0:T(8,128)S(1)}, f32[264,128]{1,0:T(8,128)S(1)}, u32[]{:S(2)}, u32[]{:S(2)}) collective-permute-start(f32[264,128]{1,0:T(8,128)S(1)} %get-tuple-element.32), channel_id=1, source_target_pairs={{0,2},{1,3},{2,0},{3,1},{4,6},{5,7},{6,4},{7,5},{8,10},{9,11},{10,... | collective-permute-start | bytes 405512 | tf_op jit(solution)/shard_map/ppermute | solution.py:448
  18.5 7.1 %collective-permute-start.4 = (f32[264,128]{1,0:T(8,128)S(1)}, f32[264,128]{1,0:T(8,128)S(1)}, u32[]{:S(2)}, u32[]{:S(2)}) collective-permute-start(f32[264,128]{1,0:T(8,128)S(1)} %get-tuple-element.30), channel_id=1, source_target_pairs={{0,2},{1,3},{2,0},{3,1},{4,6},{5,7},{6,4},{7,5},{8,10},{9,11},{10,... | collective-permute-start | bytes 405512 | tf_op jit(solution)/shard_map/ppermute | solution.py:448
  22.3 5.2 %collective-permute-start.6 = (f32[264,128]{1,0:T(8,128)S(1)}, f32[264,128]{1,0:T(8,128)S(1)}, u32[]{:S(2)}, u32[]{:S(2)}) collective-permute-start(f32[264,128]{1,0:T(8,128)S(1)} %join.1), channel_id=1, source_target_pairs={{0,4},{1,5},{2,6},{3,7},{4,0},{5,1},{6,2},{7,3},{8,12},{9,13},{10,... | collective-permute-start | bytes 405512 | tf_op jit(solution)/shard_map/ppermute | solution.py:448
  27.6 9.6 %collective-permute-start.7 = (f32[32,1024]{1,0:T(8,128)S(1)}, f32[32,1024]{1,0:T(8,128)S(1)}, u32[]{:S(2)}, u32[]{:S(2)}) collective-permute-start(f32[32,1024]{1,0:T(8,128)S(1)} %get-tuple-element.35.refs_0_), channel_id=1, source_target_pairs={{0,4},{1,5},{2,6},{3,7},{4,0},{5,1},{6,2},{7,3},{8,12},{9,13},{10,... | collective-permute-start | bytes 393224 | tf_op jit(solution)/shard_map/ppermute | solution.py:448
  29.4 12.9 %collective-permute-start.9 = (f32[32,1152]{1,0:T(8,128)S(1)}, f32[32,1152]{1,0:T(8,128)S(1)}, u32[]{:S(2)}, u32[]{:S(2)}) collective-permute-start(f32[32,1152]{1,0:T(8,128)S(1)} %get-tuple-element.36.left_ref), channel_id=1, source_target_pairs={{0,1},{1,0},{2,3},{3,2},{4,5},{5,4},{6,7},{7,6},{8,9},{9,8},{10,11... | collective-permute-start | bytes 442376 | tf_op jit(solution)/shard_map/ppermute | solution.py:448
  33.3 8.4 %collective-permute-start.11 = (f32[32,1024]{1,0:T(8,128)S(1)}, f32[32,1024]{1,0:T(8,128)S(1)}, u32[]{:S(2)}, u32[]{:S(2)}) collective-permute-start(f32[32,1024]{1,0:T(8,128)S(1)} %get-tuple-element.35.refs_0_), channel_id=1, source_target_pairs={{0,2},{1,3},{2,0},{3,1},{4,6},{5,7},{6,4},{7,5},{8,10},{9,11},{10,... | collective-permute-start | bytes 393224 | tf_op jit(solution)/shard_map/ppermute | solution.py:448
  37.2 7.5 %collective-permute-start.8 = (f32[32,1024]{1,0:T(8,128)S(1)}, f32[32,1024]{1,0:T(8,128)S(1)}, u32[]{:S(2)}, u32[]{:S(2)}) collective-permute-start(f32[32,1024]{1,0:T(8,128)S(1)} %collective-permute-done.7.refs_1_.refs_2_), channel_id=1, source_target_pairs={{0,2},{1,3},{2,0},{3,1},{4,6},{5,7},{6,4},{7,5},{8,10},{9,11},{10,... | collective-permute-start | bytes 393224 | tf_op jit(solution)/shard_map/ppermute | solution.py:448
  41.7 3.6 %collective-permute-start.12 = (f32[32,1024]{1,0:T(8,128)S(1)}, f32[32,1024]{1,0:T(8,128)S(1)}, u32[]{:S(2)}, u32[]{:S(2)}) collective-permute-start(f32[32,1024]{1,0:T(8,128)S(1)} %gate.6.refs_0_), channel_id=1, source_target_pairs={{0,1},{1,0},{2,3},{3,2},{4,5},{5,4},{6,7},{7,6},{8,9},{9,8},{10,11... | collective-permute-start | bytes 393224 | tf_op jit(solution)/shard_map/ppermute | solution.py:448
  42.3 3.0 %collective-permute-start.13 = (f32[32,1024]{1,0:T(8,128)S(1)}, f32[32,1024]{1,0:T(8,128)S(1)}, u32[]{:S(2)}, u32[]{:S(2)}) collective-permute-start(f32[32,1024]{1,0:T(8,128)S(1)} %collective-permute-done.7.refs_1_.refs_2_), channel_id=1, source_target_pairs={{0,1},{1,0},{2,3},{3,2},{4,5},{5,4},{6,7},{7,6},{8,9},{9,8},{10,11... | collective-permute-start | bytes 393224 | tf_op jit(solution)/shard_map/ppermute | solution.py:448
  44.7 2.5 %collective-permute-start.10 = (f32[32,1024]{1,0:T(8,128)S(1)}, f32[32,1024]{1,0:T(8,128)S(1)}, u32[]{:S(2)}, u32[]{:S(2)}) collective-permute-start(f32[32,1024]{1,0:T(8,128)S(1)} %gate.5.refs_1_.refs_0_), channel_id=1, source_target_pairs={{0,1},{1,0},{2,3},{3,2},{4,5},{5,4},{6,7},{7,6},{8,9},{9,8},{10,11... | collective-permute-start | bytes 393224 | tf_op jit(solution)/shard_map/ppermute | solution.py:448

commit v3 on v2

--- a/solution.py
+++ b/solution.py
@@ -7,7 +7,7 @@
 
 F32, BF16 = jnp.float32, jnp.bfloat16
 VMEM_LIMIT = 32 * 1024 * 1024
-BLOCK = 8
+BLOCK = 16
 NT = (((1,), (1,)), ((), ()))
 TN = (((0,), (0,)), ((), ()))
 NN = (((1,), (0,)), ((), ()))
@@ -55,23 +55,25 @@
     on_top = lax.axis_index("row") == 0
     col_pos = lax.axis_index("col")
 
-    panel_copy = pltpu.make_async_copy(panel_hbm, panel_ref, panel_sem)
-    panel_copy.start()
-    far_copy = pltpu.make_async_copy(far_hbm, far_ref, far_sem)
-    far_copy.start()
-    slab_copies = []
+    copies = []
     for k in range(parts):
         here = pl.ds(k * length, length)
-        slab_copies.append(pltpu.make_async_copy(slab_hbm.at[here, :], slab_ref.at[here, :], slab_sem.at[k]))
-        slab_copies[-1].start()
-
-    panel_copy.wait()
-    far_copy.wait()
+        copies.append(
+            [
+                pltpu.make_async_copy(panel_hbm.at[:, here], panel_ref.at[:, here], panel_sem.at[k]),
+                pltpu.make_async_copy(far_hbm.at[:, here], far_ref.at[:, here], far_sem.at[k]),
+                pltpu.make_async_copy(slab_hbm.at[here, :], slab_ref.at[here, :], slab_sem.at[k]),
+            ]
+        )
+        for copy in copies[k]:
+            copy.start()
+
     small = jnp.zeros((5 * nb, 3 * nb), F32)
     wide = [jnp.zeros((2 * nb, width), F32)] * 2
     for k in range(rows // chunk):
         if k * chunk % length == 0:
-            slab_copies[k * chunk // length].wait()
+            for copy in copies[k * chunk // length]:
+                copy.wait()
         here = slice(k * chunk, (k + 1) * chunk)
         terms = jnp.concatenate(split(panel_ref[:, here], 3), axis=0)
         small += fast(jnp.concatenate([terms] + split(far_ref[:, here], 2), axis=0), terms, NT)
@@ -105,14 +107,14 @@
 def sweep(nc, panel, far, slab):
     nb = panel.shape[0]
     width = slab.shape[1]
-    parts = 2
+    parts = 4
     hbm = pl.BlockSpec(memory_space=pltpu.HBM)
     return pl.pallas_call(
         lambda *refs: sweep_kernel(nc, *refs),
         in_specs=[hbm] * 3,
         out_specs=[pl.BlockSpec(memory_space=pltpu.VMEM)] * 4,
         out_shape=[pltpu.VMEM((nb, 5 * width), F32)] + [pltpu.VMEM(a.shape, F32) for a in (panel, far, slab)],
-        scratch_shapes=[pltpu.SemaphoreType.DMA, pltpu.SemaphoreType.DMA, pltpu.SemaphoreType.DMA((parts,))],
+        scratch_shapes=[pltpu.SemaphoreType.DMA((parts,))] * 3,
         compiler_params=params(57 * 1024 * 1024),
         cost_estimate=cost(4),
         name="sweep",

time: 48.9 us -> 48.2 us (0.986)
  Pallas kernels: 14.2 us -> 13.4 us
where the time goes in v3:
time: 48.2 us; the launch traced here: 48 us
  starting transfers between devices  19.8 us (41%)
  waiting for transfers between devices  14.1 us (29%)
  Pallas kernels  13.4 us (28%)
  between operations  0.73 us (2%)
    ppermute x14, starting transfers between devices, partner(): return lax.ppermute(array, axis, [(i, i ^ mask) for i in range(size)])  19.8 us
    ppermute x14, waiting for transfers between devices, partner(): return lax.ppermute(array, axis, [(i, i ^ mask) for i in range(size)])  14.1 us
    pallas_call x3, Pallas kernels, update(): pl.pallas_call(body, in_specs=[vmem] * (count + 4) + [hbm] * given, out_s...  4.85 us
    pallas_call x1, Pallas kernels, sweep(): pl.pallas_call(lambda *refs: sweep_kernel(nc, *refs), in_specs=[hbm] * 3,...  3.63 us
    pallas_call x2, Pallas kernels, images(): pl.pallas_call(lambda *refs: images_kernel(flip, *refs), out_shape=jax.Sh...  1.47 us
    pallas_call x1, Pallas kernels, decompose(): pl.pallas_call(decompose_kernel, in_specs=[vmem, vmem, pl.BlockSpec(memor...  1.1 us
  transfers between devices with their start and end apart: 14, of which 7 were waited for; matrix products, arithmetic and copies ran while one was open for 0% of the time, Pallas kernels for 14%

profile of v3, /device:TPU:1, one launch (start us, length us, event | category | flops | bytes accessed | tf_op | source)
XLA Modules:
  0.0 48.0 jit_solution(7519666042233053928)
XLA Ops:
  0.6 3.6 %sweep.1 = (f32[32,640]{1,0:T(8,128)S(1)}, f32[32,8192]{1,0:T(8,128)S(1)}, f32[32,8192]{1,0:T(8,128)S(1)}, f32[8192,128]{1,0:T(8,128)S(1)}) custom-call(f32[32,8192]{1,0:T(8,128)} %refs_0_.1, f32[32,8192]{1,0:T(8,128)} %refs_1_.1, f32[8192,128]{1,0:T(8,128)} %refs_2_.1), custom_call_target="tpu_custom_call" | custom-call | bytes 14400000 | tf_op jit(solution)/shard_map/sweep/pallas_call | solution.py:112
  4.3 3.1 %collective-permute-start.2 = (f32[32,640]{1,0:T(8,128)S(1)}, f32[32,640]{1,0:T(8,128)S(1)}, u32[]{:S(2)}, u32[]{:S(2)}) collective-permute-start(f32[32,640]{1,0:T(8,128)S(1)} %get-tuple-element.24.refs_0_), channel_id=1, source_target_pairs={{0,24},{8,16},{16,8},{24,0},{1,25},{9,17},{17,9},{25,1},{2,26},{10... | collective-permute-start | bytes 245768 | tf_op jit(solution)/shard_map/ppermute | solution.py:450
  7.7 1.8 %collective-permute-done.2.refs_3_ = f32[32,640]{1,0:T(8,128)S(1)} collective-permute-done((f32[32,640]{1,0:T(8,128)S(1)}, f32[32,640]{1,0:T(8,128)S(1)}, u32[]{:S(2)}, u32[]{:S(2)}) %collective-permute-start.2) | collective-permute-done | bytes 81952 | tf_op jit(solution)/shard_map/ppermute | solution.py:450
  9.5 1.4 %collective-permute-done.1.refs_2_ = f32[32,640]{1,0:T(8,128)S(1)} collective-permute-done((f32[32,640]{1,0:T(8,128)S(1)}, f32[32,640]{1,0:T(8,128)S(1)}, u32[]{:S(2)}, u32[]{:S(2)}) %collective-permute-start.1) | collective-permute-done | bytes 81952 | tf_op jit(solution)/shard_map/ppermute | solution.py:450
  10.9 0.8 %collective-permute-done.refs_1_ = f32[32,640]{1,0:T(8,128)S(1)} collective-permute-done((f32[32,640]{1,0:T(8,128)S(1)}, f32[32,640]{1,0:T(8,128)S(1)}, u32[]{:S(2)}, u32[]{:S(2)}) %collective-permute-start) | collective-permute-done | bytes 81952 | tf_op jit(solution)/shard_map/ppermute | solution.py:450
  11.7 0.8 %factor.1 = (f32[32,640]{1,0:T(8,128)S(1)}, f32[32,128]{1,0:T(8,128)S(1)}, f32[32,128]{1,0:T(8,128)S(1)}) custom-call(f32[32,640]{1,0:T(8,128)S(1)} %get-tuple-element.24.refs_0_, f32[32,640]{1,0:T(8,128)S(1)} %collective-permute-done.refs_1_, f32[32,640]{1,0:T(8,128)S(1)} %collective-permute-done.1.refs_2_, f32[32,640]{1,0:T(8,128)S(1)} %collective-permute-done.2.refs_3_), custom_call_target="tpu_custom_call" | custom-call | bytes 10800000 | tf_op jit(solution)/shard_map/factor/pallas_call | solution.py:156
  12.5 0.7 %images.3 = f32[32,4096]{1,0:T(8,128)S(1)} custom-call(f32[32,128]{1,0:T(8,128)S(1)} %get-tuple-element.25.refs_0_, f32[8192,128]{1,0:T(8,128)S(1)} %get-tuple-element.26.refs_1_.refs_3_.refs_5_), custom_call_target="tpu_custom_call" | custom-call | bytes 2880000 | tf_op jit(solution)/shard_map/images/pallas_call | solution.py:257
  13.2 1.8 %collective-permute-start.3 = (f32[32,4096]{1,0:T(8,128)S(1)}, f32[32,4096]{1,0:T(8,128)S(1)}, u32[]{:S(2)}, u32[]{:S(2)}) collective-permute-start(f32[32,4096]{1,0:T(8,128)S(1)} %images.3), channel_id=1, source_target_pairs={{0,1},{1,0},{2,3},{3,2},{4,5},{5,4},{6,7},{7,6},{8,9},{9,8},{10,11... | collective-permute-start | bytes 1572872 | tf_op jit(solution)/shard_map/ppermute | solution.py:450
  15.0 0.7 %images.2.refs_0_ = f32[32,4096]{1,0:T(8,128)S(1)} custom-call(f32[32,128]{1,0:T(8,128)S(1)} %get-tuple-element.25.refs_0_, f32[8192,128]{1,0:T(8,128)S(1)} %get-tuple-element.26.refs_1_.refs_3_.refs_5_), custom_call_target="tpu_custom_call" | custom-call | bytes 2880000 | tf_op jit(solution)/shard_map/images/pallas_call | solution.py:257
  16.7 1.1 %collective-permute-start.5 = (f32[264,128]{1,0:T(8,128)S(1)}, f32[264,128]{1,0:T(8,128)S(1)}, u32[]{:S(2)}, u32[]{:S(2)}) collective-permute-start(f32[264,128]{1,0:T(8,128)S(1)} %get-tuple-element.32), channel_id=1, source_target_pairs={{0,2},{1,3},{2,0},{3,1},{4,6},{5,7},{6,4},{7,5},{8,10},{9,11},{10,... | collective-permute-start | bytes 405512 | tf_op jit(solution)/shard_map/ppermute | solution.py:450
  18.2 3.3 %collective-permute-done.5.right_ref = f32[264,128]{1,0:T(8,128)S(1)} collective-permute-done((f32[264,128]{1,0:T(8,128)S(1)}, f32[264,128]{1,0:T(8,128)S(1)}, u32[]{:S(2)}, u32[]{:S(2)}) %collective-permute-start.5) | collective-permute-done | bytes 135200 | tf_op jit(solution)/shard_map/ppermute | solution.py:450
  21.6 2.2 %collective-permute-start.6 = (f32[264,128]{1,0:T(8,128)S(1)}, f32[264,128]{1,0:T(8,128)S(1)}, u32[]{:S(2)}, u32[]{:S(2)}) collective-permute-start(f32[264,128]{1,0:T(8,128)S(1)} %join.1), channel_id=1, source_target_pairs={{0,4},{1,5},{2,6},{3,7},{4,0},{5,1},{6,2},{7,3},{8,12},{9,13},{10,... | collective-permute-start | bytes 405512 | tf_op jit(solution)/shard_map/ppermute | solution.py:450
  23.8 1.1 %decompose.1 = (f32[32,128]{1,0:T(8,128)S(1)}, f32[32,128]{1,0:T(8,128)S(1)}) custom-call(f32[32,128]{1,0:T(8,128)S(1)} %get-tuple-element.28.state_ref, f32[32,640]{1,0:T(8,128)S(1)} %get-tuple-element.27.total_ref, f32[264,128]{1,0:T(8,128)S(1)} %get-tuple-element.29.after_ref.refs_0_), custom_call_target="tpu_custom_call" | custom-call | bytes 10800000 | tf_op jit(solution)/shard_map/decompose/pallas_call | solution.py:232
  24.9 2.0 %collective-permute-done.6.refs_2_ = f32[264,128]{1,0:T(8,128)S(1)} collective-permute-done((f32[264,128]{1,0:T(8,128)S(1)}, f32[264,128]{1,0:T(8,128)S(1)}, u32[]{:S(2)}, u32[]{:S(2)}) %collective-permute-start.6) | collective-permute-done | bytes 135200 | tf_op jit(solution)/shard_map/ppermute | solution.py:450
  26.9 1.8 %collective-permute-start.7 = (f32[32,1024]{1,0:T(8,128)S(1)}, f32[32,1024]{1,0:T(8,128)S(1)}, u32[]{:S(2)}, u32[]{:S(2)}) collective-permute-start(f32[32,1024]{1,0:T(8,128)S(1)} %get-tuple-element.35.refs_0_), channel_id=1, source_target_pairs={{0,4},{1,5},{2,6},{3,7},{4,0},{5,1},{6,2},{7,3},{8,12},{9,13},{10,... | collective-permute-start | bytes 393224 | tf_op jit(solution)/shard_map/ppermute | solution.py:450
  28.7 3.9 %collective-permute-start.9 = (f32[32,1152]{1,0:T(8,128)S(1)}, f32[32,1152]{1,0:T(8,128)S(1)}, u32[]{:S(2)}, u32[]{:S(2)}) collective-permute-start(f32[32,1152]{1,0:T(8,128)S(1)} %get-tuple-element.36.left_ref), channel_id=1, source_target_pairs={{0,1},{1,0},{2,3},{3,2},{4,5},{5,4},{6,7},{7,6},{8,9},{9,8},{10,11... | collective-permute-start | bytes 442376 | tf_op jit(solution)/shard_map/ppermute | solution.py:450
  32.7 3.9 %collective-permute-start.11 = (f32[32,1024]{1,0:T(8,128)S(1)}, f32[32,1024]{1,0:T(8,128)S(1)}, u32[]{:S(2)}, u32[]{:S(2)}) collective-permute-start(f32[32,1024]{1,0:T(8,128)S(1)} %get-tuple-element.35.refs_0_), channel_id=1, source_target_pairs={{0,2},{1,3},{2,0},{3,1},{4,6},{5,7},{6,4},{7,5},{8,10},{9,11},{10,... | collective-permute-start | bytes 393224 | tf_op jit(solution)/shard_map/ppermute | solution.py:450
  36.6 4.4 %collective-permute-done.11.refs_0_ = f32[32,1024]{1,0:T(8,128)S(1)} collective-permute-done((f32[32,1024]{1,0:T(8,128)S(1)}, f32[32,1024]{1,0:T(8,128)S(1)}, u32[]{:S(2)}, u32[]{:S(2)}) %collective-permute-start.11) | collective-permute-done | bytes 131104 | tf_op jit(solution)/shard_map/ppermute | solution.py:450
  41.0 0.6 %collective-permute-start.12 = (f32[32,1024]{1,0:T(8,128)S(1)}, f32[32,1024]{1,0:T(8,128)S(1)}, u32[]{:S(2)}, u32[]{:S(2)}) collective-permute-start(f32[32,1024]{1,0:T(8,128)S(1)} %gate.6.refs_0_), channel_id=1, source_target_pairs={{0,1},{1,0},{2,3},{3,2},{4,5},{5,4},{6,7},{7,6},{8,9},{9,8},{10,11... | collective-permute-start | bytes 393224 | tf_op jit(solution)/shard_map/ppermute | solution.py:450
  41.7 0.9 %edges.1 = (f32[96,128]{1,0:T(8,128)S(1)}, f32[32,96]{1,0:T(8,128)S(1)}) custom-call(f32[32,128]{1,0:T(8,128)S(1)} %get-tuple-element.34.refs_4_.factor_ref, f32[32,128]{1,0:T(8,128)S(1)} %get-tuple-element.38.own_ref, f32[32,1152]{1,0:T(8,128)S(1)} %get-tuple-element.36.left_ref, f32[32,1152]{1,0:T(8,128)S(1)} %gate.4.right_ref.refs_1_, ...), custom_call_target="tpu_custom_call" | custom-call | bytes 3600000 | tf_op jit(solution)/shard_map/edges/pallas_call | solution.py:355
  42.6 1.5 %update.3 = (f32[8192,128]{1,0:T(8,128)}, f32[32,8192]{1,0:T(8,128)}, f32[8,128]{1,0:T(8,128)S(1)}) custom-call(f32[32,1024]{1,0:T(8,128)S(1)} %get-tuple-element.35.refs_0_, f32[32,1152]{1,0:T(8,128)S(1)} %gate.4.right_ref.refs_1_, f32[32,8192]{1,0:T(8,128)S(1)} %get-tuple-element.37.refs_2_.refs_4_, ...), custom_call_target="tpu_custom_call" | custom-call | bytes 5760000 | tf_op jit(solution)/shard_map/update/pallas_call | solution.py:417
  44.1 0.6 %collective-permute-start.10 = (f32[32,1024]{1,0:T(8,128)S(1)}, f32[32,1024]{1,0:T(8,128)S(1)}, u32[]{:S(2)}, u32[]{:S(2)}) collective-permute-start(f32[32,1024]{1,0:T(8,128)S(1)} %gate.5.refs_1_.refs_0_), channel_id=1, source_target_pairs={{0,1},{1,0},{2,3},{3,2},{4,5},{5,4},{6,7},{7,6},{8,9},{9,8},{10,11... | collective-permute-start | bytes 393224 | tf_op jit(solution)/shard_map/ppermute | solution.py:450
  44.6 1.9 %update.4 = (f32[8192,128]{1,0:T(8,128)}, f32[32,8192]{1,0:T(8,128)}) custom-call(f32[32,1024]{1,0:T(8,128)S(1)} %gate.6.refs_0_, f32[32,1024]{1,0:T(8,128)S(1)} %collective-permute-done.12.refs_1_, f32[32,1024]{1,0:T(8,128)S(1)} %collective-permute-done.7.refs_1_.refs_2_, ...), custom_call_target="tpu_custom_call", output_to_operand_aliasing={{0}: (8, {}), {1}: (9, {})} | custom-call | bytes 11520000 | tf_op jit(solution)/shard_map/update/pallas_call | solution.py:417
  46.6 1.5 %update.5 = (f32[8192,128]{1,0:T(8,128)}, f32[32,8192]{1,0:T(8,128)}) custom-call(f32[32,1024]{1,0:T(8,128)S(1)} %gate.5.refs_1_.refs_0_, f32[32,1024]{1,0:T(8,128)S(1)} %collective-permute-done.10.refs_1_, f32[32,8192]{1,0:T(8,128)S(1)} %get-tuple-element.37.refs_2_.refs_4_, ...), custom_call_target="tpu_custom_call", output_to_operand_aliasing={{0}: (6, {}), {1}: (7, {})} | custom-call | bytes 5760000 | tf_op jit(solution)/shard_map/update/pallas_call | solution.py:417
  (25 shorter events, 1.9 us)
Async XLA Ops:
  4.3 9.0 %copy-start = (f32[32,8192]{1,0:T(8,128)}, f32[32,8192]{1,0:T(8,128)S(1)}, u32[]{:S(2)}) copy-start(f32[32,8192]{1,0:T(8,128)S(1)} %get-tuple-element.33.refs_3_) | copy-start | bytes 3145732
  4.3 5.2 %collective-permute-start.2 = (f32[32,640]{1,0:T(8,128)S(1)}, f32[32,640]{1,0:T(8,128)S(1)}, u32[]{:S(2)}, u32[]{:S(2)}) collective-permute-start(f32[32,640]{1,0:T(8,128)S(1)} %get-tuple-element.24.refs_0_), channel_id=1, source_target_pairs={{0,24},{8,16},{16,8},{24,0},{1,25},{9,17},{17,9},{25,1},{2,26},{10... | collective-permute-start | bytes 245768 | tf_op jit(solution)/shard_map/ppermute | solution.py:450
  7.3 3.6 %collective-permute-start.1 = (f32[32,640]{1,0:T(8,128)S(1)}, f32[32,640]{1,0:T(8,128)S(1)}, u32[]{:S(2)}, u32[]{:S(2)}) collective-permute-start(f32[32,640]{1,0:T(8,128)S(1)} %get-tuple-element.24.refs_0_), channel_id=1, source_target_pairs={{0,16},{8,24},{16,0},{24,8},{1,17},{9,25},{17,1},{25,9},{2,18},{10... | collective-permute-start | bytes 245768 | tf_op jit(solution)/shard_map/ppermute | solution.py:450
  7.6 4.2 %collective-permute-start = (f32[32,640]{1,0:T(8,128)S(1)}, f32[32,640]{1,0:T(8,128)S(1)}, u32[]{:S(2)}, u32[]{:S(2)}) collective-permute-start(f32[32,640]{1,0:T(8,128)S(1)} %get-tuple-element.24.refs_0_), channel_id=1, source_target_pairs={{0,8},{8,0},{16,24},{24,16},{1,9},{9,1},{17,25},{25,17},{2,10},{10... | collective-permute-start | bytes 245768 | tf_op jit(solution)/shard_map/ppermute | solution.py:450
  13.2 3.3 %collective-permute-start.3 = (f32[32,4096]{1,0:T(8,128)S(1)}, f32[32,4096]{1,0:T(8,128)S(1)}, u32[]{:S(2)}, u32[]{:S(2)}) collective-permute-start(f32[32,4096]{1,0:T(8,128)S(1)} %images.3), channel_id=1, source_target_pairs={{0,1},{1,0},{2,3},{3,2},{4,5},{5,4},{6,7},{7,6},{8,9},{9,8},{10,11... | collective-permute-start | bytes 1572872 | tf_op jit(solution)/shard_map/ppermute | solution.py:450
  15.0 11.8 %copy-start.1 = (f32[32,8192]{1,0:T(8,128)S(1)}, f32[32,8192]{1,0:T(8,128)}, u32[]{:S(2)}) copy-start(f32[32,8192]{1,0:T(8,128)} %copy-done) | copy-start | bytes 3145732
  16.7 4.9 %collective-permute-start.5 = (f32[264,128]{1,0:T(8,128)S(1)}, f32[264,128]{1,0:T(8,128)S(1)}, u32[]{:S(2)}, u32[]{:S(2)}) collective-permute-start(f32[264,128]{1,0:T(8,128)S(1)} %get-tuple-element.32), channel_id=1, source_target_pairs={{0,2},{1,3},{2,0},{3,1},{4,6},{5,7},{6,4},{7,5},{8,10},{9,11},{10,... | collective-permute-start | bytes 405512 | tf_op jit(solution)/shard_map/ppermute | solution.py:450
  17.9 7.0 %collective-permute-start.4 = (f32[264,128]{1,0:T(8,128)S(1)}, f32[264,128]{1,0:T(8,128)S(1)}, u32[]{:S(2)}, u32[]{:S(2)}) collective-permute-start(f32[264,128]{1,0:T(8,128)S(1)} %get-tuple-element.30), channel_id=1, source_target_pairs={{0,2},{1,3},{2,0},{3,1},{4,6},{5,7},{6,4},{7,5},{8,10},{9,11},{10,... | collective-permute-start | bytes 405512 | tf_op jit(solution)/shard_map/ppermute | solution.py:450
  21.6 5.2 %collective-permute-start.6 = (f32[264,128]{1,0:T(8,128)S(1)}, f32[264,128]{1,0:T(8,128)S(1)}, u32[]{:S(2)}, u32[]{:S(2)}) collective-permute-start(f32[264,128]{1,0:T(8,128)S(1)} %join.1), channel_id=1, source_target_pairs={{0,4},{1,5},{2,6},{3,7},{4,0},{5,1},{6,2},{7,3},{8,12},{9,13},{10,... | collective-permute-start | bytes 405512 | tf_op jit(solution)/shard_map/ppermute | solution.py:450
  26.9 9.6 %collective-permute-start.7 = (f32[32,1024]{1,0:T(8,128)S(1)}, f32[32,1024]{1,0:T(8,128)S(1)}, u32[]{:S(2)}, u32[]{:S(2)}) collective-permute-start(f32[32,1024]{1,0:T(8,128)S(1)} %get-tuple-element.35.refs_0_), channel_id=1, source_target_pairs={{0,4},{1,5},{2,6},{3,7},{4,0},{5,1},{6,2},{7,3},{8,12},{9,13},{10,... | collective-permute-start | bytes 393224 | tf_op jit(solution)/shard_map/ppermute | solution.py:450
  28.7 12.9 %collective-permute-start.9 = (f32[32,1152]{1,0:T(8,128)S(1)}, f32[32,1152]{1,0:T(8,128)S(1)}, u32[]{:S(2)}, u32[]{:S(2)}) collective-permute-start(f32[32,1152]{1,0:T(8,128)S(1)} %get-tuple-element.36.left_ref), channel_id=1, source_target_pairs={{0,1},{1,0},{2,3},{3,2},{4,5},{5,4},{6,7},{7,6},{8,9},{9,8},{10,11... | collective-permute-start | bytes 442376 | tf_op jit(solution)/shard_map/ppermute | solution.py:450
  32.7 8.4 %collective-permute-start.11 = (f32[32,1024]{1,0:T(8,128)S(1)}, f32[32,1024]{1,0:T(8,128)S(1)}, u32[]{:S(2)}, u32[]{:S(2)}) collective-permute-start(f32[32,1024]{1,0:T(8,128)S(1)} %get-tuple-element.35.refs_0_), channel_id=1, source_target_pairs={{0,2},{1,3},{2,0},{3,1},{4,6},{5,7},{6,4},{7,5},{8,10},{9,11},{10,... | collective-permute-start | bytes 393224 | tf_op jit(solution)/shard_map/ppermute | solution.py:450
  36.5 7.5 %collective-permute-start.8 = (f32[32,1024]{1,0:T(8,128)S(1)}, f32[32,1024]{1,0:T(8,128)S(1)}, u32[]{:S(2)}, u32[]{:S(2)}) collective-permute-start(f32[32,1024]{1,0:T(8,128)S(1)} %collective-permute-done.7.refs_1_.refs_2_), channel_id=1, source_target_pairs={{0,2},{1,3},{2,0},{3,1},{4,6},{5,7},{6,4},{7,5},{8,10},{9,11},{10,... | collective-permute-start | bytes 393224 | tf_op jit(solution)/shard_map/ppermute | solution.py:450
  41.0 3.6 %collective-permute-start.12 = (f32[32,1024]{1,0:T(8,128)S(1)}, f32[32,1024]{1,0:T(8,128)S(1)}, u32[]{:S(2)}, u32[]{:S(2)}) collective-permute-start(f32[32,1024]{1,0:T(8,128)S(1)} %gate.6.refs_0_), channel_id=1, source_target_pairs={{0,1},{1,0},{2,3},{3,2},{4,5},{5,4},{6,7},{7,6},{8,9},{9,8},{10,11... | collective-permute-start | bytes 393224 | tf_op jit(solution)/shard_map/ppermute | solution.py:450
  41.7 3.0 %collective-permute-start.13 = (f32[32,1024]{1,0:T(8,128)S(1)}, f32[32,1024]{1,0:T(8,128)S(1)}, u32[]{:S(2)}, u32[]{:S(2)}) collective-permute-start(f32[32,1024]{1,0:T(8,128)S(1)} %collective-permute-done.7.refs_1_.refs_2_), channel_id=1, source_target_pairs={{0,1},{1,0},{2,3},{3,2},{4,5},{5,4},{6,7},{7,6},{8,9},{9,8},{10,11... | collective-permute-start | bytes 393224 | tf_op jit(solution)/shard_map/ppermute | solution.py:450
  44.1 2.5 %collective-permute-start.10 = (f32[32,1024]{1,0:T(8,128)S(1)}, f32[32,1024]{1,0:T(8,128)S(1)}, u32[]{:S(2)}, u32[]{:S(2)}) collective-permute-start(f32[32,1024]{1,0:T(8,128)S(1)} %gate.5.refs_1_.refs_0_), channel_id=1, source_target_pairs={{0,1},{1,0},{2,3},{3,2},{4,5},{5,4},{6,7},{7,6},{8,9},{9,8},{10,11... | collective-permute-start | bytes 393224 | tf_op jit(solution)/shard_map/ppermute | solution.py:450

commit v4 on v3

--- a/solution.py
+++ b/solution.py
@@ -23,6 +23,10 @@
 
 def full(left, right, dims=NN):
     return lax.dot_general(left, right, dims, precision=lax.Precision.HIGHEST, preferred_element_type=F32)
+
+
+def good(left, right, dims=NN):
+    return lax.dot_general(left, right, dims, precision=lax.Precision.HIGH, preferred_element_type=F32)
 
 
 def fast(left, right, dims=NN):
@@ -334,20 +338,20 @@
     lower_t, spread, reflect, upper_t = (factor_ref[:, i * nb : (i + 1) * nb] for i in range(4))
     size = left_ref.shape[1] - 128
     kernel_t = left_ref[:, size : size + nb] + right_ref[:, size : size + nb]
-    half = 0.5 * full(full(lower_t, kernel_t, TN), lower_t)
+    half = 0.5 * good(good(lower_t, kernel_t, TN), lower_t)
     own_v = own_ref[...]
     own_w = (
-        full(lower_t, total_ref[:, 4 * width : 5 * width], TN)
-        - full(spread, total_ref[:, 3 * width : 4 * width])
-        - full(half, own_v)
+        good(lower_t, total_ref[:, 4 * width : 5 * width], TN)
+        - good(spread, total_ref[:, 3 * width : 4 * width])
+        - good(half, own_v)
     )
-    both = own_w - full(half, own_v, TN)
-    small_ref[0:nb, :] = -full(reflect, both, TN)
-    small_ref[nb : 2 * nb, :] = -full(spread, own_v, TN)
-    small_ref[2 * nb : 3 * nb, :] = full(upper_t, both, TN)
-    mix_ref[:, 0:nb] = full(half, reflect)
+    both = own_w - good(half, own_v, TN)
+    small_ref[0:nb, :] = -good(reflect, both, TN)
+    small_ref[nb : 2 * nb, :] = -good(spread, own_v, TN)
+    small_ref[2 * nb : 3 * nb, :] = good(upper_t, both, TN)
+    mix_ref[:, 0:nb] = good(half, reflect)
     mix_ref[:, nb : 2 * nb] = -spread
-    mix_ref[:, 2 * nb : 3 * nb] = full(half, upper_t)
+    mix_ref[:, 2 * nb : 3 * nb] = good(half, upper_t)
 
 
 def edges(factors, own_v, left, right, total):

time: 48.2 us -> 48 us (level)
  no operation moved by 1% of the time
where the time goes in v4:
time: 48 us; the launch traced here: 47.9 us
  starting transfers between devices  19.8 us (41%)
  waiting for transfers between devices  14.1 us (29%)
  Pallas kernels  13.3 us (28%)
  between operations  0.73 us (2%)
    ppermute x14, starting transfers between devices, partner(): return lax.ppermute(array, axis, [(i, i ^ mask) for i in range(size)])  19.8 us
    ppermute x14, waiting for transfers between devices, partner(): return lax.ppermute(array, axis, [(i, i ^ mask) for i in range(size)])  14.1 us
    pallas_call x3, Pallas kernels, update(): pl.pallas_call(body, in_specs=[vmem] * (count + 4) + [hbm] * given, out_s...  4.83 us
    pallas_call x1, Pallas kernels, sweep(): pl.pallas_call(lambda *refs: sweep_kernel(nc, *refs), in_specs=[hbm] * 3,...  3.63 us
    pallas_call x2, Pallas kernels, images(): pl.pallas_call(lambda *refs: images_kernel(flip, *refs), out_shape=jax.Sh...  1.47 us
    pallas_call x1, Pallas kernels, decompose(): pl.pallas_call(decompose_kernel, in_specs=[vmem, vmem, pl.BlockSpec(memor...  1.1 us
  transfers between devices with their start and end apart: 14, of which 7 were waited for; matrix products, arithmetic and copies ran while one was open for 0% of the time, Pallas kernels for 14%

profile of v4, /device:TPU:1, one launch (start us, length us, event | category | flops | bytes accessed | tf_op | source)
XLA Modules:
  0.0 47.9 jit_solution(4389804324766128593)
XLA Ops:
  0.6 3.6 %sweep.1 = (f32[32,640]{1,0:T(8,128)S(1)}, f32[32,8192]{1,0:T(8,128)S(1)}, f32[32,8192]{1,0:T(8,128)S(1)}, f32[8192,128]{1,0:T(8,128)S(1)}) custom-call(f32[32,8192]{1,0:T(8,128)} %refs_0_.1, f32[32,8192]{1,0:T(8,128)} %refs_1_.1, f32[8192,128]{1,0:T(8,128)} %refs_2_.1), custom_call_target="tpu_custom_call" | custom-call | bytes 14400000 | tf_op jit(solution)/shard_map/sweep/pallas_call | solution.py:116
  4.3 3.1 %collective-permute-start.2 = (f32[32,640]{1,0:T(8,128)S(1)}, f32[32,640]{1,0:T(8,128)S(1)}, u32[]{:S(2)}, u32[]{:S(2)}) collective-permute-start(f32[32,640]{1,0:T(8,128)S(1)} %get-tuple-element.24.refs_0_), channel_id=1, source_target_pairs={{0,24},{8,16},{16,8},{24,0},{1,25},{9,17},{17,9},{25,1},{2,26},{10... | collective-permute-start | bytes 245768 | tf_op jit(solution)/shard_map/ppermute | solution.py:454
  7.7 1.8 %collective-permute-done.2.refs_3_ = f32[32,640]{1,0:T(8,128)S(1)} collective-permute-done((f32[32,640]{1,0:T(8,128)S(1)}, f32[32,640]{1,0:T(8,128)S(1)}, u32[]{:S(2)}, u32[]{:S(2)}) %collective-permute-start.2) | collective-permute-done | bytes 81952 | tf_op jit(solution)/shard_map/ppermute | solution.py:454
  9.5 1.4 %collective-permute-done.1.refs_2_ = f32[32,640]{1,0:T(8,128)S(1)} collective-permute-done((f32[32,640]{1,0:T(8,128)S(1)}, f32[32,640]{1,0:T(8,128)S(1)}, u32[]{:S(2)}, u32[]{:S(2)}) %collective-permute-start.1) | collective-permute-done | bytes 81952 | tf_op jit(solution)/shard_map/ppermute | solution.py:454
  10.9 0.8 %collective-permute-done.refs_1_ = f32[32,640]{1,0:T(8,128)S(1)} collective-permute-done((f32[32,640]{1,0:T(8,128)S(1)}, f32[32,640]{1,0:T(8,128)S(1)}, u32[]{:S(2)}, u32[]{:S(2)}) %collective-permute-start) | collective-permute-done | bytes 81952 | tf_op jit(solution)/shard_map/ppermute | solution.py:454
  11.7 0.8 %factor.1 = (f32[32,640]{1,0:T(8,128)S(1)}, f32[32,128]{1,0:T(8,128)S(1)}, f32[32,128]{1,0:T(8,128)S(1)}) custom-call(f32[32,640]{1,0:T(8,128)S(1)} %get-tuple-element.24.refs_0_, f32[32,640]{1,0:T(8,128)S(1)} %collective-permute-done.refs_1_, f32[32,640]{1,0:T(8,128)S(1)} %collective-permute-done.1.refs_2_, f32[32,640]{1,0:T(8,128)S(1)} %collective-permute-done.2.refs_3_), custom_call_target="tpu_custom_call" | custom-call | bytes 10800000 | tf_op jit(solution)/shard_map/factor/pallas_call | solution.py:160
  12.5 0.7 %images.3 = f32[32,4096]{1,0:T(8,128)S(1)} custom-call(f32[32,128]{1,0:T(8,128)S(1)} %get-tuple-element.25.refs_0_, f32[8192,128]{1,0:T(8,128)S(1)} %get-tuple-element.26.refs_1_.refs_3_.refs_5_), custom_call_target="tpu_custom_call" | custom-call | bytes 2880000 | tf_op jit(solution)/shard_map/images/pallas_call | solution.py:261
  13.2 1.8 %collective-permute-start.3 = (f32[32,4096]{1,0:T(8,128)S(1)}, f32[32,4096]{1,0:T(8,128)S(1)}, u32[]{:S(2)}, u32[]{:S(2)}) collective-permute-start(f32[32,4096]{1,0:T(8,128)S(1)} %images.3), channel_id=1, source_target_pairs={{0,1},{1,0},{2,3},{3,2},{4,5},{5,4},{6,7},{7,6},{8,9},{9,8},{10,11... | collective-permute-start | bytes 1572872 | tf_op jit(solution)/shard_map/ppermute | solution.py:454
  15.0 0.7 %images.2.refs_0_ = f32[32,4096]{1,0:T(8,128)S(1)} custom-call(f32[32,128]{1,0:T(8,128)S(1)} %get-tuple-element.25.refs_0_, f32[8192,128]{1,0:T(8,128)S(1)} %get-tuple-element.26.refs_1_.refs_3_.refs_5_), custom_call_target="tpu_custom_call" | custom-call | bytes 2880000 | tf_op jit(solution)/shard_map/images/pallas_call | solution.py:261
  16.7 1.1 %collective-permute-start.5 = (f32[264,128]{1,0:T(8,128)S(1)}, f32[264,128]{1,0:T(8,128)S(1)}, u32[]{:S(2)}, u32[]{:S(2)}) collective-permute-start(f32[264,128]{1,0:T(8,128)S(1)} %get-tuple-element.32), channel_id=1, source_target_pairs={{0,2},{1,3},{2,0},{3,1},{4,6},{5,7},{6,4},{7,5},{8,10},{9,11},{10,... | collective-permute-start | bytes 405512 | tf_op jit(solution)/shard_map/ppermute | solution.py:454
  18.2 3.3 %collective-permute-done.5.right_ref = f32[264,128]{1,0:T(8,128)S(1)} collective-permute-done((f32[264,128]{1,0:T(8,128)S(1)}, f32[264,128]{1,0:T(8,128)S(1)}, u32[]{:S(2)}, u32[]{:S(2)}) %collective-permute-start.5) | collective-permute-done | bytes 135200 | tf_op jit(solution)/shard_map/ppermute | solution.py:454
  21.6 2.2 %collective-permute-start.6 = (f32[264,128]{1,0:T(8,128)S(1)}, f32[264,128]{1,0:T(8,128)S(1)}, u32[]{:S(2)}, u32[]{:S(2)}) collective-permute-start(f32[264,128]{1,0:T(8,128)S(1)} %join.1), channel_id=1, source_target_pairs={{0,4},{1,5},{2,6},{3,7},{4,0},{5,1},{6,2},{7,3},{8,12},{9,13},{10,... | collective-permute-start | bytes 405512 | tf_op jit(solution)/shard_map/ppermute | solution.py:454
  23.8 1.1 %decompose.1 = (f32[32,128]{1,0:T(8,128)S(1)}, f32[32,128]{1,0:T(8,128)S(1)}) custom-call(f32[32,128]{1,0:T(8,128)S(1)} %get-tuple-element.28.state_ref, f32[32,640]{1,0:T(8,128)S(1)} %get-tuple-element.27.total_ref, f32[264,128]{1,0:T(8,128)S(1)} %get-tuple-element.29.after_ref.refs_0_), custom_call_target="tpu_custom_call" | custom-call | bytes 10800000 | tf_op jit(solution)/shard_map/decompose/pallas_call | solution.py:236
  24.9 2.0 %collective-permute-done.6.refs_2_ = f32[264,128]{1,0:T(8,128)S(1)} collective-permute-done((f32[264,128]{1,0:T(8,128)S(1)}, f32[264,128]{1,0:T(8,128)S(1)}, u32[]{:S(2)}, u32[]{:S(2)}) %collective-permute-start.6) | collective-permute-done | bytes 135200 | tf_op jit(solution)/shard_map/ppermute | solution.py:454
  26.9 1.8 %collective-permute-start.7 = (f32[32,1024]{1,0:T(8,128)S(1)}, f32[32,1024]{1,0:T(8,128)S(1)}, u32[]{:S(2)}, u32[]{:S(2)}) collective-permute-start(f32[32,1024]{1,0:T(8,128)S(1)} %get-tuple-element.35.refs_0_), channel_id=1, source_target_pairs={{0,4},{1,5},{2,6},{3,7},{4,0},{5,1},{6,2},{7,3},{8,12},{9,13},{10,... | collective-permute-start | bytes 393224 | tf_op jit(solution)/shard_map/ppermute | solution.py:454
  28.7 3.9 %collective-permute-start.9 = (f32[32,1152]{1,0:T(8,128)S(1)}, f32[32,1152]{1,0:T(8,128)S(1)}, u32[]{:S(2)}, u32[]{:S(2)}) collective-permute-start(f32[32,1152]{1,0:T(8,128)S(1)} %get-tuple-element.36.left_ref), channel_id=1, source_target_pairs={{0,1},{1,0},{2,3},{3,2},{4,5},{5,4},{6,7},{7,6},{8,9},{9,8},{10,11... | collective-permute-start | bytes 442376 | tf_op jit(solution)/shard_map/ppermute | solution.py:454
  32.7 3.9 %collective-permute-start.11 = (f32[32,1024]{1,0:T(8,128)S(1)}, f32[32,1024]{1,0:T(8,128)S(1)}, u32[]{:S(2)}, u32[]{:S(2)}) collective-permute-start(f32[32,1024]{1,0:T(8,128)S(1)} %get-tuple-element.35.refs_0_), channel_id=1, source_target_pairs={{0,2},{1,3},{2,0},{3,1},{4,6},{5,7},{6,4},{7,5},{8,10},{9,11},{10,... | collective-permute-start | bytes 393224 | tf_op jit(solution)/shard_map/ppermute | solution.py:454
  36.6 4.4 %collective-permute-done.11.refs_0_ = f32[32,1024]{1,0:T(8,128)S(1)} collective-permute-done((f32[32,1024]{1,0:T(8,128)S(1)}, f32[32,1024]{1,0:T(8,128)S(1)}, u32[]{:S(2)}, u32[]{:S(2)}) %collective-permute-start.11) | collective-permute-done | bytes 131104 | tf_op jit(solution)/shard_map/ppermute | solution.py:454
  41.0 0.6 %collective-permute-start.12 = (f32[32,1024]{1,0:T(8,128)S(1)}, f32[32,1024]{1,0:T(8,128)S(1)}, u32[]{:S(2)}, u32[]{:S(2)}) collective-permute-start(f32[32,1024]{1,0:T(8,128)S(1)} %gate.6.refs_0_), channel_id=1, source_target_pairs={{0,1},{1,0},{2,3},{3,2},{4,5},{5,4},{6,7},{7,6},{8,9},{9,8},{10,11... | collective-permute-start | bytes 393224 | tf_op jit(solution)/shard_map/ppermute | solution.py:454
  41.7 0.8 %edges.1 = (f32[96,128]{1,0:T(8,128)S(1)}, f32[32,96]{1,0:T(8,128)S(1)}) custom-call(f32[32,128]{1,0:T(8,128)S(1)} %get-tuple-element.34.refs_4_.factor_ref, f32[32,128]{1,0:T(8,128)S(1)} %get-tuple-element.38.own_ref, f32[32,1152]{1,0:T(8,128)S(1)} %get-tuple-element.36.left_ref, f32[32,1152]{1,0:T(8,128)S(1)} %gate.4.right_ref.refs_1_, ...), custom_call_target="tpu_custom_call" | custom-call | bytes 3600000 | tf_op jit(solution)/shard_map/edges/pallas_call | solution.py:359
  42.4 1.5 %update.3 = (f32[8192,128]{1,0:T(8,128)}, f32[32,8192]{1,0:T(8,128)}, f32[8,128]{1,0:T(8,128)S(1)}) custom-call(f32[32,1024]{1,0:T(8,128)S(1)} %get-tuple-element.35.refs_0_, f32[32,1152]{1,0:T(8,128)S(1)} %gate.4.right_ref.refs_1_, f32[32,8192]{1,0:T(8,128)S(1)} %get-tuple-element.37.refs_2_.refs_4_, ...), custom_call_target="tpu_custom_call" | custom-call | bytes 5760000 | tf_op jit(solution)/shard_map/update/pallas_call | solution.py:421
  43.9 0.6 %collective-permute-start.10 = (f32[32,1024]{1,0:T(8,128)S(1)}, f32[32,1024]{1,0:T(8,128)S(1)}, u32[]{:S(2)}, u32[]{:S(2)}) collective-permute-start(f32[32,1024]{1,0:T(8,128)S(1)} %gate.5.refs_1_.refs_0_), channel_id=1, source_target_pairs={{0,1},{1,0},{2,3},{3,2},{4,5},{5,4},{6,7},{7,6},{8,9},{9,8},{10,11... | collective-permute-start | bytes 393224 | tf_op jit(solution)/shard_map/ppermute | solution.py:454
  44.5 1.9 %update.4 = (f32[8192,128]{1,0:T(8,128)}, f32[32,8192]{1,0:T(8,128)}) custom-call(f32[32,1024]{1,0:T(8,128)S(1)} %gate.6.refs_0_, f32[32,1024]{1,0:T(8,128)S(1)} %collective-permute-done.12.refs_1_, f32[32,1024]{1,0:T(8,128)S(1)} %collective-permute-done.7.refs_1_.refs_2_, ...), custom_call_target="tpu_custom_call", output_to_operand_aliasing={{0}: (8, {}), {1}: (9, {})} | custom-call | bytes 11520000 | tf_op jit(solution)/shard_map/update/pallas_call | solution.py:421
  46.4 1.5 %update.5 = (f32[8192,128]{1,0:T(8,128)}, f32[32,8192]{1,0:T(8,128)}) custom-call(f32[32,1024]{1,0:T(8,128)S(1)} %gate.5.refs_1_.refs_0_, f32[32,1024]{1,0:T(8,128)S(1)} %collective-permute-done.10.refs_1_, f32[32,8192]{1,0:T(8,128)S(1)} %get-tuple-element.37.refs_2_.refs_4_, ...), custom_call_target="tpu_custom_call", output_to_operand_aliasing={{0}: (6, {}), {1}: (7, {})} | custom-call | bytes 5760000 | tf_op jit(solution)/shard_map/update/pallas_call | solution.py:421
  (25 shorter events, 1.9 us)
Async XLA Ops:
  4.3 9.0 %copy-start = (f32[32,8192]{1,0:T(8,128)}, f32[32,8192]{1,0:T(8,128)S(1)}, u32[]{:S(2)}) copy-start(f32[32,8192]{1,0:T(8,128)S(1)} %get-tuple-element.33.refs_3_) | copy-start | bytes 3145732
  4.3 5.2 %collective-permute-start.2 = (f32[32,640]{1,0:T(8,128)S(1)}, f32[32,640]{1,0:T(8,128)S(1)}, u32[]{:S(2)}, u32[]{:S(2)}) collective-permute-start(f32[32,640]{1,0:T(8,128)S(1)} %get-tuple-element.24.refs_0_), channel_id=1, source_target_pairs={{0,24},{8,16},{16,8},{24,0},{1,25},{9,17},{17,9},{25,1},{2,26},{10... | collective-permute-start | bytes 245768 | tf_op jit(solution)/shard_map/ppermute | solution.py:454
  7.3 3.6 %collective-permute-start.1 = (f32[32,640]{1,0:T(8,128)S(1)}, f32[32,640]{1,0:T(8,128)S(1)}, u32[]{:S(2)}, u32[]{:S(2)}) collective-permute-start(f32[32,640]{1,0:T(8,128)S(1)} %get-tuple-element.24.refs_0_), channel_id=1, source_target_pairs={{0,16},{8,24},{16,0},{24,8},{1,17},{9,25},{17,1},{25,9},{2,18},{10... | collective-permute-start | bytes 245768 | tf_op jit(solution)/shard_map/ppermute | solution.py:454
  7.6 4.2 %collective-permute-start = (f32[32,640]{1,0:T(8,128)S(1)}, f32[32,640]{1,0:T(8,128)S(1)}, u32[]{:S(2)}, u32[]{:S(2)}) collective-permute-start(f32[32,640]{1,0:T(8,128)S(1)} %get-tuple-element.24.refs_0_), channel_id=1, source_target_pairs={{0,8},{8,0},{16,24},{24,16},{1,9},{9,1},{17,25},{25,17},{2,10},{10... | collective-permute-start | bytes 245768 | tf_op jit(solution)/shard_map/ppermute | solution.py:454
  13.2 3.3 %collective-permute-start.3 = (f32[32,4096]{1,0:T(8,128)S(1)}, f32[32,4096]{1,0:T(8,128)S(1)}, u32[]{:S(2)}, u32[]{:S(2)}) collective-permute-start(f32[32,4096]{1,0:T(8,128)S(1)} %images.3), channel_id=1, source_target_pairs={{0,1},{1,0},{2,3},{3,2},{4,5},{5,4},{6,7},{7,6},{8,9},{9,8},{10,11... | collective-permute-start | bytes 1572872 | tf_op jit(solution)/shard_map/ppermute | solution.py:454
  15.0 11.8 %copy-start.1 = (f32[32,8192]{1,0:T(8,128)S(1)}, f32[32,8192]{1,0:T(8,128)}, u32[]{:S(2)}) copy-start(f32[32,8192]{1,0:T(8,128)} %copy-done) | copy-start | bytes 3145732
  16.7 4.9 %collective-permute-start.5 = (f32[264,128]{1,0:T(8,128)S(1)}, f32[264,128]{1,0:T(8,128)S(1)}, u32[]{:S(2)}, u32[]{:S(2)}) collective-permute-start(f32[264,128]{1,0:T(8,128)S(1)} %get-tuple-element.32), channel_id=1, source_target_pairs={{0,2},{1,3},{2,0},{3,1},{4,6},{5,7},{6,4},{7,5},{8,10},{9,11},{10,... | collective-permute-start | bytes 405512 | tf_op jit(solution)/shard_map/ppermute | solution.py:454
  17.9 7.0 %collective-permute-start.4 = (f32[264,128]{1,0:T(8,128)S(1)}, f32[264,128]{1,0:T(8,128)S(1)}, u32[]{:S(2)}, u32[]{:S(2)}) collective-permute-start(f32[264,128]{1,0:T(8,128)S(1)} %get-tuple-element.30), channel_id=1, source_target_pairs={{0,2},{1,3},{2,0},{3,1},{4,6},{5,7},{6,4},{7,5},{8,10},{9,11},{10,... | collective-permute-start | bytes 405512 | tf_op jit(solution)/shard_map/ppermute | solution.py:454
  21.6 5.2 %collective-permute-start.6 = (f32[264,128]{1,0:T(8,128)S(1)}, f32[264,128]{1,0:T(8,128)S(1)}, u32[]{:S(2)}, u32[]{:S(2)}) collective-permute-start(f32[264,128]{1,0:T(8,128)S(1)} %join.1), channel_id=1, source_target_pairs={{0,4},{1,5},{2,6},{3,7},{4,0},{5,1},{6,2},{7,3},{8,12},{9,13},{10,... | collective-permute-start | bytes 405512 | tf_op jit(solution)/shard_map/ppermute | solution.py:454
  26.9 9.6 %collective-permute-start.7 = (f32[32,1024]{1,0:T(8,128)S(1)}, f32[32,1024]{1,0:T(8,128)S(1)}, u32[]{:S(2)}, u32[]{:S(2)}) collective-permute-start(f32[32,1024]{1,0:T(8,128)S(1)} %get-tuple-element.35.refs_0_), channel_id=1, source_target_pairs={{0,4},{1,5},{2,6},{3,7},{4,0},{5,1},{6,2},{7,3},{8,12},{9,13},{10,... | collective-permute-start | bytes 393224 | tf_op jit(solution)/shard_map/ppermute | solution.py:454
  28.7 12.9 %collective-permute-start.9 = (f32[32,1152]{1,0:T(8,128)S(1)}, f32[32,1152]{1,0:T(8,128)S(1)}, u32[]{:S(2)}, u32[]{:S(2)}) collective-permute-start(f32[32,1152]{1,0:T(8,128)S(1)} %get-tuple-element.36.left_ref), channel_id=1, source_target_pairs={{0,1},{1,0},{2,3},{3,2},{4,5},{5,4},{6,7},{7,6},{8,9},{9,8},{10,11... | collective-permute-start | bytes 442376 | tf_op jit(solution)/shard_map/ppermute | solution.py:454
  32.7 8.4 %collective-permute-start.11 = (f32[32,1024]{1,0:T(8,128)S(1)}, f32[32,1024]{1,0:T(8,128)S(1)}, u32[]{:S(2)}, u32[]{:S(2)}) collective-permute-start(f32[32,1024]{1,0:T(8,128)S(1)} %get-tuple-element.35.refs_0_), channel_id=1, source_target_pairs={{0,2},{1,3},{2,0},{3,1},{4,6},{5,7},{6,4},{7,5},{8,10},{9,11},{10,... | collective-permute-start | bytes 393224 | tf_op jit(solution)/shard_map/ppermute | solution.py:454
  36.5 7.4 %collective-permute-start.8 = (f32[32,1024]{1,0:T(8,128)S(1)}, f32[32,1024]{1,0:T(8,128)S(1)}, u32[]{:S(2)}, u32[]{:S(2)}) collective-permute-start(f32[32,1024]{1,0:T(8,128)S(1)} %collective-permute-done.7.refs_1_.refs_2_), channel_id=1, source_target_pairs={{0,2},{1,3},{2,0},{3,1},{4,6},{5,7},{6,4},{7,5},{8,10},{9,11},{10,... | collective-permute-start | bytes 393224 | tf_op jit(solution)/shard_map/ppermute | solution.py:454
  41.0 3.5 %collective-permute-start.12 = (f32[32,1024]{1,0:T(8,128)S(1)}, f32[32,1024]{1,0:T(8,128)S(1)}, u32[]{:S(2)}, u32[]{:S(2)}) collective-permute-start(f32[32,1024]{1,0:T(8,128)S(1)} %gate.6.refs_0_), channel_id=1, source_target_pairs={{0,1},{1,0},{2,3},{3,2},{4,5},{5,4},{6,7},{7,6},{8,9},{9,8},{10,11... | collective-permute-start | bytes 393224 | tf_op jit(solution)/shard_map/ppermute | solution.py:454
  41.7 2.8 %collective-permute-start.13 = (f32[32,1024]{1,0:T(8,128)S(1)}, f32[32,1024]{1,0:T(8,128)S(1)}, u32[]{:S(2)}, u32[]{:S(2)}) collective-permute-start(f32[32,1024]{1,0:T(8,128)S(1)} %collective-permute-done.7.refs_1_.refs_2_), channel_id=1, source_target_pairs={{0,1},{1,0},{2,3},{3,2},{4,5},{5,4},{6,7},{7,6},{8,9},{9,8},{10,11... | collective-permute-start | bytes 393224 | tf_op jit(solution)/shard_map/ppermute | solution.py:454
  43.9 2.5 %collective-permute-start.10 = (f32[32,1024]{1,0:T(8,128)S(1)}, f32[32,1024]{1,0:T(8,128)S(1)}, u32[]{:S(2)}, u32[]{:S(2)}) collective-permute-start(f32[32,1024]{1,0:T(8,128)S(1)} %gate.5.refs_1_.refs_0_), channel_id=1, source_target_pairs={{0,1},{1,0},{2,3},{3,2},{4,5},{5,4},{6,7},{7,6},{8,9},{9,8},{10,11... | collective-permute-start | bytes 393224 | tf_op jit(solution)/shard_map/ppermute | solution.py:454

commit v5 on v4

--- a/solution.py
+++ b/solution.py
@@ -379,11 +379,12 @@
     right = jnp.concatenate([right, right], axis=0)
     high, low = split(mix_ref[:, 0 : 2 * nb], 2)
     mix = jnp.concatenate([jnp.concatenate([high, high], axis=1), jnp.concatenate([low, low], axis=1)], axis=0)
-    length = size // 2
+    cuts = 4
+    length = size // cuts
     copies = []
     for i, block in enumerate(blocks):
         first = (lax.axis_index("row") == 0) & (block == 0)
-        for k in range(2):
+        for k in range(cuts):
             here = pl.ds(pl.multiple_of(block * size + k * length, 128), length)
             there = slice(k * length, (k + 1) * length)
             left = jnp.concatenate([panel_ref[:, here], pieces[i][:, there]], axis=0)
@@ -395,7 +396,7 @@
             if k == 0:
                 buffer[i, 0:nb, :] -= jnp.where(first, small_ref[2 * nb : 3 * nb, :], 0.0)
                 factors[i, :, 0:nb] -= jnp.where(first, mix_ref[:, 2 * nb : 3 * nb], 0.0)
-            copies.append(pltpu.make_async_copy(buffer.at[i, there, :], out_hbm.at[here, :], out_sem.at[2 * i + k]))
+            copies.append(pltpu.make_async_copy(buffer.at[i, there, :], out_hbm.at[here, :], out_sem.at[cuts * i + k]))
             copies[-1].start()
         here = pl.ds(pl.multiple_of(block * size, 128), size)
         copies.append(pltpu.make_async_copy(factors.at[i], weights_hbm.at[:, here], weights_sem.at[i]))
@@ -426,7 +427,7 @@
         scratch_shapes=[
             pltpu.VMEM((count, size, width), F32),
             pltpu.VMEM((count, nb, size), F32),
-            pltpu.SemaphoreType.DMA((2 * count,)),
+            pltpu.SemaphoreType.DMA((4 * count,)),
             pltpu.SemaphoreType.DMA((count,)),
         ],
         input_output_aliases={count + 4 + i: i for i in range(given)},

time: 48 us -> 48 us (level)
  no operation moved by 1% of the time
where the time goes in v5:
time: 48 us; the launch traced here: 47.8 us
  starting transfers between devices  19.8 us (41%)
  waiting for transfers between devices  14.1 us (29%)
  Pallas kernels  13.2 us (28%)
  between operations  0.73 us (2%)
    ppermute x14, starting transfers between devices, partner(): return lax.ppermute(array, axis, [(i, i ^ mask) for i in range(size)])  19.8 us
    ppermute x14, waiting for transfers between devices, partner(): return lax.ppermute(array, axis, [(i, i ^ mask) for i in range(size)])  14.1 us
    pallas_call x3, Pallas kernels, update(): pl.pallas_call(body, in_specs=[vmem] * (count + 4) + [hbm] * given, out_s...  4.77 us
    pallas_call x1, Pallas kernels, sweep(): pl.pallas_call(lambda *refs: sweep_kernel(nc, *refs), in_specs=[hbm] * 3,...  3.63 us
    pallas_call x2, Pallas kernels, images(): pl.pallas_call(lambda *refs: images_kernel(flip, *refs), out_shape=jax.Sh...  1.47 us
    pallas_call x1, Pallas kernels, decompose(): pl.pallas_call(decompose_kernel, in_specs=[vmem, vmem, pl.BlockSpec(memor...  1.1 us
  transfers between devices with their start and end apart: 14, of which 7 were waited for; matrix products, arithmetic and copies ran while one was open for 0% of the time, Pallas kernels for 14%

profile of v5, /device:TPU:1, one launch (start us, length us, event | category | flops | bytes accessed | tf_op | source)
XLA Modules:
  0.0 47.8 jit_solution(16503129120761274340)
XLA Ops:
  0.6 3.6 %sweep.1 = (f32[32,640]{1,0:T(8,128)S(1)}, f32[32,8192]{1,0:T(8,128)S(1)}, f32[32,8192]{1,0:T(8,128)S(1)}, f32[8192,128]{1,0:T(8,128)S(1)}) custom-call(f32[32,8192]{1,0:T(8,128)} %refs_0_.1, f32[32,8192]{1,0:T(8,128)} %refs_1_.1, f32[8192,128]{1,0:T(8,128)} %refs_2_.1), custom_call_target="tpu_custom_call" | custom-call | bytes 14400000 | tf_op jit(solution)/shard_map/sweep/pallas_call | solution.py:116
  4.3 3.1 %collective-permute-start.2 = (f32[32,640]{1,0:T(8,128)S(1)}, f32[32,640]{1,0:T(8,128)S(1)}, u32[]{:S(2)}, u32[]{:S(2)}) collective-permute-start(f32[32,640]{1,0:T(8,128)S(1)} %get-tuple-element.24.refs_0_), channel_id=1, source_target_pairs={{0,24},{8,16},{16,8},{24,0},{1,25},{9,17},{17,9},{25,1},{2,26},{10... | collective-permute-start | bytes 245768 | tf_op jit(solution)/shard_map/ppermute | solution.py:455
  7.7 1.8 %collective-permute-done.2.refs_3_ = f32[32,640]{1,0:T(8,128)S(1)} collective-permute-done((f32[32,640]{1,0:T(8,128)S(1)}, f32[32,640]{1,0:T(8,128)S(1)}, u32[]{:S(2)}, u32[]{:S(2)}) %collective-permute-start.2) | collective-permute-done | bytes 81952 | tf_op jit(solution)/shard_map/ppermute | solution.py:455
  9.5 1.4 %collective-permute-done.1.refs_2_ = f32[32,640]{1,0:T(8,128)S(1)} collective-permute-done((f32[32,640]{1,0:T(8,128)S(1)}, f32[32,640]{1,0:T(8,128)S(1)}, u32[]{:S(2)}, u32[]{:S(2)}) %collective-permute-start.1) | collective-permute-done | bytes 81952 | tf_op jit(solution)/shard_map/ppermute | solution.py:455
  10.9 0.8 %collective-permute-done.refs_1_ = f32[32,640]{1,0:T(8,128)S(1)} collective-permute-done((f32[32,640]{1,0:T(8,128)S(1)}, f32[32,640]{1,0:T(8,128)S(1)}, u32[]{:S(2)}, u32[]{:S(2)}) %collective-permute-start) | collective-permute-done | bytes 81952 | tf_op jit(solution)/shard_map/ppermute | solution.py:455
  11.7 0.8 %factor.1 = (f32[32,640]{1,0:T(8,128)S(1)}, f32[32,128]{1,0:T(8,128)S(1)}, f32[32,128]{1,0:T(8,128)S(1)}) custom-call(f32[32,640]{1,0:T(8,128)S(1)} %get-tuple-element.24.refs_0_, f32[32,640]{1,0:T(8,128)S(1)} %collective-permute-done.refs_1_, f32[32,640]{1,0:T(8,128)S(1)} %collective-permute-done.1.refs_2_, f32[32,640]{1,0:T(8,128)S(1)} %collective-permute-done.2.refs_3_), custom_call_target="tpu_custom_call" | custom-call | bytes 10800000 | tf_op jit(solution)/shard_map/factor/pallas_call | solution.py:160
  12.5 0.7 %images.3 = f32[32,4096]{1,0:T(8,128)S(1)} custom-call(f32[32,128]{1,0:T(8,128)S(1)} %get-tuple-element.25.refs_0_, f32[8192,128]{1,0:T(8,128)S(1)} %get-tuple-element.26.refs_1_.refs_3_.refs_5_), custom_call_target="tpu_custom_call" | custom-call | bytes 2880000 | tf_op jit(solution)/shard_map/images/pallas_call | solution.py:261
  13.2 1.8 %collective-permute-start.3 = (f32[32,4096]{1,0:T(8,128)S(1)}, f32[32,4096]{1,0:T(8,128)S(1)}, u32[]{:S(2)}, u32[]{:S(2)}) collective-permute-start(f32[32,4096]{1,0:T(8,128)S(1)} %images.3), channel_id=1, source_target_pairs={{0,1},{1,0},{2,3},{3,2},{4,5},{5,4},{6,7},{7,6},{8,9},{9,8},{10,11... | collective-permute-start | bytes 1572872 | tf_op jit(solution)/shard_map/ppermute | solution.py:455
  15.0 0.7 %images.2.refs_0_ = f32[32,4096]{1,0:T(8,128)S(1)} custom-call(f32[32,128]{1,0:T(8,128)S(1)} %get-tuple-element.25.refs_0_, f32[8192,128]{1,0:T(8,128)S(1)} %get-tuple-element.26.refs_1_.refs_3_.refs_5_), custom_call_target="tpu_custom_call" | custom-call | bytes 2880000 | tf_op jit(solution)/shard_map/images/pallas_call | solution.py:261
  16.7 1.1 %collective-permute-start.5 = (f32[264,128]{1,0:T(8,128)S(1)}, f32[264,128]{1,0:T(8,128)S(1)}, u32[]{:S(2)}, u32[]{:S(2)}) collective-permute-start(f32[264,128]{1,0:T(8,128)S(1)} %get-tuple-element.32), channel_id=1, source_target_pairs={{0,2},{1,3},{2,0},{3,1},{4,6},{5,7},{6,4},{7,5},{8,10},{9,11},{10,... | collective-permute-start | bytes 405512 | tf_op jit(solution)/shard_map/ppermute | solution.py:455
  18.2 3.3 %collective-permute-done.5.right_ref = f32[264,128]{1,0:T(8,128)S(1)} collective-permute-done((f32[264,128]{1,0:T(8,128)S(1)}, f32[264,128]{1,0:T(8,128)S(1)}, u32[]{:S(2)}, u32[]{:S(2)}) %collective-permute-start.5) | collective-permute-done | bytes 135200 | tf_op jit(solution)/shard_map/ppermute | solution.py:455
  21.6 2.2 %collective-permute-start.6 = (f32[264,128]{1,0:T(8,128)S(1)}, f32[264,128]{1,0:T(8,128)S(1)}, u32[]{:S(2)}, u32[]{:S(2)}) collective-permute-start(f32[264,128]{1,0:T(8,128)S(1)} %join.1), channel_id=1, source_target_pairs={{0,4},{1,5},{2,6},{3,7},{4,0},{5,1},{6,2},{7,3},{8,12},{9,13},{10,... | collective-permute-start | bytes 405512 | tf_op jit(solution)/shard_map/ppermute | solution.py:455
  23.8 1.1 %decompose.1 = (f32[32,128]{1,0:T(8,128)S(1)}, f32[32,128]{1,0:T(8,128)S(1)}) custom-call(f32[32,128]{1,0:T(8,128)S(1)} %get-tuple-element.28.state_ref, f32[32,640]{1,0:T(8,128)S(1)} %get-tuple-element.27.total_ref, f32[264,128]{1,0:T(8,128)S(1)} %get-tuple-element.29.after_ref.refs_0_), custom_call_target="tpu_custom_call" | custom-call | bytes 10800000 | tf_op jit(solution)/shard_map/decompose/pallas_call | solution.py:236
  24.9 2.0 %collective-permute-done.6.refs_2_ = f32[264,128]{1,0:T(8,128)S(1)} collective-permute-done((f32[264,128]{1,0:T(8,128)S(1)}, f32[264,128]{1,0:T(8,128)S(1)}, u32[]{:S(2)}, u32[]{:S(2)}) %collective-permute-start.6) | collective-permute-done | bytes 135200 | tf_op jit(solution)/shard_map/ppermute | solution.py:455
  26.9 1.8 %collective-permute-start.7 = (f32[32,1024]{1,0:T(8,128)S(1)}, f32[32,1024]{1,0:T(8,128)S(1)}, u32[]{:S(2)}, u32[]{:S(2)}) collective-permute-start(f32[32,1024]{1,0:T(8,128)S(1)} %get-tuple-element.35.refs_0_), channel_id=1, source_target_pairs={{0,4},{1,5},{2,6},{3,7},{4,0},{5,1},{6,2},{7,3},{8,12},{9,13},{10,... | collective-permute-start | bytes 393224 | tf_op jit(solution)/shard_map/ppermute | solution.py:455
  28.7 3.9 %collective-permute-start.9 = (f32[32,1152]{1,0:T(8,128)S(1)}, f32[32,1152]{1,0:T(8,128)S(1)}, u32[]{:S(2)}, u32[]{:S(2)}) collective-permute-start(f32[32,1152]{1,0:T(8,128)S(1)} %get-tuple-element.36.left_ref), channel_id=1, source_target_pairs={{0,1},{1,0},{2,3},{3,2},{4,5},{5,4},{6,7},{7,6},{8,9},{9,8},{10,11... | collective-permute-start | bytes 442376 | tf_op jit(solution)/shard_map/ppermute | solution.py:455
  32.7 3.9 %collective-permute-start.11 = (f32[32,1024]{1,0:T(8,128)S(1)}, f32[32,1024]{1,0:T(8,128)S(1)}, u32[]{:S(2)}, u32[]{:S(2)}) collective-permute-start(f32[32,1024]{1,0:T(8,128)S(1)} %get-tuple-element.35.refs_0_), channel_id=1, source_target_pairs={{0,2},{1,3},{2,0},{3,1},{4,6},{5,7},{6,4},{7,5},{8,10},{9,11},{10,... | collective-permute-start | bytes 393224 | tf_op jit(solution)/shard_map/ppermute | solution.py:455
  36.6 4.4 %collective-permute-done.11.refs_0_ = f32[32,1024]{1,0:T(8,128)S(1)} collective-permute-done((f32[32,1024]{1,0:T(8,128)S(1)}, f32[32,1024]{1,0:T(8,128)S(1)}, u32[]{:S(2)}, u32[]{:S(2)}) %collective-permute-start.11) | collective-permute-done | bytes 131104 | tf_op jit(solution)/shard_map/ppermute | solution.py:455
  41.0 0.6 %collective-permute-start.12 = (f32[32,1024]{1,0:T(8,128)S(1)}, f32[32,1024]{1,0:T(8,128)S(1)}, u32[]{:S(2)}, u32[]{:S(2)}) collective-permute-start(f32[32,1024]{1,0:T(8,128)S(1)} %gate.6.refs_0_), channel_id=1, source_target_pairs={{0,1},{1,0},{2,3},{3,2},{4,5},{5,4},{6,7},{7,6},{8,9},{9,8},{10,11... | collective-permute-start | bytes 393224 | tf_op jit(solution)/shard_map/ppermute | solution.py:455
  41.7 0.8 %edges.1 = (f32[96,128]{1,0:T(8,128)S(1)}, f32[32,96]{1,0:T(8,128)S(1)}) custom-call(f32[32,128]{1,0:T(8,128)S(1)} %get-tuple-element.34.refs_4_.factor_ref, f32[32,128]{1,0:T(8,128)S(1)} %get-tuple-element.38.own_ref, f32[32,1152]{1,0:T(8,128)S(1)} %get-tuple-element.36.left_ref, f32[32,1152]{1,0:T(8,128)S(1)} %gate.4.right_ref.refs_1_, ...), custom_call_target="tpu_custom_call" | custom-call | bytes 3600000 | tf_op jit(solution)/shard_map/edges/pallas_call | solution.py:359
  42.4 1.4 %update.3 = (f32[8192,128]{1,0:T(8,128)}, f32[32,8192]{1,0:T(8,128)}, f32[8,128]{1,0:T(8,128)S(1)}) custom-call(f32[32,1024]{1,0:T(8,128)S(1)} %get-tuple-element.35.refs_0_, f32[32,1152]{1,0:T(8,128)S(1)} %gate.4.right_ref.refs_1_, f32[32,8192]{1,0:T(8,128)S(1)} %get-tuple-element.37.refs_2_.refs_4_, ...), custom_call_target="tpu_custom_call" | custom-call | bytes 5760000 | tf_op jit(solution)/shard_map/update/pallas_call | solution.py:422
  43.9 0.6 %collective-permute-start.10 = (f32[32,1024]{1,0:T(8,128)S(1)}, f32[32,1024]{1,0:T(8,128)S(1)}, u32[]{:S(2)}, u32[]{:S(2)}) collective-permute-start(f32[32,1024]{1,0:T(8,128)S(1)} %gate.5.refs_1_.refs_0_), channel_id=1, source_target_pairs={{0,1},{1,0},{2,3},{3,2},{4,5},{5,4},{6,7},{7,6},{8,9},{9,8},{10,11... | collective-permute-start | bytes 393224 | tf_op jit(solution)/shard_map/ppermute | solution.py:455
  44.5 1.9 %update.4 = (f32[8192,128]{1,0:T(8,128)}, f32[32,8192]{1,0:T(8,128)}) custom-call(f32[32,1024]{1,0:T(8,128)S(1)} %gate.6.refs_0_, f32[32,1024]{1,0:T(8,128)S(1)} %collective-permute-done.12.refs_1_, f32[32,1024]{1,0:T(8,128)S(1)} %collective-permute-done.7.refs_1_.refs_2_, ...), custom_call_target="tpu_custom_call", output_to_operand_aliasing={{0}: (8, {}), {1}: (9, {})} | custom-call | bytes 11520000 | tf_op jit(solution)/shard_map/update/pallas_call | solution.py:422
  46.4 1.4 %update.5 = (f32[8192,128]{1,0:T(8,128)}, f32[32,8192]{1,0:T(8,128)}) custom-call(f32[32,1024]{1,0:T(8,128)S(1)} %gate.5.refs_1_.refs_0_, f32[32,1024]{1,0:T(8,128)S(1)} %collective-permute-done.10.refs_1_, f32[32,8192]{1,0:T(8,128)S(1)} %get-tuple-element.37.refs_2_.refs_4_, ...), custom_call_target="tpu_custom_call", output_to_operand_aliasing={{0}: (6, {}), {1}: (7, {})} | custom-call | bytes 5760000 | tf_op jit(solution)/shard_map/update/pallas_call | solution.py:422
  (25 shorter events, 1.9 us)
Async XLA Ops:
  4.3 9.0 %copy-start = (f32[32,8192]{1,0:T(8,128)}, f32[32,8192]{1,0:T(8,128)S(1)}, u32[]{:S(2)}) copy-start(f32[32,8192]{1,0:T(8,128)S(1)} %get-tuple-element.33.refs_3_) | copy-start | bytes 3145732
  4.3 5.2 %collective-permute-start.2 = (f32[32,640]{1,0:T(8,128)S(1)}, f32[32,640]{1,0:T(8,128)S(1)}, u32[]{:S(2)}, u32[]{:S(2)}) collective-permute-start(f32[32,640]{1,0:T(8,128)S(1)} %get-tuple-element.24.refs_0_), channel_id=1, source_target_pairs={{0,24},{8,16},{16,8},{24,0},{1,25},{9,17},{17,9},{25,1},{2,26},{10... | collective-permute-start | bytes 245768 | tf_op jit(solution)/shard_map/ppermute | solution.py:455
  7.3 3.6 %collective-permute-start.1 = (f32[32,640]{1,0:T(8,128)S(1)}, f32[32,640]{1,0:T(8,128)S(1)}, u32[]{:S(2)}, u32[]{:S(2)}) collective-permute-start(f32[32,640]{1,0:T(8,128)S(1)} %get-tuple-element.24.refs_0_), channel_id=1, source_target_pairs={{0,16},{8,24},{16,0},{24,8},{1,17},{9,25},{17,1},{25,9},{2,18},{10... | collective-permute-start | bytes 245768 | tf_op jit(solution)/shard_map/ppermute | solution.py:455
  7.6 4.2 %collective-permute-start = (f32[32,640]{1,0:T(8,128)S(1)}, f32[32,640]{1,0:T(8,128)S(1)}, u32[]{:S(2)}, u32[]{:S(2)}) collective-permute-start(f32[32,640]{1,0:T(8,128)S(1)} %get-tuple-element.24.refs_0_), channel_id=1, source_target_pairs={{0,8},{8,0},{16,24},{24,16},{1,9},{9,1},{17,25},{25,17},{2,10},{10... | collective-permute-start | bytes 245768 | tf_op jit(solution)/shard_map/ppermute | solution.py:455
  13.2 3.3 %collective-permute-start.3 = (f32[32,4096]{1,0:T(8,128)S(1)}, f32[32,4096]{1,0:T(8,128)S(1)}, u32[]{:S(2)}, u32[]{:S(2)}) collective-permute-start(f32[32,4096]{1,0:T(8,128)S(1)} %images.3), channel_id=1, source_target_pairs={{0,1},{1,0},{2,3},{3,2},{4,5},{5,4},{6,7},{7,6},{8,9},{9,8},{10,11... | collective-permute-start | bytes 1572872 | tf_op jit(solution)/shard_map/ppermute | solution.py:455
  15.0 11.8 %copy-start.1 = (f32[32,8192]{1,0:T(8,128)S(1)}, f32[32,8192]{1,0:T(8,128)}, u32[]{:S(2)}) copy-start(f32[32,8192]{1,0:T(8,128)} %copy-done) | copy-start | bytes 3145732
  16.7 4.9 %collective-permute-start.5 = (f32[264,128]{1,0:T(8,128)S(1)}, f32[264,128]{1,0:T(8,128)S(1)}, u32[]{:S(2)}, u32[]{:S(2)}) collective-permute-start(f32[264,128]{1,0:T(8,128)S(1)} %get-tuple-element.32), channel_id=1, source_target_pairs={{0,2},{1,3},{2,0},{3,1},{4,6},{5,7},{6,4},{7,5},{8,10},{9,11},{10,... | collective-permute-start | bytes 405512 | tf_op jit(solution)/shard_map/ppermute | solution.py:455
  17.9 7.0 %collective-permute-start.4 = (f32[264,128]{1,0:T(8,128)S(1)}, f32[264,128]{1,0:T(8,128)S(1)}, u32[]{:S(2)}, u32[]{:S(2)}) collective-permute-start(f32[264,128]{1,0:T(8,128)S(1)} %get-tuple-element.30), channel_id=1, source_target_pairs={{0,2},{1,3},{2,0},{3,1},{4,6},{5,7},{6,4},{7,5},{8,10},{9,11},{10,... | collective-permute-start | bytes 405512 | tf_op jit(solution)/shard_map/ppermute | solution.py:455
  21.6 5.2 %collective-permute-start.6 = (f32[264,128]{1,0:T(8,128)S(1)}, f32[264,128]{1,0:T(8,128)S(1)}, u32[]{:S(2)}, u32[]{:S(2)}) collective-permute-start(f32[264,128]{1,0:T(8,128)S(1)} %join.1), channel_id=1, source_target_pairs={{0,4},{1,5},{2,6},{3,7},{4,0},{5,1},{6,2},{7,3},{8,12},{9,13},{10,... | collective-permute-start | bytes 405512 | tf_op jit(solution)/shard_map/ppermute | solution.py:455
  26.9 9.6 %collective-permute-start.7 = (f32[32,1024]{1,0:T(8,128)S(1)}, f32[32,1024]{1,0:T(8,128)S(1)}, u32[]{:S(2)}, u32[]{:S(2)}) collective-permute-start(f32[32,1024]{1,0:T(8,128)S(1)} %get-tuple-element.35.refs_0_), channel_id=1, source_target_pairs={{0,4},{1,5},{2,6},{3,7},{4,0},{5,1},{6,2},{7,3},{8,12},{9,13},{10,... | collective-permute-start | bytes 393224 | tf_op jit(solution)/shard_map/ppermute | solution.py:455
  28.7 12.9 %collective-permute-start.9 = (f32[32,1152]{1,0:T(8,128)S(1)}, f32[32,1152]{1,0:T(8,128)S(1)}, u32[]{:S(2)}, u32[]{:S(2)}) collective-permute-start(f32[32,1152]{1,0:T(8,128)S(1)} %get-tuple-element.36.left_ref), channel_id=1, source_target_pairs={{0,1},{1,0},{2,3},{3,2},{4,5},{5,4},{6,7},{7,6},{8,9},{9,8},{10,11... | collective-permute-start | bytes 442376 | tf_op jit(solution)/shard_map/ppermute | solution.py:455
  32.7 8.4 %collective-permute-start.11 = (f32[32,1024]{1,0:T(8,128)S(1)}, f32[32,1024]{1,0:T(8,128)S(1)}, u32[]{:S(2)}, u32[]{:S(2)}) collective-permute-start(f32[32,1024]{1,0:T(8,128)S(1)} %get-tuple-element.35.refs_0_), channel_id=1, source_target_pairs={{0,2},{1,3},{2,0},{3,1},{4,6},{5,7},{6,4},{7,5},{8,10},{9,11},{10,... | collective-permute-start | bytes 393224 | tf_op jit(solution)/shard_map/ppermute | solution.py:455
  36.5 7.3 %collective-permute-start.8 = (f32[32,1024]{1,0:T(8,128)S(1)}, f32[32,1024]{1,0:T(8,128)S(1)}, u32[]{:S(2)}, u32[]{:S(2)}) collective-permute-start(f32[32,1024]{1,0:T(8,128)S(1)} %collective-permute-done.7.refs_1_.refs_2_), channel_id=1, source_target_pairs={{0,2},{1,3},{2,0},{3,1},{4,6},{5,7},{6,4},{7,5},{8,10},{9,11},{10,... | collective-permute-start | bytes 393224 | tf_op jit(solution)/shard_map/ppermute | solution.py:455
  41.0 3.4 %collective-permute-start.12 = (f32[32,1024]{1,0:T(8,128)S(1)}, f32[32,1024]{1,0:T(8,128)S(1)}, u32[]{:S(2)}, u32[]{:S(2)}) collective-permute-start(f32[32,1024]{1,0:T(8,128)S(1)} %gate.6.refs_0_), channel_id=1, source_target_pairs={{0,1},{1,0},{2,3},{3,2},{4,5},{5,4},{6,7},{7,6},{8,9},{9,8},{10,11... | collective-permute-start | bytes 393224 | tf_op jit(solution)/shard_map/ppermute | solution.py:455
  41.7 2.8 %collective-permute-start.13 = (f32[32,1024]{1,0:T(8,128)S(1)}, f32[32,1024]{1,0:T(8,128)S(1)}, u32[]{:S(2)}, u32[]{:S(2)}) collective-permute-start(f32[32,1024]{1,0:T(8,128)S(1)} %collective-permute-done.7.refs_1_.refs_2_), channel_id=1, source_target_pairs={{0,1},{1,0},{2,3},{3,2},{4,5},{5,4},{6,7},{7,6},{8,9},{9,8},{10,11... | collective-permute-start | bytes 393224 | tf_op jit(solution)/shard_map/ppermute | solution.py:455
  43.9 2.5 %collective-permute-start.10 = (f32[32,1024]{1,0:T(8,128)S(1)}, f32[32,1024]{1,0:T(8,128)S(1)}, u32[]{:S(2)}, u32[]{:S(2)}) collective-permute-start(f32[32,1024]{1,0:T(8,128)S(1)} %gate.5.refs_1_.refs_0_), channel_id=1, source_target_pairs={{0,1},{1,0},{2,3},{3,2},{4,5},{5,4},{6,7},{7,6},{8,9},{9,8},{10,11... | collective-permute-start | bytes 393224 | tf_op jit(solution)/shard_map/ppermute | solution.py:455
